TPU v7x, 32 devices: a whole 2x2x4 slice. The times are simulated.
32 devices in a mesh: ctx: 8 (over z, core), expert: 4 (over y, x).
Axes of the slice: x: 2, y: 2, z: 4, core: 2. Of those that a mesh axis runs over, the one named last changes fastest.
Arguments:
- inputs: bfloat16 [4, 4096, 1536], P('expert', 'ctx'), may hold values from -6 to 6
- cotangent: bfloat16 [4, 4096, 1536], P('expert', 'ctx'), may hold values from -6 to 6
- routes: int32 [4, 4096, 8], P('expert', 'ctx'), may hold values from 0 to 39, all different within a row; in each aligned block of 512 rows (0 to 511, 512 to 1023, ..., all dimensions but the last counted through in order) at most 128 rows name the same one
- attn_gain: bfloat16 [1536], P('ctx'), may hold values from 0.5 to 1.5
- query_weight: bfloat16 [1536, 1536], P('ctx'), may hold values from -0.15625 to 0.15625
- key_matrix: bfloat16 [1536, 512], P('ctx'), may hold values from -0.15625 to 0.15625
- value_matrix: bfloat16 [1536, 512], P('ctx'), may hold values from -0.15625 to 0.15625
- output_matrix: bfloat16 [1536, 1536], P('ctx'), may hold values from -0.3125 to 0.3125
- ffn_gain: bfloat16 [1536], P('ctx'), may hold values from 0.5 to 1.5
- router_weight: bfloat16 [1536, 40], P('ctx')
- gateup_weight: bfloat16 [40, 1536, 1024], P('expert'), may hold values from -0.15625 to 0.15625
- down_weight: bfloat16 [40, 512, 1536], P('expert'), may hold values from -0.375 to 0.375
Outputs:
- output: bfloat16 [4, 4096, 1536], P('expert', 'ctx')
- input_grad: bfloat16 [4, 4096, 1536], P('expert', 'ctx')
- attn_gain_grad: float32 [1536], P('ctx')
- query_grad: float32 [1536, 1536], P('ctx')
- key_grad: float32 [1536, 512], P('ctx')
- value_grad: float32 [1536, 512], P('ctx')
- outproj_grad: float32 [1536, 1536], P('ctx')
- ffn_gain_grad: float32 [1536], P('ctx')
- router_grad: float32 [1536, 40], P('ctx')
- gateup_grad: float32 [40, 1536, 1024], P('expert', 'ctx')
- down_grad: float32 [40, 512, 1536], P('expert', None, 'ctx')
Inputs may be any that keep to these rules, and one draw needn't show every extreme that they name: `routes`: each row names 8 different experts. In each block of 512 positions of a sequence no expert is named by more than 128 rows, and in some blocks one is named by exactly 128 rows.
All inputs are finite; a program needn't handle non-finite values.
Results may differ from a plain program's by a relative error of at most 0.025.
Values may be sent and summed in bfloat16 or wider, within the bound.
No kernel may reach another device: no remote copies, remote signals or barrier semaphores. Data moves between devices by JAX's collectives and lax.ppermute only.
A program may use at most 448 MiB of HBM per device.

v0:
```python
import math

import jax
import jax.numpy as jnp
from jax import lax
from jax.sharding import PartitionSpec as P

QUERY_HEADS = 24
KEY_VALUE_HEADS = 8
HEAD_SIZE = 64
FFE = 512
EXPERTS = 40
TOPK = 8


EPS = 1e-05
NEG = -1e30
THETA = 10000.0


def norm_rows(values, gain):
    factor = lax.rsqrt(jnp.mean(values * values, axis=-1, keepdims=True) + EPS)
    return ((values * factor * gain).astype(jnp.bfloat16), factor)


def norm_back(grad_norm, values, factor, gain):
    gain_grad = jnp.sum(grad_norm * values * factor, axis=0)
    inner = grad_norm * gain
    part = factor * inner - values * factor**3 * jnp.mean(inner * values, axis=-1, keepdims=True)
    return (gain_grad, part)


def angles(positions):
    half = HEAD_SIZE // 2
    freq = jnp.power(THETA, -jnp.arange(half).astype(jnp.float32) / half)
    turned = positions[:, None] * freq[None, :]
    return (jnp.cos(turned)[:, None, :], jnp.sin(turned)[:, None, :])


def rotary_tables(values, cosine_table, sine_table):
    half = values.shape[-1] // 2
    first_term = values[..., :half]
    second_term = values[..., half:]
    return jnp.concatenate(
        [
            first_term * cosine_table - second_term * sine_table,
            second_term * cosine_table + first_term * sine_table,
        ],
        axis=-1,
    )


def per_device(
    inputs,
    cotangent,
    routes,
    attn_gain,
    query_weight,
    key_matrix,
    value_matrix,
    output_matrix,
    ffn_gain,
    router_weight,
    gateup_weight,
    down_weight,
):
    single_float = jnp.float32
    brain_float_half = jnp.bfloat16
    sequences_local, block_span, width = inputs.shape
    query_groups = QUERY_HEADS // KEY_VALUE_HEADS
    key_value_width = KEY_VALUE_HEADS * HEAD_SIZE
    scale_factor = HEAD_SIZE ** (-0.5)
    n_ctx = lax.axis_size("ctx")
    n_owner = lax.axis_size("expert")
    position_zero = lax.axis_index("ctx") * block_span
    last_query = position_zero + block_span - 1
    local_experts = gateup_weight.shape[0]
    capacity = block_span // 4
    total_rows = sequences_local * block_span
    full_len = block_span * n_ctx
    gathered = (
        lax.all_gather(attn_gain, "ctx", axis=0, tiled=True),
        lax.all_gather(query_weight, "ctx", axis=0, tiled=True),
        lax.all_gather(key_matrix, "ctx", axis=0, tiled=True),
        lax.all_gather(value_matrix, "ctx", axis=0, tiled=True),
        lax.all_gather(output_matrix, "ctx", axis=0, tiled=True),
        lax.all_gather(ffn_gain, "ctx", axis=0, tiled=True),
        lax.all_gather(router_weight, "ctx", axis=0, tiled=True),
    )
    gain_one = gathered[0].astype(single_float)
    w_query = gathered[1]
    key_projection = gathered[2]
    w_value = gathered[3]
    w_output = gathered[4]
    gain_two = gathered[5].astype(single_float)
    w_router = gathered[6]
    flat_in = inputs.reshape(total_rows, width).astype(single_float)
    normalized_input, rms_one = norm_rows(flat_in, gain_one)
    query_pos = position_zero + jnp.arange(block_span)
    cosine_table, sine_table = angles(query_pos.astype(single_float))
    query_unrotated = jnp.dot(
        normalized_input, w_query, preferred_element_type=single_float
    ).reshape(sequences_local, block_span, QUERY_HEADS, HEAD_SIZE)
    query_rows = (
        rotary_tables(query_unrotated, cosine_table, sine_table)
        .astype(brain_float_half)
        .reshape(sequences_local, block_span, KEY_VALUE_HEADS, query_groups, HEAD_SIZE)
    )
    key_unrotated = jnp.dot(
        normalized_input, key_projection, preferred_element_type=single_float
    ).reshape(sequences_local, block_span, KEY_VALUE_HEADS, HEAD_SIZE)
    key_rows = rotary_tables(key_unrotated, cosine_table, sine_table).astype(brain_float_half)
    value_matrix_rows = jnp.dot(
        normalized_input, w_value, preferred_element_type=single_float
    ).astype(brain_float_half)
    packed = jnp.concatenate(
        [
            key_rows.reshape(sequences_local, block_span, key_value_width),
            value_matrix_rows.reshape(sequences_local, block_span, key_value_width),
        ],
        axis=-1,
    )

    def masked_scores(position_block, start):
        block_count = position_block.shape[1]
        key_portion = position_block[..., :key_value_width].reshape(
            sequences_local, block_count, KEY_VALUE_HEADS, HEAD_SIZE
        )
        value_portion = position_block[..., key_value_width:].reshape(
            sequences_local, block_count, KEY_VALUE_HEADS, HEAD_SIZE
        )
        scores = (
            jnp.einsum(
                "bqngd,bknd->bqngk", query_rows, key_portion, preferred_element_type=single_float
            )
            * scale_factor
        )
        allowed = ((start + jnp.arange(block_count))[None, :] <= query_pos[:, None])[
            None, :, None, None, :
        ]
        return (jnp.where(allowed, scores, NEG), allowed, key_portion, value_portion)

    def attend_block(carry, position_block, start):
        peak, total_w, accum = carry
        scores, allowed, key_portion, value_portion = masked_scores(position_block, start)
        new_peak = jnp.maximum(peak, jnp.max(scores, axis=-1))
        weights = jnp.where(allowed, jnp.exp(scores - new_peak[..., None]), 0.0)
        factor = jnp.exp(peak - new_peak)
        total_w = total_w * factor + jnp.sum(weights, axis=-1)
        accum = accum * factor[..., None] + jnp.einsum(
            "bqngk,bknd->bqngd",
            weights.astype(brain_float_half),
            value_portion,
            preferred_element_type=single_float,
        )
        return (new_peak, total_w, accum)

    statistic_shape = (sequences_local, block_span, KEY_VALUE_HEADS, query_groups)
    start_state = (
        jnp.full(statistic_shape, NEG, single_float),
        jnp.zeros(statistic_shape, single_float),
        jnp.zeros(statistic_shape + (HEAD_SIZE,), single_float),
    )
    piece = lax.all_gather(packed, "ctx", axis=1, tiled=True)
    stride = math.gcd(piece.shape[1], block_span)

    def inner(number, state):
        position_block = lax.dynamic_slice_in_dim(piece, number * stride, stride, 1)
        begin = number * stride
        return lax.cond(
            begin <= last_query,
            lambda held: attend_block(held, position_block, begin),
            lambda held: held,
            state,
        )

    state = lax.fori_loop(0, piece.shape[1] // stride, inner, start_state)
    peak, total_w, accum = state
    attention_result = (accum / total_w[..., None]).astype(brain_float_half)
    log_sum_exponent = peak + jnp.log(total_w)
    flat_att = attention_result.reshape(total_rows, QUERY_HEADS * HEAD_SIZE)
    hidden = flat_in + jnp.dot(flat_att, w_output, preferred_element_type=single_float)
    normed_two, rms_two = norm_rows(hidden, gain_two)
    logits = jnp.dot(normed_two, w_router, preferred_element_type=single_float)
    route_flat = routes.reshape(total_rows, TOPK)
    picks = route_flat[..., None] == jnp.arange(EXPERTS)
    chosen = jnp.sum(jnp.where(picks, logits[:, None, :], 0.0), axis=-1)
    probs = jax.nn.softmax(chosen, axis=-1)
    assigned = routes.reshape(sequences_local, block_span * TOPK)
    hits = (assigned[..., None] == jnp.arange(EXPERTS)).astype(jnp.int32)
    rank = jnp.sum((jnp.cumsum(hits, axis=1) - hits) * hits, axis=-1)
    slots = (
        (assigned * sequences_local + jnp.arange(sequences_local)[:, None]) * capacity + rank
    ).reshape(-1)
    sources = (
        jnp.arange(sequences_local)[:, None] * block_span
        + jnp.arange(block_span * TOPK)[None, :] // TOPK
    ).reshape(-1)
    buffer_rows = EXPERTS * sequences_local * capacity
    layout = (n_owner, local_experts, sequences_local * capacity, width)
    outgoing = (
        jnp.zeros((buffer_rows, width), brain_float_half)
        .at[slots]
        .set(normed_two[sources])
        .reshape(layout)
    )
    expert_arrived = lax.all_to_all(outgoing, "expert", split_axis=0, concat_axis=0, tiled=True)
    mixed = jnp.einsum(
        "aerd,edf->aerf", expert_arrived, gateup_weight, preferred_element_type=single_float
    )
    gate_val = mixed[..., :FFE]
    up_val = mixed[..., FFE:]
    expert_activ = (gate_val * jax.nn.sigmoid(gate_val) * up_val).astype(brain_float_half)
    result = jnp.einsum(
        "aerf,efd->aerd", expert_activ, down_weight, preferred_element_type=single_float
    ).astype(brain_float_half)
    expert_out, mixed, activ, arrived = (result, mixed, expert_activ, expert_arrived)
    returned = lax.all_to_all(
        expert_out, "expert", split_axis=0, concat_axis=0, tiled=True
    ).reshape(buffer_rows, width)
    per_route = returned[slots].reshape(total_rows, TOPK, width).astype(single_float)
    combined = jnp.sum(probs[..., None] * per_route, axis=1)
    output = (
        (hidden + combined).astype(brain_float_half).reshape(sequences_local, block_span, width)
    )
    grad = cotangent.reshape(total_rows, width).astype(single_float)
    route_grad = jnp.sum(grad[:, None, :] * per_route, axis=-1)
    sent_grad = (
        (probs[..., None] * grad[:, None, :])
        .astype(brain_float_half)
        .reshape(total_rows * TOPK, width)
    )
    grad_buffer = (
        jnp.zeros((buffer_rows, width), brain_float_half).at[slots].set(sent_grad).reshape(layout)
    )
    arrived_grad = lax.all_to_all(grad_buffer, "expert", split_axis=0, concat_axis=0, tiled=True)
    act_grad = jnp.einsum(
        "aerd,efd->aerf", arrived_grad, down_weight, preferred_element_type=single_float
    )
    gate_val = mixed[..., :FFE]
    up_val = mixed[..., FFE:]
    logistic = jax.nn.sigmoid(gate_val)
    mix_grad = jnp.concatenate(
        [
            act_grad * up_val * logistic * (1.0 + gate_val * (1.0 - logistic)),
            act_grad * gate_val * logistic,
        ],
        axis=-1,
    ).astype(brain_float_half)
    input_back = jnp.einsum(
        "aerf,edf->aerd", mix_grad, gateup_weight, preferred_element_type=single_float
    ).astype(brain_float_half)
    returned_grad = lax.all_to_all(
        input_back, "expert", split_axis=0, concat_axis=0, tiled=True
    ).reshape(buffer_rows, width)
    normed_two_grad = jnp.sum(
        returned_grad[slots].reshape(total_rows, TOPK, width).astype(single_float), axis=1
    )
    expert_sums = lax.psum_scatter(
        jnp.concatenate(
            [
                jnp.einsum(
                    "aerc,aerf->cef", arrived, mix_grad, preferred_element_type=single_float
                ),
                jnp.einsum(
                    "aerf,aerc->cef", activ, arrived_grad, preferred_element_type=single_float
                ),
            ],
            axis=-1,
        ).astype(jnp.bfloat16),
        "ctx",
        scatter_dimension=0,
        tiled=True,
    ).astype(jnp.float32)
    gateup_grad = jnp.transpose(expert_sums[..., : 2 * FFE], (1, 0, 2))
    down_grad = jnp.transpose(expert_sums[..., 2 * FFE :], (1, 2, 0))
    chosen_grad = probs * (route_grad - jnp.sum(probs * route_grad, axis=-1, keepdims=True))
    logit_grad = jnp.sum(jnp.where(picks, chosen_grad[..., None], 0.0), axis=1).astype(
        brain_float_half
    )
    router_full = jnp.dot(normed_two.T, logit_grad, preferred_element_type=single_float)
    normed_two_grad = normed_two_grad + jnp.dot(
        logit_grad, w_router.T, preferred_element_type=single_float
    )
    ffn_gain_full, hidden_part = norm_back(normed_two_grad, hidden, rms_two, gain_two)
    hidden_grad = grad + hidden_part
    hidden_reduced = hidden_grad.astype(brain_float_half)
    outproj_full = jnp.dot(flat_att.T, hidden_reduced, preferred_element_type=single_float)
    attention_result_grad = (
        jnp.dot(hidden_reduced, w_output.T, preferred_element_type=single_float)
        .astype(brain_float_half)
        .reshape(sequences_local, block_span, KEY_VALUE_HEADS, query_groups, HEAD_SIZE)
    )
    delta = jnp.sum(
        attention_result_grad.astype(single_float) * attention_result.astype(single_float), axis=-1
    )

    def back_block(carry, position_block, start):
        query_sum, kv_sum = carry
        block_count = position_block.shape[1]
        scores, allowed, key_portion, value_portion = masked_scores(position_block, start)
        prob_full = jnp.where(allowed, jnp.exp(scores - log_sum_exponent[..., None]), 0.0)
        value_part_grad = jnp.einsum(
            "bqngk,bqngd->bknd",
            prob_full.astype(brain_float_half),
            attention_result_grad,
            preferred_element_type=single_float,
        )
        dots = jnp.einsum(
            "bqngd,bknd->bqngk",
            attention_result_grad,
            value_portion,
            preferred_element_type=single_float,
        )
        score_grad = (prob_full * (dots - delta[..., None]) * scale_factor).astype(brain_float_half)
        query_sum = query_sum + jnp.einsum(
            "bqngk,bknd->bqngd", score_grad, key_portion, preferred_element_type=single_float
        )
        key_part_grad = jnp.einsum(
            "bqngk,bqngd->bknd", score_grad, query_rows, preferred_element_type=single_float
        )
        update = jnp.concatenate(
            [
                key_part_grad.reshape(sequences_local, block_count, key_value_width),
                value_part_grad.reshape(sequences_local, block_count, key_value_width),
            ],
            axis=-1,
        )
        current = lax.dynamic_slice_in_dim(kv_sum, start, block_count, 1)
        kv_sum = lax.dynamic_update_slice_in_dim(kv_sum, current + update, start, 1)
        return (query_sum, kv_sum)

    back_start = (
        jnp.zeros(statistic_shape + (HEAD_SIZE,), single_float),
        jnp.zeros((sequences_local, full_len, 2 * key_value_width), single_float),
    )
    back_piece = lax.all_gather(packed, "ctx", axis=1, tiled=True)
    back_stride = math.gcd(back_piece.shape[1], block_span)

    def inner(number, state):
        position_block = lax.dynamic_slice_in_dim(back_piece, number * back_stride, back_stride, 1)
        begin = number * back_stride
        return lax.cond(
            begin <= last_query,
            lambda held: back_block(held, position_block, begin),
            lambda held: held,
            state,
        )

    back_state = lax.fori_loop(0, back_piece.shape[1] // back_stride, inner, back_start)
    key_value_owned = lax.psum_scatter(
        back_state[1].astype(jnp.bfloat16), "ctx", scatter_dimension=1, tiled=True
    ).astype(jnp.float32)
    query_back = (
        rotary_tables(
            back_state[0].reshape(sequences_local, block_span, QUERY_HEADS, HEAD_SIZE),
            cosine_table,
            -sine_table,
        )
        .astype(brain_float_half)
        .reshape(total_rows, QUERY_HEADS * HEAD_SIZE)
    )
    key_backward = (
        rotary_tables(
            key_value_owned[..., :key_value_width].reshape(
                sequences_local, block_span, KEY_VALUE_HEADS, HEAD_SIZE
            ),
            cosine_table,
            -sine_table,
        )
        .astype(brain_float_half)
        .reshape(total_rows, key_value_width)
    )
    value_backward = (
        key_value_owned[..., key_value_width:]
        .astype(brain_float_half)
        .reshape(total_rows, key_value_width)
    )
    query_full = jnp.dot(normalized_input.T, query_back, preferred_element_type=single_float)
    key_full = jnp.dot(normalized_input.T, key_backward, preferred_element_type=single_float)
    value_full = jnp.dot(normalized_input.T, value_backward, preferred_element_type=single_float)
    normed_one_grad = jnp.dot(query_back, w_query.T, preferred_element_type=single_float)
    normed_one_grad = normed_one_grad + jnp.dot(
        key_backward, key_projection.T, preferred_element_type=single_float
    )
    normed_one_grad = normed_one_grad + jnp.dot(
        value_backward, w_value.T, preferred_element_type=single_float
    )
    attn_gain_full, input_part = norm_back(normed_one_grad, flat_in, rms_one, gain_one)
    input_grad = (
        (hidden_grad + input_part)
        .astype(brain_float_half)
        .reshape(sequences_local, block_span, width)
    )
    reduced = (
        lax.psum_scatter(
            attn_gain_full.astype(jnp.bfloat16), "ctx", scatter_dimension=0, tiled=True
        ).astype(jnp.float32),
        lax.psum_scatter(
            query_full.astype(jnp.bfloat16), "ctx", scatter_dimension=0, tiled=True
        ).astype(jnp.float32),
        lax.psum_scatter(
            key_full.astype(jnp.bfloat16), "ctx", scatter_dimension=0, tiled=True
        ).astype(jnp.float32),
        lax.psum_scatter(
            value_full.astype(jnp.bfloat16), "ctx", scatter_dimension=0, tiled=True
        ).astype(jnp.float32),
        lax.psum_scatter(
            outproj_full.astype(jnp.bfloat16), "ctx", scatter_dimension=0, tiled=True
        ).astype(jnp.float32),
        lax.psum_scatter(
            ffn_gain_full.astype(jnp.bfloat16), "ctx", scatter_dimension=0, tiled=True
        ).astype(jnp.float32),
        lax.psum_scatter(
            router_full.astype(jnp.bfloat16), "ctx", scatter_dimension=0, tiled=True
        ).astype(jnp.float32),
    )
    summed = (
        lax.psum(reduced[0].astype(jnp.bfloat16), "expert").astype(jnp.float32),
        lax.psum(reduced[1].astype(jnp.bfloat16), "expert").astype(jnp.float32),
        lax.psum(reduced[2].astype(jnp.bfloat16), "expert").astype(jnp.float32),
        lax.psum(reduced[3].astype(jnp.bfloat16), "expert").astype(jnp.float32),
        lax.psum(reduced[4].astype(jnp.bfloat16), "expert").astype(jnp.float32),
        lax.psum(reduced[5].astype(jnp.bfloat16), "expert").astype(jnp.float32),
        lax.psum(reduced[6].astype(jnp.bfloat16), "expert").astype(jnp.float32),
    )
    return (
        output,
        input_grad,
        summed[0],
        summed[1],
        summed[2],
        summed[3],
        summed[4],
        summed[5],
        summed[6],
        gateup_grad,
        down_grad,
    )


def solution(mesh):
    placed = (
        P("expert", "ctx", None),
        P("expert", "ctx", None),
        P("expert", "ctx", None),
        P("ctx"),
        P("ctx", None),
        P("ctx", None),
        P("ctx", None),
        P("ctx", None),
        P("ctx"),
        P("ctx", None),
        P("expert", None, None),
        P("expert", None, None),
    )
    return jax.shard_map(
        per_device,
        mesh=mesh,
        in_specs=placed,
        out_specs=(
            P("expert", "ctx", None),
            P("expert", "ctx", None),
            P("ctx"),
            P("ctx", None),
            P("ctx", None),
            P("ctx", None),
            P("ctx", None),
            P("ctx"),
            P("ctx", None),
            P("expert", "ctx", None),
            P("expert", None, "ctx"),
        ),
        check_vma=False,
    )
```

profile of v0, /device:TPU:0, one launch (start us, length us, event | category | flops | bytes accessed | tf_op | source)
XLA Modules:
  0.0 2738.7 jit_solution(8831181291854862279)
XLA Ops:
  13.2 19.2 all-reduce.5
  40.9 23.2 all-gather.9.cloned.1.call-done
  69.3 11.5 reduce-window.6
  86.0 31.0 %all-gather.13.cloned.1.call-done = bf16[1536,1536]{1,0:T(8,128)(2,1)} async-done(((bf16[192,1536]{1,0:T(8,128)(2,1)}), bf16[1536,1536]{1,0:T(8,128)(2,1)}) %all-gather.13.cloned.1.call-update) | async-done | bytes 4718608 | tf_op jit(solution)/shard_map/all_gather | solution.py:83
  130.5 69.4 %all-gather.11.cloned.1.call-done = bf16[1,4096,1024]{1,2,0:T(8,128)(2,1)} async-done(((bf16[1,512,1024]{1,2,0:T(8,128)(2,1)}), bf16[1,4096,1024]{1,2,0:T(8,128)(2,1)}) %all-gather.11.cloned.1.call-update) | async-done | bytes 8388624 | tf_op jit(solution)/shard_map/all_gather | solution.py:164
  202.1 31.0 %while.34 = (s32[]{:T(128)}, f32[1,512,8,3]{1,3,2,0:T(4,128)S(1)}, f32[1,512,8,3]{1,3,2,0:T(4,128)S(1)}, f32[1,512,8,3,64]{1,4,3,2,0:T(8,128)}, s32[]{:T(128)}, ...) while((s32[]{:T(128)}, f32[1,512,8,3]{1,3,2,0:T(4,128)S(1)}, ...), condition=%wide.region_6.7_spmd.clone, body=%wide.region_1.6_spmd.clone.sunk | while | flops 1694274560 | bytes 189018464 | solution.py:177
  202.1 30.7 %conditional.6 = ((f32[1,512,8,3]{1,3,2,0:T(4,128)S(1)}, f32[1,512,8,3]{1,3,2,0:T(4,128)S(1)}, f32[1,512,8,3,64]{1,4,3,2,0:T(8,128)})) conditional(s32[]{:T(128)} %convert_element_type.499, (f32[1,512,8,3]{1,3,2,0:T(4,128)S(1)}, f32[1,512,8,3]{1,3,2,0:T(4,128)S(1)}, f32[1,512,8,3,64]{1,4,3,2,0:T(8,128)}) %tuple.124, (s32[]{:T(128)}, s32[]{:T(128)}, ...), branch_computations={%region_2.0_spmd, %region_3.5_spmd} | conditional | flops 1694274560 | bytes 189016192 | solution.py:170
  218.7 14.0 bitcast_add_fusion
  235.6 16.2 all-gather.15.cloned.1.call-done
  258.8 70.2 %scatter_custom_fusion = bf16[5120,1536]{1,0:T(8,128)(2,1)} fusion(s32[4096]{0:T(1024)} %bitcast.394, bf16[512,1536]{1,0:T(8,128)(2,1)S(1)} %multiply_convert_fusion.1, s32[4096]{0:T(1024)} %broadcast_clamp_fusion.1, bf16[]{:T(256)} %constant.164.clone.1), kind=kCustom, calls=%fused_computation.85 | custom fusion | bytes 15729152 | tf_op jit(solution)/shard_map/scatter | solution.py:204
  336.0 205.4 %all-gather = bf16[8,192,40]{1,2,0:T(8,128)(2,1)S(1)} all-gather(bf16[1,192,40]{1,2,0:T(8,128)(2,1)S(1)} %bitcast.399), channel_id=1, replica_groups=mesh['ctx'=8,'expert'=4] {'ctx'}, dimensions={0}, use_global_device_ids=true | all-gather | bytes 138240 | tf_op jit(solution)/shard_map/all_gather | solution.py:88
  548.3 30.1 %scatter_custom_fusion.1 = bf16[5120,1536]{1,0:T(8,128)(2,1)} fusion(s32[4096]{0:T(1024)} %bitcast.395, f32[512,1536]{1,0:T(8,128)S(1)} %bitcast_convert_fusion.2, f32[4096]{0:T(1024)S(1)} %div.71, bf16[]{:T(256)} %constant.164.clone.1), kind=kCustom, calls=%fused_computation.84 | custom fusion | flops 12582912 | bytes 18891264 | tf_op jit(solution)/shard_map/scatter | solution.py:234
  585.4 30.5 %fusion.72 = f32[4,10,128,1024]{3,2,0,1:T(8,128)} fusion(bf16[10,1536,1024]{2,1,0:T(8,128)(2,1)} %param.30, bf16[4,10,128,1536]{3,2,1,0:T(8,128)(2,1)} %all-to-all-done), kind=kOutput, calls=%fused_computation.101 | convolution fusion | flops 16106127360 | bytes 68157440 | tf_op jit(solution)/shard_map/aerd,edf->aerf/dot_general | solution.py:208
  615.8 141.4 %all-to-all-done.2 = bf16[4,10,128,1536]{3,2,1,0:T(8,128)(2,1)} async-done(((bf16[4,10,128,1536]{3,2,1,0:T(8,128)(2,1)}), bf16[4,10,128,1536]{3,2,1,0:T(8,128)(2,1)}, u32[]{:S(2)}, u32[]{:S(2)}) %all-to-all-start.2) | async-done | bytes 15728672 | tf_op jit(solution)/shard_map/all_to_all | solution.py:236
  757.2 25.6 fusion.69
  782.8 26.8 convert_bitcast_fusion
  809.6 13.4 copy.122
  830.1 16.6 convert_bitcast_fusion.1
  846.7 13.3 copy.119
  860.0 141.2 %all-to-all-done.3 = bf16[4,10,128,1536]{3,2,1,0:T(8,128)(2,1)} async-done(((bf16[4,10,128,1536]{3,2,1,0:T(8,128)(2,1)}), bf16[4,10,128,1536]{3,2,1,0:T(8,128)(2,1)}, u32[]{:S(2)}, u32[]{:S(2)}) %all-to-all-start.3) | async-done | bytes 15728672 | tf_op jit(solution)/shard_map/all_to_all | solution.py:253
  1008.8 33.1 %gather_fusion.1 = bf16[4096,1536]{1,0:T(8,128)(2,1)} fusion(bf16[5120,1536]{1,0:T(8,128)(2,1)} %bitcast.91, s32[4096]{0:T(1024)S(1)} %broadcast_clamp_fusion), kind=kCustom, calls=%fused_computation.2 | custom fusion | bytes 25182208 | tf_op jit(solution)/shard_map/gather | solution.py:257
  1041.9 12.6 convert_reduce_fusion
  1054.5 124.0 %all-to-all-done.1 = bf16[4,10,128,1536]{3,2,1,0:T(8,128)(2,1)} async-done(((bf16[4,10,128,1536]{3,2,1,0:T(8,128)(2,1)}), bf16[4,10,128,1536]{3,2,1,0:T(8,128)(2,1)}, u32[]{:S(2)}, u32[]{:S(2)}) %all-to-all-start.1) | async-done | bytes 15728672 | tf_op jit(solution)/shard_map/all_to_all | solution.py:218
  1178.6 33.0 %gather_fusion = bf16[4096,1536]{1,0:T(8,128)(2,1)} fusion(bf16[5120,1536]{1,0:T(8,128)(2,1)} %bitcast.80, s32[4096]{0:T(1024)S(1)} %broadcast_clamp_fusion), kind=kCustom, calls=%fused_computation.1 | custom fusion | bytes 25182208 | tf_op jit(solution)/shard_map/gather | solution.py:221
  1211.6 17.3 fusion.46
  1255.8 63.7 %while.35 = (s32[]{:T(128)}, f32[1,512,8,3,64]{1,4,3,2,0:T(8,128)}, f32[1,4096,1024]{1,2,0:T(8,128)}, s32[]{:T(128)}, bf16[1,4096,1024]{1,2,0:T(8,128)(2,1)}, /*...) while((s32[]{:T(128)}, f32[1,512,8,3,64]{1,4,3,2,0:T(8,128)}, ...), condition=%wide.region_26.27_spmd.clone, body=%wide.region_23.26_spmd.clone.sunk | while | flops 4110418944 | bytes 145125760 | solution.py:350
  1255.9 63.2 %conditional.7 = ((f32[1,512,8,3,64]{1,4,3,2,0:T(8,128)}, f32[1,4096,1024]{1,2,0:T(8,128)})) conditional(s32[]{:T(128)} %convert_element_type.500, (f32[1,512,8,3,64]{1,4,3,2,0:T(8,128)}, f32[1,4096,1024]{1,2,0:T(8,128)}) %tuple.127, (s32[]{:T(128)}, bf16[1,4096,1024]{1,2,0:T(8,128)(2,1)}, s32[]{:T(128)}, ...), branch_computations={%region_24.24_spmd, %region_25.25_spmd} | conditional | flops 4110418944 | bytes 145123456 | solution.py:343
  1257.2 10.2 fusion.36
  1267.6 17.4 fusion.27
  1285.0 9.5 bitcast_add_fusion.2
  1294.5 12.4 fusion.28
  1306.9 8.4 fusion.34
  1319.4 9.1 convert_element_type.333
  1344.9 604.7 %reduce-scatter.12.cloned.1.call-done = bf16[1,512,1024]{1,2,0:T(8,128)(2,1)} async-done(((bf16[1,4096,1024]{1,2,0:T(8,128)(2,1)}), bf16[1,512,1024]{1,2,0:T(8,128)(2,1)}) %reduce-scatter.12.cloned.1.call-update) | async-done | bytes 1048592 | tf_op jit(solution)/shard_map/reduce_scatter | solution.py:351
  1956.7 28.2 %fusion.48 = bf16[1536,10,1024]{0,2,1:T(8,128)(2,1)} fusion(bf16[4,10,128,1536]{3,2,1,0:T(8,128)(2,1)} %all-to-all-done, bf16[4,10,128,512]{3,2,0,1:T(8,128)(2,1)} %get-tuple-element.692, bf16[4,10,128,512]{3,2,0,1:T(8,128)(2,1)} %get-tuple-element.691), kind=kOutput, calls=%fused_computation.74 | convolution fusion | flops 16142827520 | bytes 57671680 | tf_op jit(solution)/shard_map/aerc,aerf->cef/dot_general | solution.py:262
  1986.3 18.2 fusion.66
  2005.3 55.7 %reduce-scatter.20.cloned.1.call-done = bf16[192,1536]{1,0:T(8,128)(2,1)} async-done(((bf16[1536,1536]{1,0:T(8,128)(2,1)}), bf16[192,1536]{1,0:T(8,128)(2,1)}) %reduce-scatter.20.cloned.1.call-update) | async-done | bytes 589840 | tf_op jit(solution)/shard_map/reduce_scatter | solution.py:408
  2060.9 35.6 %reduce-scatter.16.cloned.1.call-done = bf16[192,512]{1,0:T(8,128)(2,1)} async-done(((bf16[1536,512]{1,0:T(8,128)(2,1)}), bf16[192,512]{1,0:T(8,128)(2,1)}) %reduce-scatter.16.cloned.1.call-update) | async-done | bytes 196624 | tf_op jit(solution)/shard_map/reduce_scatter | solution.py:402
  2096.5 34.2 %reduce-scatter.18.cloned.1.call-done = bf16[192,512]{1,0:T(8,128)(2,1)} async-done(((bf16[1536,512]{1,0:T(8,128)(2,1)}), bf16[192,512]{1,0:T(8,128)(2,1)}) %reduce-scatter.18.cloned.1.call-update) | async-done | bytes 196624 | tf_op jit(solution)/shard_map/reduce_scatter | solution.py:405
  2130.8 33.0 %pad_maximum_fusion = bf16[1536,10,1536]{0,2,1:T(8,128)(2,1)} fusion(bf16[1536,10,512]{0,2,1:T(8,128)(2,1)} %fusion.66, bf16[1536,10,1024]{0,2,1:T(8,128)(2,1)} %fusion.48), kind=kLoop, calls=%fused_computation.61 | loop fusion | flops 94371840 | bytes 94371840 | tf_op jit(solution)/shard_map/concatenate | solution.py:260
  2163.9 60.7 %copy.151 = bf16[1536,15360]{1,0:T(8,128)(2,1)} copy(bf16[1536,15360]{0,1:T(8,128)(2,1)} %bitcast.354) | data formatting | bytes 94371840
  2240.7 14.7 all-reduce.4
  2255.5 16.7 all-reduce.6
  2285.8 396.4 %reduce-scatter.24.cloned.1.call-done = bf16[192,15360]{1,0:T(8,128)(2,1)} async-done(((bf16[1536,15360]{1,0:T(8,128)(2,1)}), bf16[192,15360]{1,0:T(8,128)(2,1)}) %reduce-scatter.24.cloned.1.call-update) | async-done | bytes 5898256
  2682.2 9.6 copy.152
  2691.8 10.1 convert_element_type.351
  2701.9 8.7 slice_bitcast_fusion
  2715.9 10.4 copy.129
  (319 shorter events, 198.5 us)
Async XLA Ops:
  7.2 32.3 %copy-start.9 = (bf16[1,512,1536]{2,1,0:T(8,128)(2,1)S(1)}, bf16[1,512,1536]{2,1,0:T(8,128)(2,1)}, u32[]{:S(2)}) copy-start(bf16[1,512,1536]{2,1,0:T(8,128)(2,1)} %param.20) | copy-start | bytes 4718596
  7.2 30.6 %all-gather.7.cloned.1.call-start = ((), (), s32[]{:S(2)}) async-start(), calls=%async_computation.11 | async-start | bytes 1769472 | tf_op jit(solution)/shard_map/all_gather | solution.py:84
  7.9 56.1 %all-gather.9.cloned.1.call-start = ((), (), s32[]{:S(2)}) async-start(), calls=%async_computation.12 | async-start | bytes 1769472 | tf_op jit(solution)/shard_map/all_gather | solution.py:85
  8.7 108.4 %all-gather.13.cloned.1.call-start = ((), (), s32[]{:S(2)}) async-start(), calls=%async_computation.14 | async-start | bytes 5308416 | tf_op jit(solution)/shard_map/all_gather | solution.py:83
  9.4 190.6 %all-gather.11.cloned.1.call-start = ((), (), s32[]{:S(2)}) async-start(), calls=%async_computation.13 | async-start | bytes 9437184 | tf_op jit(solution)/shard_map/all_gather | solution.py:164
  32.4 31.6 %copy-start.50 = (f32[1536]{0:T(1024)}, f32[1536]{0:T(1024)S(1)}, u32[]{:S(2)}) copy-start(f32[1536]{0:T(1024)S(1)} %convert_element_type.302) | copy-start | bytes 18436
  34.9 29.2 %copy-start.62 = (f32[512]{0:T(512)}, f32[512]{0:T(512)S(1)}, u32[]{:S(2)}) copy-start(f32[512]{0:T(512)S(1)} %get-tuple-element.708) | copy-start | bytes 6148
  67.7 184.1 %all-gather.15.cloned.1.call-start = ((), (), s32[]{:S(2)}) async-start(), calls=%async_computation.15 | async-start | bytes 5308416 | tf_op jit(solution)/shard_map/all_gather | solution.py:86
  210.2 8.5 copy-start
  233.0 23.6 copy-start.16
  233.1 23.6 copy-start.22
  233.1 18.7 copy-start.10
  235.6 21.2 copy-start.32
  257.3 71.6 %copy-start.57 = (f32[512]{0:T(512)}, f32[512]{0:T(512)S(1)}, u32[]{:S(2)}) copy-start(f32[512]{0:T(512)S(1)} %get-tuple-element.710) | copy-start | bytes 6148
  258.8 70.2 %copy-start.7 = (bf16[512,1536]{1,0:T(8,128)(2,1)}, bf16[512,1536]{1,0:T(8,128)(2,1)S(1)}, u32[]{:S(2)}) copy-start(bf16[512,1536]{1,0:T(8,128)(2,1)S(1)} %multiply_convert_fusion.1) | copy-start | bytes 4718596
  329.0 249.4 %all-to-all-start = ((bf16[4,10,128,1536]{3,2,1,0:T(8,128)(2,1)}), bf16[4,10,128,1536]{3,2,1,0:T(8,128)(2,1)}, u32[]{:S(2)}, u32[]{:S(2)}) async-start(bf16[4,10,128,1536]{3,2,1,0:T(8,128)(2,1)} %bitcast.360), calls=%async_computation | async-start | bytes 31457280 | tf_op jit(solution)/shard_map/all_to_all | solution.py:207
  543.5 34.9 %copy-start.3 = (f32[512,1536]{1,0:T(8,128)}, f32[512,1536]{1,0:T(8,128)S(1)}, u32[]{:S(2)}) copy-start(f32[512,1536]{1,0:T(8,128)S(1)} %bitcast_convert_fusion.2) | copy-start | bytes 9437188
  548.1 30.3 %copy-start.24 = (f32[512,8]{1,0:T(8,128)}, f32[512,8]{1,0:T(8,128)S(1)}, u32[]{:S(2)}) copy-start(f32[512,8]{1,0:T(8,128)S(1)} %copy.113) | copy-start | bytes 49156
  578.4 178.8 %all-to-all-start.2 = ((bf16[4,10,128,1536]{3,2,1,0:T(8,128)(2,1)}), bf16[4,10,128,1536]{3,2,1,0:T(8,128)(2,1)}, u32[]{:S(2)}, u32[]{:S(2)}) async-start(bf16[4,10,128,1536]{3,2,1,0:T(8,128)(2,1)} %bitcast.361), calls=%async_computation.2 | async-start | bytes 31457280 | tf_op jit(solution)/shard_map/all_to_all | solution.py:236
  823.1 178.2 %all-to-all-start.3 = ((bf16[4,10,128,1536]{3,2,1,0:T(8,128)(2,1)}), bf16[4,10,128,1536]{3,2,1,0:T(8,128)(2,1)}, u32[]{:S(2)}, u32[]{:S(2)}) async-start(bf16[4,10,128,1536]{3,2,1,0:T(8,128)(2,1)} %copy.122), calls=%async_computation.3 | async-start | bytes 31457280 | tf_op jit(solution)/shard_map/all_to_all | solution.py:253
  860.0 148.1 %copy-start.54 = (s32[4096,1]{0,1:T(1,128)S(1)}, s32[4096,1]{0,1:T(1,128)}, u32[]{:S(2)}) copy-start(s32[4096,1]{0,1:T(1,128)} %compare_select_fusion.1) | copy-start | bytes 49156
  860.0 148.1 %copy-start.17 = (f32[1,512,8,3]{1,3,2,0:T(4,128)S(1)}, f32[1,512,8,3]{1,3,2,0:T(4,128)}, u32[]{:S(2)}) copy-start(f32[1,512,8,3]{1,3,2,0:T(4,128)} %copy-done.16) | copy-start | bytes 147460
  860.0 148.1 %copy-start.23 = (f32[1,512,8,3]{1,3,2,0:T(4,128)S(1)}, f32[1,512,8,3]{1,3,2,0:T(4,128)}, u32[]{:S(2)}) copy-start(f32[1,512,8,3]{1,3,2,0:T(4,128)} %copy-done.22) | copy-start | bytes 147460
  1001.2 177.3 %all-to-all-start.1 = ((bf16[4,10,128,1536]{3,2,1,0:T(8,128)(2,1)}), bf16[4,10,128,1536]{3,2,1,0:T(8,128)(2,1)}, u32[]{:S(2)}, u32[]{:S(2)}) async-start(bf16[4,10,128,1536]{3,2,1,0:T(8,128)(2,1)} %copy.119), calls=%async_computation.1 | async-start | bytes 31457280 | tf_op jit(solution)/shard_map/all_to_all | solution.py:218
  1008.0 941.6 %reduce-scatter.12.cloned.1.call-start = ((), (), s32[]{:S(2)}) async-start(), calls=%async_computation.16 | async-start | bytes 9437184 | tf_op jit(solution)/shard_map/reduce_scatter | solution.py:351
  1178.5 33.0 %copy-start.4 = (f32[512,1536]{1,0:T(8,128)S(1)}, f32[512,1536]{1,0:T(8,128)}, u32[]{:S(2)}) copy-start(f32[512,1536]{1,0:T(8,128)} %copy-done.3) | copy-start | bytes 9437188
  1178.5 33.0 %copy-start.25 = (f32[512,8]{1,0:T(8,128)S(1)}, f32[512,8]{1,0:T(8,128)}, u32[]{:S(2)}) copy-start(f32[512,8]{1,0:T(8,128)} %copy-done.24) | copy-start | bytes 49156
  1211.5 18.4 copy-start.41
  1211.5 18.4 copy-start.56
  1211.6 18.4 copy-start.60
  1211.6 18.5 copy-start.46
  1211.6 18.5 copy-start.49
  1211.6 18.5 copy-start.58
  1230.2 9.1 slice-start
  1247.9 7.9 copy-start.53
  1285.0 9.5 copy-start.21
  1328.5 676.7 %reduce-scatter.14.cloned.1.call-start = ((), (), s32[]{:S(2)}) async-start(), calls=%async_computation.17 | async-start | bytes 5308416 | tf_op jit(solution)/shard_map/reduce_scatter | solution.py:399
  1337.2 723.7 %reduce-scatter.20.cloned.1.call-start = ((), (), s32[]{:S(2)}) async-start(), calls=%async_computation.20 | async-start | bytes 5308416 | tf_op jit(solution)/shard_map/reduce_scatter | solution.py:408
  1344.8 607.0 %copy-start.12 = (bf16[1,512,1536]{2,1,0:T(8,128)(2,1)S(1)}, bf16[1,512,1536]{2,1,0:T(8,128)(2,1)}, u32[]{:S(2)}) copy-start(bf16[1,512,1536]{2,1,0:T(8,128)(2,1)} %param.20) | copy-start | bytes 4718596
  1344.8 751.7 %reduce-scatter.16.cloned.1.call-start = ((), (), s32[]{:S(2)}) async-start(), calls=%async_computation.18 | async-start | bytes 1769472 | tf_op jit(solution)/shard_map/reduce_scatter | solution.py:402
  1954.2 176.5 %reduce-scatter.18.cloned.1.call-start = ((), (), s32[]{:S(2)}) async-start(), calls=%async_computation.19 | async-start | bytes 1769472 | tf_op jit(solution)/shard_map/reduce_scatter | solution.py:405
  1956.6 28.3 %copy-start.8 = (bf16[512,1536]{1,0:T(8,128)(2,1)S(1)}, bf16[512,1536]{1,0:T(8,128)(2,1)}, u32[]{:S(2)}) copy-start(bf16[512,1536]{1,0:T(8,128)(2,1)} %copy-done.7) | copy-start | bytes 4718596
  1956.7 28.3 %copy-start.43 = (bf16[512,40]{0,1:T(8,128)(2,1)S(1)}, bf16[512,40]{0,1:T(8,128)(2,1)}, u32[]{:S(2)}) copy-start(bf16[512,40]{0,1:T(8,128)(2,1)} %copy-done.42) | copy-start | bytes 122884
  1956.7 275.8 %reduce-scatter.22.cloned.1.call-start = ((), (), s32[]{:S(2)}) async-start(), calls=%async_computation.21 | async-start | bytes 442368
  1986.3 292.7 %all-reduce.10.cloned.1.call-start = ((), (), s32[]{:S(2)}) async-start(), calls=%async_computation.23 | async-start | bytes 3145728 | tf_op jit(solution)/shard_map/psum | solution.py:420
  2130.8 551.5 %reduce-scatter.24.cloned.1.call-start = ((), (), s32[]{:S(2)}) async-start(), calls=%async_computation.22 | async-start | bytes 53084160
  2225.2 8.1 copy-start.19
  2237.4 36.6 %copy-start.67 = (f32[512]{0:T(512)S(1)}, f32[512]{0:T(512)}, u32[]{:S(2)}) copy-start(f32[512]{0:T(512)} %get-tuple-element.707) | copy-start | bytes 6148
  (39 other events, 138.3 us)
Sparse Core Ops, SparseCore 0:
  9.7 28.0 all-gather.6
  39.4 24.5 all-gather.8
  65.7 51.2 all-gather.12
  119.1 80.8 all-gather.10
  201.4 50.2 all-gather.14
  1328.6 620.9 reduce-scatter.11
  1951.9 53.3 reduce-scatter.13
  2007.6 53.3 reduce-scatter.19
  2063.8 32.6 reduce-scatter.15
  2098.7 32.0 reduce-scatter.17
  2133.6 28.7 reduce-scatter.21
  2166.0 59.6 all-reduce.9
  2228.0 454.1 reduce-scatter.23
where the time goes:
time: 2750 us; the launch traced here: 2740 us
  waiting for transfers between devices  1680 us (61%)
  local copies, waits for them, and re-layouts  310 us (11%)
  matrix products  278 us (10%)
  blocking collectives  256 us (9%)
  other arithmetic  170 us (6%)
  starting transfers between devices  28.8 us (1%)
    reduce_scatter x1, waiting for transfers between devices, per_device(): lax.psum_scatter(back_state[1].astype(jnp.bfloat16), 'ctx', scatter_dimen...  605 us
    unnamed x15, waiting for transfers between devices  399 us
    all_gather x1, blocking collectives, per_device(): lax.all_gather(router_weight, 'ctx', axis=0, tiled=True)  205 us
    all_to_all x1, waiting for transfers between devices, per_device(): lax.all_to_all(grad_buffer, 'expert', split_axis=0, concat_axis=0, tiled=...  141 us
    all_to_all x1, waiting for transfers between devices, per_device(): lax.all_to_all(input_back, 'expert', split_axis=0, concat_axis=0, tiled=T...  141 us
    all_to_all x1, waiting for transfers between devices, per_device(): lax.all_to_all(expert_out, 'expert', split_axis=0, concat_axis=0, tiled=T...  124 us
    unnamed x152, local copies, waits for them, and re-layouts  103 us
    scatter x1, local copies, waits for them, and re-layouts, per_device(): outgoing = jnp.zeros((buffer_rows, width), brain_float_half).at[slots].se...  70.2 us
  transfers between devices with their start and end apart: 17, of which 14 were waited for; matrix products, arithmetic and copies ran while one was open for 15% of the time, Pallas kernels for 0%

commit v1 on v0

v1 whole, which is shorter than its diff:
```python
import functools

import jax
import jax.numpy as jnp
from jax import lax
from jax.experimental import pallas as pl
from jax.experimental.pallas import tpu as pltpu
from jax.sharding import PartitionSpec as P

QUERY_HEADS = 24
KEY_VALUE_HEADS = 8
HEAD_SIZE = 64
GROUP = QUERY_HEADS // KEY_VALUE_HEADS
QROWS = GROUP * HEAD_SIZE
SLICE = QROWS + 2 * HEAD_SIZE
FFE = 512
EXPERTS = 40
TOPK = 8
EXTRA = 128

EPS = 1e-05
NEG = -1e30
THETA = 10000.0

F32 = jnp.float32
BF16 = jnp.bfloat16
VMEM_LIMIT = 60 * 1024 * 1024
COST = pl.CostEstimate(flops=1024, bytes_accessed=1024, transcendentals=0)


def contract(left, right, a, b):
    return lax.dot_general(left, right, (((a,), (b,)), ((), ())), preferred_element_type=F32)


def params(*order):
    return pltpu.CompilerParams(vmem_limit_bytes=VMEM_LIMIT, dimension_semantics=order)


def whole(*shape):
    return pl.BlockSpec(shape, lambda *_: (0,) * len(shape))


def project_kernel(x_ref, gain_ref, w_ref, table_ref, *refs):
    n_ref, q_ref, kv_ref = refs[-3:]
    half = HEAD_SIZE // 2
    x = x_ref[0].astype(F32)
    factor = lax.rsqrt(jnp.mean(x * x, axis=-1, keepdims=True) + EPS)
    normed = (x * factor * gain_ref[...]).astype(BF16)
    n_ref[0] = normed
    raw = contract(w_ref[...], normed, 1, 1)
    cosine, sine = table_ref[0, :half], table_ref[0, half:]
    scale = HEAD_SIZE**-0.5
    for g in range(GROUP + 1):
        a, b = raw[g * HEAD_SIZE : g * HEAD_SIZE + half], raw[g * HEAD_SIZE + half : (g + 1) * HEAD_SIZE]
        turned = jnp.concatenate([a * cosine - b * sine, b * cosine + a * sine], axis=0).astype(BF16)
        if g < GROUP:
            q_ref[0, g * HEAD_SIZE : (g + 1) * HEAD_SIZE, :] = turned * BF16(scale)
        else:
            kv_ref[0, :HEAD_SIZE, :] = turned
    kv_ref[0, HEAD_SIZE:, :] = raw[QROWS + HEAD_SIZE :].astype(BF16)


def project(x, gain, w_rows, table, which, held):
    blocks, columns, width = x.shape
    span = table.shape[2]
    shapes = [(blocks, span, width), (blocks, QROWS, span), (blocks, 2 * HEAD_SIZE, span)]
    return pl.pallas_call(
        project_kernel,
        grid=(blocks,),
        in_specs=[
            pl.BlockSpec((1, columns, width), lambda b: (b, 0, 0)),
            whole(1, width),
            whole(SLICE, width),
            pl.BlockSpec((1, HEAD_SIZE, columns), lambda b: (b, 0, which)),
        ]
        + [pl.BlockSpec(memory_space=pl.ANY)] * len(held),
        out_specs=[
            pl.BlockSpec((1, columns, width), lambda b: (b, which, 0)),
            pl.BlockSpec((1, QROWS, columns), lambda b: (b, 0, which)),
            pl.BlockSpec((1, 2 * HEAD_SIZE, columns), lambda b: (b, 0, which)),
        ],
        out_shape=[jax.ShapeDtypeStruct(shape, BF16) for shape in shapes],
        input_output_aliases={4 + i: i for i in range(len(held))},
        compiler_params=params("arbitrary"),
        cost_estimate=COST,
        name="project",
    )(x, gain, w_rows, table, *held)


def head_grads_kernel(back_ref, n_ref, grad_ref, acc):
    b = pl.program_id(0)
    part = contract(n_ref[0], back_ref[0], 0, 1)

    @pl.when(b == 0)
    def _():
        acc[...] = part

    @pl.when(b > 0)
    def _():
        acc[...] += part

    @pl.when(b == pl.num_programs(0) - 1)
    def _():
        grad_ref[...] = acc[...].astype(BF16)


def head_grads(back, normed):
    blocks, rows, span = back.shape
    width = normed.shape[2]
    return pl.pallas_call(
        head_grads_kernel,
        grid=(blocks,),
        in_specs=[
            pl.BlockSpec((1, rows, span), lambda b: (b, 0, 0)),
            pl.BlockSpec((1, span, width), lambda b: (b, 0, 0)),
        ],
        out_specs=whole(width, rows),
        out_shape=jax.ShapeDtypeStruct((width, rows), BF16),
        scratch_shapes=[pltpu.VMEM((width, rows), F32)],
        compiler_params=params("arbitrary"),
        cost_estimate=COST,
        name="head_grads",
    )(back, normed)


def key_tiles(first, count, sub, span, part, bk):
    low = (first // sub) * span + part * sub + first % sub
    last = first + count - 1
    high = (last // sub) * span + part * sub + last % sub
    return (low + 1) // bk, (high + bk) // bk


def loop(first, last, step):
    def body(j, carry):
        step(j)
        return carry

    lax.fori_loop(first, last, body, 0)


def unpack_blocks(refs, out):
    groups, size, _ = out.shape
    for i in range(refs.shape[0]):
        columns = refs.shape[2]
        for g in range(groups):
            out[g, :, i * columns : (i + 1) * columns] = refs[i, g * size : (g + 1) * size, :]


def attend_kernel(bk, sub, span, part_ref, pos_ref, q_ref, kv_ref, o_ref, lse_ref, q, keys, values, peak, total, acc):
    groups, size, bq = q.shape
    tile = pl.program_id(0)

    @pl.when(tile == 0)
    def _():
        for i in range(kv_ref.shape[0]):
            part = slice(i * span, (i + 1) * span)
            keys[part, :] = jnp.transpose(kv_ref[i, :size, :], (1, 0))
            values[:, part] = kv_ref[i, size:, :]

    unpack_blocks(q_ref, q)
    unmasked, ends = key_tiles(tile * bq, bq, sub, span, part_ref[0], bk)
    peak[...] = jnp.full(peak.shape, NEG, F32)
    total[...] = jnp.zeros(total.shape, F32)
    acc[...] = jnp.zeros(acc.shape, F32)

    def step(j, masked):
        start = pl.multiple_of(j * bk, bk)
        k = keys[pl.ds(start, bk), :]
        v = values[:, pl.ds(start, bk)]
        if masked:
            allowed = (start + lax.broadcasted_iota(jnp.int32, (bk, bq), 0)) <= pos_ref[...]
        for g in range(groups):
            scores = jnp.dot(k, q[g], preferred_element_type=F32)
            if masked:
                scores = jnp.where(allowed, scores, NEG)
            old = peak[g]
            new = jnp.maximum(old, jnp.max(scores, axis=0, keepdims=True))
            weights = jnp.exp(scores - new)
            factor = jnp.exp(old - new)
            peak[g] = new
            total[g] = total[g] * factor + jnp.sum(weights, axis=0, keepdims=True)
            acc[g] = acc[g] * factor + jnp.dot(v, weights.astype(BF16), preferred_element_type=F32)

    loop(0, unmasked, lambda j: step(j, False))
    loop(unmasked, ends, lambda j: step(j, True))
    for g in range(groups):
        out = (acc[g] / total[g]).astype(BF16)
        lse_ref[g] = peak[g] + jnp.log(total[g])
        for i in range(o_ref.shape[0]):
            o_ref[i, g * size : (g + 1) * size, :] = out[:, i * o_ref.shape[2] : (i + 1) * o_ref.shape[2]]


def attend(part, pos, q, kv, bq, bk, sub, span):
    nq, blocks = pos.shape[1], pos.shape[1] // sub
    nk = blocks * span
    groups, size, rows = GROUP, HEAD_SIZE, QROWS
    tile = pl.BlockSpec((bq // sub, rows, sub), lambda i: (i, 0, 0))
    stat = pl.BlockSpec((groups, 1, bq), lambda i: (0, 0, i))
    return pl.pallas_call(
        functools.partial(attend_kernel, bk, sub, span),
        grid=(nq // bq,),
        in_specs=[
            pl.BlockSpec(memory_space=pltpu.SMEM),
            pl.BlockSpec((1, bq), lambda i: (0, i)),
            tile,
            whole(blocks, 2 * size, span),
        ],
        out_specs=[tile, stat],
        out_shape=[
            jax.ShapeDtypeStruct((blocks, rows, sub), BF16),
            jax.ShapeDtypeStruct((groups, 1, nq), F32),
        ],
        scratch_shapes=[
            pltpu.VMEM((groups, size, bq), BF16),
            pltpu.VMEM((nk, size), BF16),
            pltpu.VMEM((size, nk), BF16),
            pltpu.VMEM((groups, 1, bq), F32),
            pltpu.VMEM((groups, 1, bq), F32),
            pltpu.VMEM((groups, size, bq), F32),
        ],
        compiler_params=params("arbitrary"),
        cost_estimate=COST,
        name="attend",
    )(part, pos, q, kv)


def turn_back(rows, cosine, sine):
    half = HEAD_SIZE // 2
    a, b = rows[:half], rows[half:]
    return jnp.concatenate([a * cosine + b * sine, b * cosine - a * sine], axis=0)


def attend_back_kernel(
    bk, sub, span, part_ref, pos_ref, q_ref, o_ref, do_ref, lse_ref, kv_ref, qtab_ref, ktab_ref, *refs
):
    *outs, q, keys, keys_t, values, q_rows, do, do_rows, delta, dq, dk, dv = refs
    dq_ref, dkv_ref = outs[0], outs[-1]
    groups, size, bq = q.shape
    half = size // 2
    tile = pl.program_id(0)

    @pl.when(tile == 0)
    def _():
        for i in range(kv_ref.shape[0]):
            part = slice(i * span, (i + 1) * span)
            keys[part, :] = jnp.transpose(kv_ref[i, :size, :], (1, 0))
            keys_t[:, part] = kv_ref[i, :size, :]
            values[part, :] = jnp.transpose(kv_ref[i, size:, :], (1, 0))
        dk[...] = jnp.zeros(dk.shape, F32)
        dv[...] = jnp.zeros(dv.shape, F32)

    unpack_blocks(q_ref, q)
    unpack_blocks(do_ref, do)
    pieces, columns = do_ref.shape[0], do_ref.shape[2]
    for g in range(groups):
        for i in range(pieces):
            both = do_ref[i, g * size : (g + 1) * size, :].astype(F32) * o_ref[i, g * size : (g + 1) * size, :].astype(F32)
            delta[g, :, i * columns : (i + 1) * columns] = jnp.sum(both, axis=0, keepdims=True)
        q_rows[g] = jnp.transpose(q[g], (1, 0))
        do_rows[g] = jnp.transpose(do[g], (1, 0))
    dq[...] = jnp.zeros(dq.shape, F32)
    unmasked, ends = key_tiles(tile * bq, bq, sub, span, part_ref[0], bk)

    def step(j, masked):
        start = pl.multiple_of(j * bk, bk)
        k = keys[pl.ds(start, bk), :]
        kt = keys_t[:, pl.ds(start, bk)]
        v = values[pl.ds(start, bk), :]
        if masked:
            allowed = (start + lax.broadcasted_iota(jnp.int32, (bk, bq), 0)) <= pos_ref[...]
        dv_part = jnp.zeros((bk, size), F32)
        dk_part = jnp.zeros((bk, size), F32)
        for g in range(groups):
            scores = jnp.dot(k, q[g], preferred_element_type=F32)
            prob = jnp.exp(scores - lse_ref[g])
            if masked:
                prob = jnp.where(allowed, prob, 0.0)
            dv_part = dv_part + jnp.dot(prob.astype(BF16), do_rows[g], preferred_element_type=F32)
            dots = jnp.dot(v, do[g], preferred_element_type=F32)
            score_grad = (prob * (dots - delta[g])).astype(BF16)
            dk_part = dk_part + jnp.dot(score_grad, q_rows[g], preferred_element_type=F32)
            dq[g] += jnp.dot(kt, score_grad, preferred_element_type=F32)
        dv[pl.ds(start, bk), :] += dv_part
        dk[pl.ds(start, bk), :] += dk_part

    loop(0, unmasked, lambda j: step(j, False))
    loop(unmasked, ends, lambda j: step(j, True))
    scale = HEAD_SIZE**-0.5
    packed = len(outs) == 1
    for i in range(pieces):
        cols = slice(i * columns, (i + 1) * columns)
        for g in range(groups):
            out = turn_back(dq[g, :, cols], qtab_ref[i, :half], qtab_ref[i, half:])
            dq_ref[tile if packed else i, g * size : (g + 1) * size, :] = (out * scale).astype(BF16)

    @pl.when(tile == pl.num_programs(0) - 1)
    def _():
        base = QROWS if packed else 0
        for i in range(dkv_ref.shape[0]):
            part = slice(i * span, (i + 1) * span)
            back = turn_back(jnp.transpose(dk[part, :], (1, 0)), ktab_ref[i, :half], ktab_ref[i, half:])
            dkv_ref[i, base : base + size, :] = back.astype(BF16)
            dkv_ref[i, base + size : base + 2 * size, :] = jnp.transpose(dv[part, :], (1, 0)).astype(BF16)


def attend_back(part, pos, q, o, do, lse, kv, qtab, ktab, bq, bk, sub, span):
    nq, blocks = pos.shape[1], pos.shape[1] // sub
    nk = blocks * span
    groups, size, rows = GROUP, HEAD_SIZE, QROWS
    tile = pl.BlockSpec((bq // sub, rows, sub), lambda i: (i, 0, 0))
    if sub == span == bq:
        out_specs = [whole(blocks, SLICE, span)]
        out_shape = [jax.ShapeDtypeStruct((blocks, SLICE, span), BF16)]
    else:
        out_specs = [tile, whole(blocks, 2 * size, span)]
        out_shape = [
            jax.ShapeDtypeStruct((blocks, rows, sub), BF16),
            jax.ShapeDtypeStruct((blocks, 2 * size, span), BF16),
        ]
    return pl.pallas_call(
        functools.partial(attend_back_kernel, bk, sub, span),
        grid=(nq // bq,),
        in_specs=[
            pl.BlockSpec(memory_space=pltpu.SMEM),
            pl.BlockSpec((1, bq), lambda i: (0, i)),
            tile,
            tile,
            tile,
            pl.BlockSpec((groups, 1, bq), lambda i: (0, 0, i)),
            whole(blocks, 2 * size, span),
            pl.BlockSpec((bq // sub, size, sub), lambda i: (i, 0, 0)),
            whole(blocks, size, span),
        ],
        out_specs=out_specs,
        out_shape=out_shape,
        scratch_shapes=[
            pltpu.VMEM((groups, size, bq), BF16),
            pltpu.VMEM((nk, size), BF16),
            pltpu.VMEM((size, nk), BF16),
            pltpu.VMEM((nk, size), BF16),
            pltpu.VMEM((groups, bq, size), BF16),
            pltpu.VMEM((groups, size, bq), BF16),
            pltpu.VMEM((groups, bq, size), BF16),
            pltpu.VMEM((groups, 1, bq), F32),
            pltpu.VMEM((groups, size, bq), F32),
            pltpu.VMEM((nk, size), F32),
            pltpu.VMEM((nk, size), F32),
        ],
        compiler_params=params("arbitrary"),
        cost_estimate=COST,
        name="attend_back",
    )(part, pos, q, o, do, lse, kv, qtab, ktab)


def chosen_rows(rank, cap):
    return lax.broadcasted_iota(jnp.int32, (cap, rank.shape[1]), 0) == rank


def dispatch_kernel(cap, rank_ref, token_ref, row_ref):
    for e in range(rank_ref.shape[0]):
        one = chosen_rows(rank_ref[e], cap).astype(F32).astype(BF16)
        row_ref[e] = jnp.dot(one, token_ref[...], preferred_element_type=F32).astype(BF16)


def dispatch(rank, tokens, block, cap, wide):
    count = rank.shape[0]
    span, width = tokens.shape
    return pl.pallas_call(
        functools.partial(dispatch_kernel, cap),
        grid=(width // wide,),
        in_specs=[
            pl.BlockSpec((count, 1, span), lambda i: (0, 0, block)),
            pl.BlockSpec((span, wide), lambda i: (0, i)),
        ],
        out_specs=pl.BlockSpec((count, cap, wide), lambda i: (0, 0, i)),
        out_shape=jax.ShapeDtypeStruct((count, cap, width), BF16),
        compiler_params=params("arbitrary"),
        cost_estimate=COST,
        name="dispatch",
    )(rank, tokens)


def experts_kernel(span, cap, offset, blocks, place_ref, rank_ref, prob_ref, *refs):
    x_refs, g_refs = refs[:blocks], refs[blocks : 2 * blocks]
    gu_ref, dn_ref, back_ref, out_ref, mine_ref, theirs_ref, grads = refs[2 * blocks :]
    e = pl.program_id(0)
    x = jnp.concatenate([ref[0] for ref in x_refs], axis=0)
    g = jnp.concatenate([ref[0] for ref in g_refs], axis=0)
    width = x.shape[1]
    ps = []
    for i in range(blocks):
        rows = slice(i * span, (i + 1) * span)
        hit = chosen_rows(rank_ref[0, :, rows], cap)
        ps.append(jnp.sum(jnp.where(hit, prob_ref[0, :, rows], 0.0), axis=1, keepdims=True))
    prob = jnp.concatenate(ps, axis=0)
    mixed = jnp.dot(x, gu_ref[0], preferred_element_type=F32)
    gate, up = mixed[:, :FFE], mixed[:, FFE:]
    logistic = 1.0 / (1.0 + jnp.exp(-gate))
    act = (gate * logistic * up).astype(BF16)
    sent = (prob * g.astype(F32)).astype(BF16)
    act_grad = contract(sent, dn_ref[0], 1, 1)
    mix = jnp.concatenate(
        [act_grad * up * logistic * (1.0 + gate * (1.0 - logistic)), act_grad * gate * logistic], axis=1
    ).astype(BF16)
    out = jnp.dot(act, dn_ref[0], preferred_element_type=F32).astype(BF16).astype(F32)
    route = jnp.sum(g.astype(F32) * out, axis=1, keepdims=True)
    out_ref[0] = (prob * out).astype(BF16)
    back_ref[0, :, :width] = contract(mix, gu_ref[0], 1, 1).astype(BF16)
    high = route.astype(BF16).astype(F32)
    place = lax.broadcasted_iota(jnp.int32, (route.shape[0], EXTRA), 1) - (place_ref[0] + offset + e)
    extra = jnp.where(place == 0, high, jnp.where(place == EXPERTS, route - high, 0.0))
    back_ref[0, :, width:] = extra.astype(BF16)
    grads[:, : 2 * FFE] = contract(x, mix, 0, 0).astype(BF16)
    grads[:, 2 * FFE :] = contract(sent, act, 0, 0).astype(BF16)
    pairs, _, own, _ = mine_ref.shape
    core = place_ref[1]
    for i in range(pairs):
        mine_ref[i, 0] = grads[pl.ds(pl.multiple_of((2 * i + core) * own, own), own), :]
        theirs_ref[i, 0] = grads[pl.ds(pl.multiple_of((2 * i + 1 - core) * own, own), own), :]


def run_experts(place, rank, prob, xs, gs, gateup, down, offset, count, n_ctx, span, cap):
    blocks = len(xs)
    width = gateup.shape[1]
    rows = blocks * cap
    tokens = blocks * span
    own = width // n_ctx
    pairs = n_ctx // 2

    def picked(*shape):
        return pl.BlockSpec((1,) + shape, lambda e: (e + offset, 0, 0))

    def row(wide):
        return pl.BlockSpec((1, rows, wide), lambda e: (e, 0, 0))

    half = pl.BlockSpec((pairs, 1, own, 3 * FFE), lambda e: (0, e, 0, 0))
    half_shape = jax.ShapeDtypeStruct((pairs, count, own, 3 * FFE), BF16)
    return pl.pallas_call(
        functools.partial(experts_kernel, span, cap, offset, blocks),
        grid=(count,),
        in_specs=[pl.BlockSpec(memory_space=pltpu.SMEM), picked(1, tokens), picked(1, tokens)]
        + [picked(cap, width)] * (2 * blocks)
        + [picked(width, 2 * FFE), picked(FFE, width)],
        out_specs=[row(width + EXTRA), row(width), half, half],
        out_shape=[
            jax.ShapeDtypeStruct((count, rows, width + EXTRA), BF16),
            jax.ShapeDtypeStruct((count, rows, width), BF16),
            half_shape,
            half_shape,
        ],
        scratch_shapes=[pltpu.VMEM((width, 3 * FFE), BF16)],
        compiler_params=params("arbitrary"),
        cost_estimate=COST,
        name="experts",
    )(place, rank, prob, *xs, *gs, gateup, down)


def unpack_kernel(sum_ref, *refs):
    gateup_ref, down_ref = refs[-2:]
    gateup_ref[0] = sum_ref[0, :, : 2 * FFE].astype(F32)
    down_ref[0] = jnp.transpose(sum_ref[0, :, 2 * FFE :].astype(F32), (1, 0))


def unpack(total, offset, experts, held):
    count, own, wide = total.shape
    return pl.pallas_call(
        unpack_kernel,
        grid=(count,),
        in_specs=[pl.BlockSpec((1, own, wide), lambda e: (e, 0, 0))] + [pl.BlockSpec(memory_space=pl.ANY)] * len(held),
        out_specs=[
            pl.BlockSpec((1, own, 2 * FFE), lambda e: (e + offset, 0, 0)),
            pl.BlockSpec((1, FFE, own), lambda e: (e + offset, 0, 0)),
        ],
        out_shape=[
            jax.ShapeDtypeStruct((experts, own, 2 * FFE), F32),
            jax.ShapeDtypeStruct((experts, FFE, own), F32),
        ],
        input_output_aliases={1 + i: i for i in range(len(held))},
        compiler_params=params("arbitrary"),
        cost_estimate=COST,
        name="unpack",
    )(total, *held)


def combine_kernel(cap, n_parts, *refs):
    rank_refs, row_refs, out_ref = refs[:n_parts], refs[n_parts : 2 * n_parts], refs[-1]
    total = None
    for rank_ref, row_ref in zip(rank_refs, row_refs):
        ones, rows = [], []
        for e in range(rank_ref.shape[0]):
            ones.append(chosen_rows(rank_ref[e], cap).astype(F32).astype(BF16))
            rows.append(row_ref[e])
        part = contract(jnp.concatenate(ones, axis=0), jnp.concatenate(rows, axis=0), 0, 0)
        total = part if total is None else total + part
    out_ref[...] = total.astype(BF16)


def combine(ranks, rows, block, span, cap, wide):
    width = rows[0].shape[2]
    count = sum(r.shape[0] for r in ranks)
    return pl.pallas_call(
        functools.partial(combine_kernel, cap, len(ranks)),
        grid=(width // wide,),
        in_specs=[pl.BlockSpec((r.shape[0], 1, span), lambda i: (0, 0, block)) for r in ranks]
        + [pl.BlockSpec((r.shape[0], cap, wide), lambda i: (0, block, i)) for r in rows],
        out_specs=pl.BlockSpec((span, wide), lambda i: (0, i)),
        out_shape=jax.ShapeDtypeStruct((span, width), BF16),
        compiler_params=params("arbitrary"),
        cost_estimate=COST,
        name="combine",
    )(*ranks, *rows)


def swapped(array, axis, mask):
    count = lax.axis_size(axis)
    return lax.ppermute(array, axis, [(i, i ^ mask) for i in range(count)])


def gather_blocks(array, axis):
    count = lax.axis_size(axis)
    if count != 4:
        return [array] + [swapped(array, axis, k) for k in range(1, count)]
    half = array.shape[0] // 2
    one, two = swapped(array, axis, 1), swapped(array, axis, 2)
    far = jnp.concatenate([swapped(two[:half], axis, 1), swapped(one[half:], axis, 2)], axis=0)
    return [array, one, two, far]


def gather_start(array, axis):
    return [array, swapped(array, axis, 1), swapped(array, axis, 2)]


def gather_end(array, one, two, axis):
    count = lax.axis_size(axis)
    if count != 4:
        return [array, one, two] + [swapped(array, axis, k) for k in range(3, count)]
    half = array.shape[0] // 2
    far = jnp.concatenate([swapped(two[:half], axis, 1), swapped(one[half:], axis, 2)], axis=0)
    return [array, one, two, far]


def gather_rows(array, axis, use, early):
    count = lax.axis_size(axis)
    if count != 4:
        return [use(block, k) for k, block in enumerate(gather_blocks(array, axis))], early
    half = array.shape[0] // 2
    one, two = swapped(array, axis, 1), swapped(array, axis, 2)
    own = use(array, 0)
    own, one, two, early = lax.optimization_barrier((own, one, two, early))
    far = jnp.concatenate([swapped(two[:half], axis, 1), swapped(one[half:], axis, 2)], axis=0)
    return [own, use(one, 1), use(two, 2), use(far, 3)], early


def wide_sum(*arrays):
    return sum(array.astype(F32) for array in arrays)


def return_start(parts, axis):
    if lax.axis_size(axis) != 4:
        return [parts[0]] + [swapped(parts[k], axis, k) for k in range(1, len(parts))]
    own, one, two, far = parts
    half = own.shape[0] // 2
    via_one, via_two = swapped(far[:half], axis, 1), swapped(far[half:], axis, 2)
    return [own, one, two, via_one, via_two, swapped(one[:half], axis, 1), swapped(two[half:], axis, 2)]


def return_end(held, axis):
    if lax.axis_size(axis) != 4:
        return wide_sum(*held)
    own, one, two, via_one, via_two, one_low, two_high = held
    half = own.shape[0] // 2
    one_high = swapped(wide_sum(one[half:], via_two).astype(BF16), axis, 1)
    two_low = swapped(wide_sum(two[:half], via_one).astype(BF16), axis, 2)
    return jnp.concatenate(
        [wide_sum(own[:half], one_low, two_low), wide_sum(own[half:], one_high, two_high)], axis=0
    )


def for_partners(array, axis, dim):
    count, me = lax.axis_size(axis), lax.axis_index(axis)
    return [lax.dynamic_index_in_dim(array, me ^ k, dim, keepdims=False) for k in range(count)]


def sum_from_partners(parts, axis):
    return wide_sum(parts[0], *[swapped(parts[k], axis, k) for k in range(1, len(parts))]).astype(BF16)


def in_order(blocks, axis):
    me = lax.axis_index(axis)
    blocks = jnp.stack(blocks)
    return jnp.stack([lax.dynamic_index_in_dim(blocks, me ^ k, 0, keepdims=False) for k in range(blocks.shape[0])])


def all_of_expert(array):
    count = lax.axis_size("expert")
    return in_order([array] + [swapped(array, "expert", k) for k in range(1, count)], "expert")


def norm_rows(values, gain):
    factor = lax.rsqrt(jnp.mean(values * values, axis=-1, keepdims=True) + EPS)
    return (values * factor * gain).astype(BF16), factor


def norm_back(grad_norm, values, factor, gain):
    inner = grad_norm * gain
    return factor * inner - values * factor**3 * jnp.mean(inner * values, axis=-1, keepdims=True)


def angles(positions):
    half = HEAD_SIZE // 2
    freq = jnp.power(THETA, -jnp.arange(half).astype(F32) / half)
    turned = freq[None, :, None] * positions.astype(F32)[:, None, :]
    return jnp.concatenate([jnp.cos(turned), jnp.sin(turned)], axis=1)


def per_device(
    inputs,
    cotangent,
    routes,
    attn_gain,
    query_weight,
    key_matrix,
    value_matrix,
    output_matrix,
    ffn_gain,
    router_weight,
    gateup_weight,
    down_weight,
):
    _, span, width = inputs.shape
    n_ctx = lax.axis_size("ctx")
    n_owner = lax.axis_size("expert")
    own_rows = query_weight.shape[0]
    local_experts = gateup_weight.shape[0]
    cap = span // 4
    parts = n_ctx // KEY_VALUE_HEADS
    sub = span // parts
    part = lax.axis_index("ctx") % parts
    part_arg = part.astype(jnp.int32).reshape(1)

    tokens_in = inputs.reshape(span, width)
    me = lax.axis_index("expert")
    piece = own_rows // n_owner

    def a_part(array):
        return lax.dynamic_slice_in_dim(array, me * piece, piece, 0)

    heads = jnp.concatenate(
        [
            a_part(query_weight).reshape(piece, KEY_VALUE_HEADS, QROWS),
            a_part(key_matrix).reshape(piece, KEY_VALUE_HEADS, HEAD_SIZE),
            a_part(value_matrix).reshape(piece, KEY_VALUE_HEADS, HEAD_SIZE),
        ],
        axis=-1,
    ).transpose(1, 0, 2)
    small = jnp.concatenate([attn_gain[:, None], ffn_gain[:, None], router_weight], axis=1)
    small = a_part(jnp.pad(small, ((0, 0), (0, HEAD_SIZE - small.shape[1]))))
    sends = jnp.concatenate(
        [jnp.repeat(heads, parts, axis=0), jnp.broadcast_to(small[None], (n_ctx,) + small.shape)], axis=-1
    )
    weights = all_of_expert(lax.all_to_all(sends, "ctx", 0, 0, tiled=True))
    weights = weights.transpose(1, 0, 2, 3).reshape(width, -1)
    head_weight = weights[:, :SLICE].T
    gain_one = weights[:, SLICE].astype(F32)
    gain_two = weights[:, SLICE + 1].astype(F32)
    router = weights[:, SLICE + 2 : SLICE + 2 + EXPERTS]

    names = routes.reshape(span, TOPK)
    hits = jnp.any(names[:, :, None] == jnp.arange(EXPERTS), axis=1)
    upto = (jnp.arange(span)[:, None] <= jnp.arange(span)[None, :]).astype(BF16)
    counted = contract(hits.astype(BF16), upto, 0, 0)
    ranks = jnp.where(hits.T, counted - 1.0, -1.0).astype(BF16)

    def to_owners(array):
        array = lax.all_to_all(array.reshape(n_owner, local_experts, span), "expert", 0, 0, tiled=True)
        blocks = [lax.dynamic_index_in_dim(array, me ^ k, 0, keepdims=False) for k in range(n_owner)]
        return jnp.concatenate(blocks, axis=1)[:, None]

    every = jnp.arange(n_ctx * span, dtype=jnp.int32).reshape(n_ctx, span)
    table = angles(every)
    pieces = 2
    x_pieces = [
        lax.all_gather(piece, "ctx", axis=0, tiled=False)
        for piece in jnp.split(tokens_in, pieces, axis=0)
    ]
    grad_in = cotangent.reshape(span, width)
    held = gather_start(grad_in, "expert")
    rank = to_owners(ranks)
    x_pieces[0], held, head_weight, rank = lax.optimization_barrier((x_pieces[0], held, head_weight, rank))
    rank = rank.astype(jnp.int32)
    grad_blocks = gather_end(*held, "expert")
    buffers = project(x_pieces[0], gain_one[None], head_weight, table, 0, ())
    x_pieces[1], grad_blocks, buffers = lax.optimization_barrier((x_pieces[1], grad_blocks, buffers))
    normed_all, q_all, kv_all = project(x_pieces[1], gain_one[None], head_weight, table, 1, buffers)
    if parts == 1:
        queries, positions, q_table = q_all, every, table
    else:

        def mine(array):
            array = array.reshape(array.shape[:-1] + (parts, sub))
            return lax.dynamic_index_in_dim(array, part, array.ndim - 2, keepdims=False)

        queries, positions, q_table = mine(q_all), mine(every), mine(table)
    pos = positions.reshape(1, -1)

    output_matrix, w_heads, queries = lax.optimization_barrier((output_matrix, head_weight, queries))
    w_output = lax.all_gather(output_matrix, "ctx", axis=0, tiled=True)
    grad_rows = [dispatch(rank, block, k, cap, width // 2) for k, block in enumerate(grad_blocks)]
    tile = min(512, n_ctx * sub)
    attended, lse = attend(part_arg, pos, queries, kv_all, tile, tile, sub, span)

    def to_rows(array):
        array = lax.all_to_all(array, "ctx", 0, 0, tiled=True)
        array = array.reshape(KEY_VALUE_HEADS, parts, -1, sub).transpose(0, 2, 1, 3)
        return array.reshape(-1, span)

    attended_rows, grad_rows = lax.optimization_barrier((to_rows(attended), grad_rows))
    flat_in = tokens_in.astype(F32)
    hidden = flat_in + contract(attended_rows, w_output, 0, 0)
    normed_two, rms_two = norm_rows(hidden, gain_two)
    w_heads, normed_two = lax.optimization_barrier((w_heads, normed_two))
    w_heads = lax.all_gather(w_heads, "ctx", axis=0, tiled=False)[::parts].reshape(-1, width)
    logits = jnp.dot(normed_two, router, preferred_element_type=F32)
    masked = jnp.where(hits, logits, NEG)
    powers = jnp.where(hits, jnp.exp(masked - jnp.max(masked, axis=-1, keepdims=True)), 0.0)
    probs = powers / jnp.sum(powers, axis=-1, keepdims=True)
    prob = to_owners(probs.T)

    place = jnp.stack([me * local_experts, lax.axis_index("ctx") % 2]).astype(jnp.int32)
    token_rows, prob = gather_rows(
        normed_two, "expert", lambda block, k: dispatch(rank, block, k, cap, width // 2), prob
    )
    cuts, offset = [], 0
    for count in (1, 1, 3, 3, local_experts):
        if offset < local_experts:
            cuts.append((offset, min(count, local_experts - offset)))
            offset += count
    backs, outs, sums = [], [], []
    core_line = [[z * 2 + core for z in range(n_ctx // 2)] for core in range(2)]

    def pair_sum(mine, theirs):
        return wide_sum(mine, swapped(theirs, "ctx", 1)).astype(BF16)

    def line_sum(pair):
        total = lax.psum_scatter(
            pair.reshape(-1, 3 * FFE), "ctx", scatter_dimension=0, tiled=True, axis_index_groups=core_line
        )
        return total.reshape(-1, own_rows, 3 * FFE)

    for number, (offset, count) in enumerate(cuts):
        back, out, mine, theirs = run_experts(
            place, rank, prob, token_rows, grad_rows, gateup_weight, down_weight, offset, count, n_ctx, span, cap
        )
        backs.append(back)
        outs.append(out)
        if number < len(cuts) - 1:
            sums.append(line_sum(pair_sum(mine, theirs)))
            if number == 1:
                w_heads, place = lax.optimization_barrier((w_heads, place))
    ranks = [rank[offset : offset + count] for offset, count in cuts]

    def to_tokens(rows):
        return [combine(ranks, rows, k, span, cap, rows[0].shape[2]) for k in reversed(range(n_owner))][::-1]

    back_sum = return_end(return_start(to_tokens(backs), "expert"), "expert")

    grad = cotangent.reshape(span, width).astype(F32)
    route_grad = back_sum[:, width : width + EXPERTS] + back_sum[:, width + EXPERTS : width + 2 * EXPERTS]
    chosen_grad = probs * (route_grad - jnp.sum(probs * route_grad, axis=-1, keepdims=True))
    logit_grad = chosen_grad.astype(BF16)
    router_full = contract(normed_two, logit_grad, 0, 0)
    normed_two_grad = back_sum[:, :width] + contract(logit_grad, router, 1, 1)
    ffn_gain_full = jnp.sum(normed_two_grad * hidden * rms_two, axis=0)
    hidden_grad = grad + norm_back(normed_two_grad, hidden, rms_two, gain_two)
    hidden_low = hidden_grad.astype(BF16)
    attended_grad = contract(w_output, hidden_low, 1, 1).astype(BF16)
    attended_grad = attended_grad.reshape(KEY_VALUE_HEADS, QROWS, parts, sub).transpose(0, 2, 1, 3)
    attended_grad = lax.all_to_all(attended_grad.reshape(n_ctx, QROWS, sub), "ctx", 0, 0, tiled=True)
    outproj_full = jnp.dot(attended_rows, hidden_low, preferred_element_type=F32)
    column = jnp.arange(EXTRA)[None]
    side = jnp.where(
        column == EXPERTS, ffn_gain_full[:, None], jnp.pad(router_full, ((0, 0), (0, EXTRA - EXPERTS)))
    ).astype(BF16)
    mixed_full = jnp.concatenate([outproj_full.astype(BF16), lax.optimization_barrier(side)], axis=1)

    mixed_parts = for_partners(mixed_full.reshape(n_ctx, n_owner, -1, mixed_full.shape[1]), "expert", 1)
    theirs, hidden_low = lax.optimization_barrier((theirs, hidden_low))
    pair, outs, mixed_parts = lax.optimization_barrier((pair_sum(mine, theirs), outs, mixed_parts))
    mixed_part = sum_from_partners(mixed_parts, "expert")
    out_parts = return_start(to_tokens(outs), "expert")
    out_parts, attended_grad, mixed_part = lax.optimization_barrier((out_parts, attended_grad, mixed_part))
    mixed_part = lax.all_to_all(mixed_part, "ctx", 0, 0, tiled=True)
    backs = attend_back(
        part_arg, pos, queries, attended, attended_grad, lse, kv_all, q_table, table, tile, tile, sub, span
    )
    mixed_part, backs = lax.optimization_barrier((mixed_part, backs))
    output = hidden + return_end(out_parts, "expert")
    output = output.astype(BF16).reshape(1, span, width)
    if len(backs) == 1:
        rows_back = lax.all_to_all(backs[0], "ctx", 0, 0, tiled=True).reshape(-1, span)
        head_grad = head_grads(backs[0], normed_all)
    else:
        query_back, kv_back = backs
        query_rows = to_rows(query_back).reshape(KEY_VALUE_HEADS, QROWS, span)
        kv_rows = lax.all_to_all(kv_back, "ctx", 0, 0, tiled=True).astype(F32)
        kv_rows = jnp.sum(kv_rows.reshape(KEY_VALUE_HEADS, parts, 2 * HEAD_SIZE, span), axis=1).astype(BF16)
        rows_back = jnp.concatenate([query_rows, kv_rows], axis=1).reshape(-1, span)
        normed_part = normed_all.reshape(n_ctx, parts, sub, width)
        normed_part = lax.dynamic_index_in_dim(normed_part, part, 1, keepdims=False)
        head_grad = jnp.concatenate([head_grads(query_back, normed_part), head_grads(kv_back, normed_all)], axis=1)
    head_parts = for_partners(head_grad.reshape(n_ctx, n_owner, -1, SLICE), "expert", 1)
    head_part = sum_from_partners(head_parts, "expert")
    pair, rows_back, head_part = lax.optimization_barrier((pair, rows_back, head_part))
    head_part = lax.all_to_all(head_part, "ctx", 0, 0, tiled=True)
    sums.append(line_sum(pair))
    grads = ()
    for (offset, _), total in zip(cuts, sums):
        grads = unpack(total, offset, local_experts, grads)
    gateup_grad, down_grad = grads
    mixed_sum = jnp.sum(mixed_part.astype(F32), axis=0).astype(BF16)
    head_sum = jnp.sum(head_part.astype(F32).reshape(KEY_VALUE_HEADS, parts, -1, SLICE), axis=1).astype(BF16)
    head_sum = head_sum.transpose(1, 0, 2).reshape(-1, KEY_VALUE_HEADS * SLICE)
    last = all_of_expert(jnp.concatenate([mixed_sum, head_sum], axis=1)).reshape(own_rows, -1).astype(F32)
    mixed_sum = last[:, : -KEY_VALUE_HEADS * SLICE]
    head_grad = last[:, -KEY_VALUE_HEADS * SLICE :].reshape(own_rows, KEY_VALUE_HEADS, SLICE)
    normed_one_grad = contract(rows_back, w_heads, 0, 0)
    rms_one = lax.rsqrt(jnp.mean(flat_in * flat_in, axis=-1, keepdims=True) + EPS)
    input_grad = (
        (hidden_grad + norm_back(normed_one_grad, flat_in, rms_one, gain_one)).astype(BF16).reshape(1, span, width)
    )

    outproj_grad = mixed_sum[:, :width]
    router_grad = mixed_sum[:, width : width + EXPERTS]
    ffn_gain_grad = mixed_sum[:, width + EXPERTS]
    query_grad = head_grad[..., :QROWS].reshape(own_rows, -1)
    key_grad = head_grad[..., QROWS : QROWS + HEAD_SIZE].reshape(own_rows, -1)
    value_grad = head_grad[..., QROWS + HEAD_SIZE :].reshape(own_rows, -1)
    attn_gain_grad = (
        jnp.sum(query_weight.astype(F32) * query_grad, axis=1)
        + jnp.sum(key_matrix.astype(F32) * key_grad, axis=1)
        + jnp.sum(value_matrix.astype(F32) * value_grad, axis=1)
    ) / attn_gain.astype(F32)
    return (
        output,
        input_grad,
        attn_gain_grad,
        query_grad,
        key_grad,
        value_grad,
        outproj_grad,
        ffn_gain_grad,
        router_grad,
        gateup_grad,
        down_grad,
    )


def solution(mesh):
    tokens = P("expert", "ctx", None)
    row = P("ctx")
    rows = P("ctx", None)
    owned = P("expert", None, None)
    return jax.shard_map(
        per_device,
        mesh=mesh,
        in_specs=(tokens, tokens, tokens, row, rows, rows, rows, rows, row, rows, owned, owned),
        out_specs=(
            tokens,
            tokens,
            row,
            rows,
            rows,
            rows,
            rows,
            row,
            rows,
            P("expert", "ctx", None),
            P("expert", None, "ctx"),
        ),
        check_vma=False,
    )
```

time: 2750 us -> 986 us (0.36)
  waiting for transfers between devices: 1680 us -> 291 us
  Pallas kernels: 0 us -> 399 us
  blocking collectives: 256 us -> 0 us
  matrix products: 278 us -> 32.7 us
  local copies, waits for them, and re-layouts: 310 us -> 76.6 us
  other arithmetic: 170 us -> 85.4 us
  starting transfers between devices: 28.8 us -> 75.8 us
    reduce_scatter x5, waiting for transfers between devices: 731 us -> 0.01 us  [line_sum(): lax.psum_scatter(pair.reshape(-1, 3 * FFE), 'ctx', scatter_dimension=0, t...]
    pallas_call x0 -> x31, Pallas kernels: none -> 399 us  [the longest x5 115 us: run_experts(): pl.pallas_call(functools.partial(experts_kernel, span, cap, offset, block...]
    unnamed x15 -> x9, waiting for transfers between devices: 399 us -> 0.83 us
    all_to_all x4 -> x8, waiting for transfers between devices: 407 us -> 91.9 us  [the longest x2 27.8 us: to_owners(): lax.all_to_all(array.reshape(n_owner, local_experts, span), 'expert', 0,...]
    dot_general x28 -> x8, matrix products: 278 us -> 32.7 us  [the longest x6 27.6 us: contract(): lax.dot_general(left, right, (((a,), (b,)), ((), ())), preferred_element_...]
    all_gather x1 -> x0, blocking collectives: 205 us -> none  [per_device(): lax.all_gather(router_weight, 'ctx', axis=0, tiled=True)]
    ppermute x0 -> x37, waiting for transfers between devices: none -> 140 us  [swapped(): return lax.ppermute(array, axis, [(i, i ^ mask) for i in range(count)])]
    all_gather x5 -> x4, waiting for transfers between devices: 142 us -> 58.6 us  [the longest x2 58.6 us: per_device(): lax.all_gather(piece, 'ctx', axis=0, tiled=False)]
  transfers between devices with their start and end apart: 17 -> 54, of which waited for: 14 -> 29; matrix products, arithmetic and copies ran while one was open for 15% -> 18% of each run, Pallas kernels for 0% -> 40%
where the time goes in v1:
time: 986 us; the launch traced here: 976 us
  Pallas kernels  399 us (40%)
  waiting for transfers between devices  291 us (30%)
  other arithmetic  85.4 us (9%)
  local copies, waits for them, and re-layouts  76.6 us (8%)
  starting transfers between devices  75.8 us (8%)
  matrix products  32.7 us (3%)
  between operations  14.9 us (2%)
    ppermute x37, waiting for transfers between devices, swapped(): return lax.ppermute(array, axis, [(i, i ^ mask) for i in range(count)])  140 us
    pallas_call x5, Pallas kernels, run_experts(): pl.pallas_call(functools.partial(experts_kernel, span, cap, offset, block...  115 us
    pallas_call x1, Pallas kernels, attend_back(): pl.pallas_call(functools.partial(attend_back_kernel, bk, sub, span), grid...  84.1 us
    pallas_call x1, Pallas kernels, attend(): pl.pallas_call(functools.partial(attend_kernel, bk, sub, span), grid=(nq...  61 us
    all_gather x2, waiting for transfers between devices, per_device(): lax.all_gather(piece, 'ctx', axis=0, tiled=False)  58.6 us
    pallas_call x8, Pallas kernels, combine(): pl.pallas_call(functools.partial(combine_kernel, cap, len(ranks)), grid=(...  53.3 us
    ppermute x37, starting transfers between devices, swapped(): return lax.ppermute(array, axis, [(i, i ^ mask) for i in range(count)])  40.6 us
    pallas_call x8, Pallas kernels, dispatch(): pl.pallas_call(functools.partial(dispatch_kernel, cap), grid=(width // wi...  39.3 us
  transfers between devices with their start and end apart: 54, of which 29 were waited for; matrix products, arithmetic and copies ran while one was open for 18% of the time, Pallas kernels for 40%

profile of v1, /device:TPU:0, one launch (start us, length us, event | category | flops | bytes accessed | tf_op | source)
XLA Modules:
  0.0 975.9 jit_solution(4823886647462637232)
XLA Ops:
  25.2 16.7 %all-to-all-done = bf16[8,48,384]{2,1,0:T(8,128)(2,1)S(1)} async-done(((bf16[8,48,384]{2,1,0:T(8,128)(2,1)}), bf16[8,48,384]{2,1,0:T(8,128)(2,1)S(1)}, u32[]{:S(2)}, u32[]{:S(2)}) %all-to-all-start) | async-done | bytes 294944 | tf_op jit(solution)/shard_map/all_to_all | solution.py:661
  56.0 7.0 collective-permute-done.3
  65.1 18.9 %all-gather.6.cloned.1.call-done.x_ref = bf16[8,256,1536]{2,1,0:T(8,128)(2,1)} async-done(((bf16[1,256,1536]{2,1,0:T(8,128)(2,1)}), bf16[8,256,1536]{2,1,0:T(8,128)(2,1)}) %all-gather.6.cloned.1.call-update) | async-done | bytes 6291472 | tf_op jit(solution)/shard_map/all_gather | solution.py:683
  93.5 9.3 project.2
  109.8 39.7 %all-gather.8.cloned.1.call-done.x_ref = bf16[8,256,1536]{2,1,0:T(8,128)(2,1)} async-done(((bf16[1,256,1536]{2,1,0:T(8,128)(2,1)}), bf16[8,256,1536]{2,1,0:T(8,128)(2,1)}) %all-gather.8.cloned.1.call-update) | async-done | bytes 6291472 | tf_op jit(solution)/shard_map/all_gather | solution.py:683
  149.5 9.1 project.3
  159.3 61.0 %attend.1 = (bf16[8,192,512]{2,1,0:T(8,128)(2,1)}, f32[3,1,4096]{2,1,0:T(1,128)}) custom-call(s32[1]{0:T(128)} %constant.112.clone.1.part_ref, s32[1,4096]{1,0:T(1,128)} %iota.44.pos_ref, bf16[8,192,512]{2,1,0:T(8,128)(2,1)} %get-tuple-element.117.q_ref, bf16[8,128,512]{2,1,0:T(8,128)(2,1)} %get-tuple-element.118.kv_ref), custom_call_target="tpu_custom_call" | custom-call | flops 1024 | bytes 1024 | tf_op jit(solution)/shard_map/attend/pallas_call | solution.py:199
  225.8 4.9 dispatch.8.refs_4_
  240.5 5.0 dispatch.11.refs_7_
  245.5 16.9 %all-to-all-done.2 = bf16[8,192,512]{2,1,0:T(8,128)(2,1)} async-done(((bf16[8,192,512]{2,1,0:T(8,128)(2,1)}), bf16[8,192,512]{2,1,0:T(8,128)(2,1)}, u32[]{:S(2)}, u32[]{:S(2)}) %all-to-all-start.2) | async-done | bytes 1572896 | tf_op jit(solution)/shard_map/all_to_all | solution.py:713
  262.4 5.3 multiply_reduce_fusion.2
  278.3 4.9 dispatch.12.refs_0_
  283.2 25.1 %all-to-all-done.3 = f32[4,10,512]{2,1,0:T(8,128)S(1)} async-done(((f32[4,10,512]{2,1,0:T(8,128)}), f32[4,10,512]{2,1,0:T(8,128)S(1)}, u32[]{:S(2)}, u32[]{:S(2)}) %all-to-all-start.3) | async-done | bytes 81952 | tf_op jit(solution)/shard_map/all_to_all | solution.py:675
  313.6 14.4 %collective-permute-done.10 = bf16[256,1536]{1,0:T(8,128)(2,1)S(1)} collective-permute-done((bf16[256,1536]{1,0:T(8,128)(2,1)S(1)}, bf16[256,1536]{1,0:T(8,128)(2,1)S(1)}, u32[]{:S(2)}, u32[]{:S(2)}) %collective-permute-start.10) | collective-permute-done | bytes 786464 | tf_op jit(solution)/shard_map/ppermute | solution.py:516
  337.2 4.9 dispatch.13.refs_1_
  342.1 5.0 dispatch.15.refs_3_
  347.1 13.9 %experts.6 = (bf16[1,512,1664]{2,1,0:T(8,128)(2,1)}, bf16[1,512,1536]{2,1,0:T(8,128)(2,1)}, bf16[4,1,192,1536]{3,2,1,0:T(8,128)(2,1)}, bf16[4,1,192,1536]{3,2,1,0:T(8,128)(2,1)}) custom-call(s32[2]{0:T(128)} %pad_add_fusion.place_ref, s32[10,1,2048]{2,1,0:T(1,128)} %copy_convert_fusion.rank_ref, f32[10,1,2048]{2,1,0:T(1,128)} %broadcast_in_dim.74.prob_ref, ...), custom_call_target="tpu_custom_call" | custom-call | flops 1024 | bytes 1024 | tf_op jit(solution)/shard_map/experts/pallas_call | solution.py:438
  369.6 31.9 %experts.8 = (bf16[3,512,1664]{2,1,0:T(8,128)(2,1)}, bf16[3,512,1536]{2,1,0:T(8,128)(2,1)}, bf16[4,3,192,1536]{3,2,1,0:T(8,128)(2,1)}, bf16[4,3,192,1536]{3,2,1,0:T(8,128)(2,1)}) custom-call(s32[2]{0:T(128)} %pad_add_fusion.place_ref, s32[10,1,2048]{2,1,0:T(1,128)} %copy_convert_fusion.rank_ref, f32[10,1,2048]{2,1,0:T(1,128)} %broadcast_in_dim.74.prob_ref, ...), custom_call_target="tpu_custom_call" | custom-call | flops 1024 | bytes 1024 | tf_op jit(solution)/shard_map/experts/pallas_call | solution.py:438
  401.7 13.8 %experts.7 = (bf16[1,512,1664]{2,1,0:T(8,128)(2,1)}, bf16[1,512,1536]{2,1,0:T(8,128)(2,1)}, bf16[4,1,192,1536]{3,2,1,0:T(8,128)(2,1)}, bf16[4,1,192,1536]{3,2,1,0:T(8,128)(2,1)}) custom-call(s32[2]{0:T(128)} %pad_add_fusion.place_ref, s32[10,1,2048]{2,1,0:T(1,128)} %copy_convert_fusion.rank_ref, f32[10,1,2048]{2,1,0:T(1,128)} %broadcast_in_dim.74.prob_ref, ...), custom_call_target="tpu_custom_call" | custom-call | flops 1024 | bytes 1024 | tf_op jit(solution)/shard_map/experts/pallas_call | solution.py:438
  424.0 10.1 %add_convert_fusion = bf16[4,3,192,1536]{3,2,1,0:T(8,128)(2,1)} fusion(bf16[4,3,192,1536]{3,2,1,0:T(8,128)(2,1)} %collective-permute-done.34, bf16[4,3,192,1536]{3,2,1,0:T(8,128)(2,1)} %get-tuple-element.181), kind=kLoop, calls=%fused_computation | loop fusion | flops 14155776 | bytes 21233664 | tf_op jit(solution)/shard_map/convert_element_type | solution.py:742
  434.1 31.6 %experts.9 = (bf16[3,512,1664]{2,1,0:T(8,128)(2,1)}, bf16[3,512,1536]{2,1,0:T(8,128)(2,1)}, bf16[4,3,192,1536]{3,2,1,0:T(8,128)(2,1)}, bf16[4,3,192,1536]{3,2,1,0:T(8,128)(2,1)}) custom-call(s32[2]{0:T(128)} %pad_add_fusion.place_ref, s32[10,1,2048]{2,1,0:T(1,128)} %copy_convert_fusion.rank_ref, f32[10,1,2048]{2,1,0:T(1,128)} %broadcast_in_dim.74.prob_ref, ...), custom_call_target="tpu_custom_call" | custom-call | flops 1024 | bytes 1024 | tf_op jit(solution)/shard_map/experts/pallas_call | solution.py:438
  468.0 23.3 %experts.5 = (bf16[2,512,1664]{2,1,0:T(8,128)(2,1)}, bf16[2,512,1536]{2,1,0:T(8,128)(2,1)}, bf16[4,2,192,1536]{3,2,1,0:T(8,128)(2,1)}, bf16[4,2,192,1536]{3,2,1,0:T(8,128)(2,1)}) custom-call(s32[2]{0:T(128)} %pad_add_fusion.place_ref, s32[10,1,2048]{2,1,0:T(1,128)} %copy_convert_fusion.rank_ref, f32[10,1,2048]{2,1,0:T(1,128)} %broadcast_in_dim.74.prob_ref, ...), custom_call_target="tpu_custom_call" | custom-call | flops 1024 | bytes 1024 | tf_op jit(solution)/shard_map/experts/pallas_call | solution.py:438
  491.3 7.0 combine.11
  503.5 6.8 combine.10
  510.3 7.1 combine.9
  530.1 7.0 combine.8
  542.8 16.7 %collective-permute-done.13 = bf16[256,1664]{1,0:T(8,128)(2,1)S(1)} collective-permute-done((bf16[256,1664]{1,0:T(8,128)(2,1)}, bf16[256,1664]{1,0:T(8,128)(2,1)S(1)}, u32[]{:S(2)}, u32[]{:S(2)}) %collective-permute-start.13) | collective-permute-done | bytes 852000 | tf_op jit(solution)/shard_map/ppermute | solution.py:516
  569.1 10.1 %add_convert_fusion.1 = bf16[4,3,192,1536]{3,2,1,0:T(8,128)(2,1)} fusion(bf16[4,3,192,1536]{3,2,1,0:T(8,128)(2,1)} %collective-permute-done.33, bf16[4,3,192,1536]{3,2,1,0:T(8,128)(2,1)} %get-tuple-element.179), kind=kLoop, calls=%fused_computation.1 | loop fusion | flops 14155776 | bytes 21233664 | tf_op jit(solution)/shard_map/convert_element_type | solution.py:742
  588.4 7.6 copy.134
  596.0 6.7 convolution_convert_fusion.1
  607.3 5.0 dynamic-slice_bitcast_fusion
  612.4 5.8 add_convert_fusion.2
  621.7 6.4 combine.15
  628.1 6.3 combine.14
  634.4 6.3 combine.13
  650.8 27.7 %collective-permute-done.23 = bf16[8,48,1664]{2,1,0:T(8,128)(2,1)} collective-permute-done((bf16[8,48,1664]{2,1,0:T(8,128)(2,1)}, bf16[8,48,1664]{2,1,0:T(8,128)(2,1)}, u32[]{:S(2)}, u32[]{:S(2)}) %collective-permute-start.23) | collective-permute-done | bytes 1277984 | tf_op jit(solution)/shard_map/ppermute | solution.py:516
  678.8 6.4 combine.12
  695.3 16.1 %collective-permute-done.21 = bf16[256,1536]{1,0:T(8,128)(2,1)} collective-permute-done((bf16[256,1536]{1,0:T(8,128)(2,1)}, bf16[256,1536]{1,0:T(8,128)(2,1)}, u32[]{:S(2)}, u32[]{:S(2)}) %collective-permute-start.21) | collective-permute-done | bytes 786464 | tf_op jit(solution)/shard_map/ppermute | solution.py:516
  711.5 5.2 all-to-all-start.5
  717.3 84.1 %attend_back.1.back_ref = bf16[8,320,512]{2,1,0:T(8,128)(2,1)} custom-call(s32[1]{0:T(128)} %constant.112.clone.1.part_ref, s32[1,4096]{1,0:T(1,128)} %iota.49.pos_ref, bf16[8,192,512]{2,1,0:T(8,128)(2,1)} %get-tuple-element.117.q_ref, bf16[8,192,512]{2,1,0:T(8,128)(2,1)} %get-tuple-element.119.o_ref, bf16[8,192,512]{2,1,0:T(8,128)(2,1)} %all-to-all-done.4.do_ref, ...), custom_call_target="tpu_custom_call" | custom-call | flops 1024 | bytes 1024 | tf_op jit(solution)/shard_map/attend_back/pallas_call | solution.py:320
  801.3 5.2 all-to-all-start.6
  809.3 13.5 %head_grads.1 = bf16[1536,320]{1,0:T(8,128)(2,1)} custom-call(bf16[8,320,512]{2,1,0:T(8,128)(2,1)} %attend_back.1.back_ref, bf16[8,512,1536]{2,1,0:T(8,128)(2,1)} %get-tuple-element.173.n_ref), custom_call_target="tpu_custom_call" | custom-call | flops 1024 | bytes 1024 | tf_op jit(solution)/shard_map/head_grads/pallas_call | solution.py:110
  835.9 6.2 collective-permute-done.28
  843.9 23.0 %all-to-all-done.6 = bf16[8,320,512]{2,1,0:T(8,128)(2,1)} async-done(((bf16[8,320,512]{2,1,0:T(8,128)(2,1)}), bf16[8,320,512]{2,1,0:T(8,128)(2,1)}, u32[]{:S(2)}, u32[]{:S(2)}) %all-to-all-start.6) | async-done | bytes 2621472 | tf_op jit(solution)/shard_map/all_to_all | solution.py:800
  884.6 11.0 %fusion.2 = (f32[512]{0:T(512)S(1)}, f32[512]{0:T(512)S(1)}, f32[512,1536]{1,0:T(8,128)}) fusion(bf16[1,512,1536]{2,1,0:T(8,128)(2,1)} %param.12, f32[1536]{0:T(1024)S(1)} %copy-done.30, bf16[2560,512]{1,0:T(8,128)(2,1)} %bitcast.33, bf16[2560,1536]{1,0:T(8,128)(2,1)} %all-gather.12.cloned.1.call-done), kind=kOutput, calls=%fused_computation.18 | convolution fusion | flops 4031249408 | bytes 15214592 | tf_op jit(solution)/shard_map/dot_general | solution.py:32
  895.6 7.5 all-to-all-done.7
  918.3 9.0 collective-permute-done.31
  963.6 5.5 copy.144
  (313 shorter events, 269.1 us)
Async XLA Ops:
  7.2 76.7 %all-gather.6.cloned.1.call-start = ((), (), s32[]{:S(2)}) async-start(), calls=%async_computation.13 | async-start | bytes 7077888 | tf_op jit(solution)/shard_map/all_gather | solution.py:683
  10.0 139.5 %all-gather.8.cloned.1.call-start = ((), (), s32[]{:S(2)}) async-start(), calls=%async_computation.14 | async-start | bytes 7077888 | tf_op jit(solution)/shard_map/all_gather | solution.py:683
  10.8 54.3 %collective-permute-start = (bf16[512,1536]{1,0:T(8,128)(2,1)S(1)}, bf16[512,1536]{1,0:T(8,128)(2,1)}, u32[]{:S(2)}, u32[]{:S(2)}) collective-permute-start(bf16[512,1536]{1,0:T(8,128)(2,1)S(1)} %bitcast.132), channel_id=1, source_target_pairs={{0,1},{1,0},{2,3},{3,2},{4,5},{5,4},{6,7},{7,6},{8,9},{9,8},{10,11... | collective-permute-start | bytes 4718600 | tf_op jit(solution)/shard_map/ppermute | solution.py:516
  13.8 51.3 %collective-permute-start.1 = (bf16[512,1536]{1,0:T(8,128)(2,1)S(1)}, bf16[512,1536]{1,0:T(8,128)(2,1)}, u32[]{:S(2)}, u32[]{:S(2)}) collective-permute-start(bf16[512,1536]{1,0:T(8,128)(2,1)S(1)} %bitcast.133), channel_id=1, source_target_pairs={{0,2},{1,3},{2,0},{3,1},{4,6},{5,7},{6,4},{7,5},{8,10},{9,11},{10,... | collective-permute-start | bytes 4718600 | tf_op jit(solution)/shard_map/ppermute | solution.py:516
  18.7 23.1 %all-to-all-start = ((bf16[8,48,384]{2,1,0:T(8,128)(2,1)}), bf16[8,48,384]{2,1,0:T(8,128)(2,1)S(1)}, u32[]{:S(2)}, u32[]{:S(2)}) async-start(bf16[8,48,384]{2,1,0:T(8,128)(2,1)} %copy.127), calls=%async_computation | async-start | bytes 589824 | tf_op jit(solution)/shard_map/all_to_all | solution.py:661
  45.2 217.2 %all-gather.10.cloned.1.call-start = ((), (), s32[]{:S(2)}) async-start(), calls=%async_computation.15 | async-start | bytes 5308416 | tf_op jit(solution)/shard_map/all_gather | solution.py:707
  47.2 15.8 %collective-permute-start.3 = (bf16[8,48,384]{2,1,0:T(8,128)(2,1)S(1)}, bf16[8,48,384]{2,1,0:T(8,128)(2,1)S(1)}, u32[]{:S(2)}, u32[]{:S(2)}) collective-permute-start(bf16[8,48,384]{2,1,0:T(8,128)(2,1)S(1)} %all-to-all-done), channel_id=1, source_target_pairs={{0,2},{1,3},{2,0},{3,1},{4,6},{5,7},{6,4},{7,5},{8,10},{9,11},{10,... | collective-permute-start | bytes 884744 | tf_op jit(solution)/shard_map/ppermute | solution.py:516
  48.6 14.3 %collective-permute-start.4 = (bf16[8,48,384]{2,1,0:T(8,128)(2,1)S(1)}, bf16[8,48,384]{2,1,0:T(8,128)(2,1)S(1)}, u32[]{:S(2)}, u32[]{:S(2)}) collective-permute-start(bf16[8,48,384]{2,1,0:T(8,128)(2,1)S(1)} %all-to-all-done), channel_id=1, source_target_pairs={{0,3},{1,2},{2,1},{3,0},{4,7},{5,6},{6,5},{7,4},{8,11},{9,10},{10,... | collective-permute-start | bytes 884744 | tf_op jit(solution)/shard_map/ppermute | solution.py:516
  85.1 19.8 %collective-permute-start.5 = (bf16[256,1536]{1,0:T(8,128)(2,1)S(1)}, bf16[256,1536]{1,0:T(8,128)(2,1)S(1)}, u32[]{:S(2)}, u32[]{:S(2)}) collective-permute-start(bf16[256,1536]{1,0:T(8,128)(2,1)S(1)} %slice.124), channel_id=1, source_target_pairs={{0,1},{1,0},{2,3},{3,2},{4,5},{5,4},{6,7},{7,6},{8,9},{9,8},{10,11... | collective-permute-start | bytes 2359304 | tf_op jit(solution)/shard_map/ppermute | solution.py:516
  87.9 19.6 %collective-permute-start.6 = (bf16[256,1536]{1,0:T(8,128)(2,1)S(1)}, bf16[256,1536]{1,0:T(8,128)(2,1)}, u32[]{:S(2)}, u32[]{:S(2)}) collective-permute-start(bf16[256,1536]{1,0:T(8,128)(2,1)S(1)} %slice.125), channel_id=1, source_target_pairs={{0,2},{1,3},{2,0},{3,1},{4,6},{5,7},{6,4},{7,5},{8,10},{9,11},{10,... | collective-permute-start | bytes 2359304 | tf_op jit(solution)/shard_map/ppermute | solution.py:516
  220.3 42.1 %all-to-all-start.2 = ((bf16[8,192,512]{2,1,0:T(8,128)(2,1)}), bf16[8,192,512]{2,1,0:T(8,128)(2,1)}, u32[]{:S(2)}, u32[]{:S(2)}) async-start(bf16[8,192,512]{2,1,0:T(8,128)(2,1)} %get-tuple-element.119.o_ref), calls=%async_computation.2 | async-start | bytes 3145728 | tf_op jit(solution)/shard_map/all_to_all | solution.py:713
  224.6 145.0 %all-gather.12.cloned.1.call-start = ((), (), s32[]{:S(2)}) async-start(), calls=%async_computation.21 | async-start | bytes 8847360 | tf_op jit(solution)/shard_map/all_gather | solution.py:722
  269.7 39.3 %collective-permute-start.7 = (bf16[512,1536]{1,0:T(8,128)(2,1)S(1)}, bf16[512,1536]{1,0:T(8,128)(2,1)}, u32[]{:S(2)}, u32[]{:S(2)}) collective-permute-start(bf16[512,1536]{1,0:T(8,128)(2,1)S(1)} %multiply_convert_fusion.token_ref), channel_id=1, source_target_pairs={{0,1},{1,0},{2,3},{3,2},{4,5},{5,4},{6,7},{7,6},{8,9},{9,8},{10,11... | collective-permute-start | bytes 4718600 | tf_op jit(solution)/shard_map/ppermute | solution.py:516
  271.3 37.8 %collective-permute-start.8 = (bf16[512,1536]{1,0:T(8,128)(2,1)S(1)}, bf16[512,1536]{1,0:T(8,128)(2,1)}, u32[]{:S(2)}, u32[]{:S(2)}) collective-permute-start(bf16[512,1536]{1,0:T(8,128)(2,1)S(1)} %multiply_convert_fusion.token_ref), channel_id=1, source_target_pairs={{0,2},{1,3},{2,0},{3,1},{4,6},{5,7},{6,4},{7,5},{8,10},{9,11},{10,... | collective-permute-start | bytes 4718600 | tf_op jit(solution)/shard_map/ppermute | solution.py:516
  274.9 33.4 %all-to-all-start.3 = ((f32[4,10,512]{2,1,0:T(8,128)}), f32[4,10,512]{2,1,0:T(8,128)S(1)}, u32[]{:S(2)}, u32[]{:S(2)}) async-start(f32[4,10,512]{2,1,0:T(8,128)} %reshape.229), calls=%async_computation.3 | async-start | bytes 262144 | tf_op jit(solution)/shard_map/all_to_all | solution.py:675
  278.3 591.3 %reduce-scatter.14.cloned.1.call-start = ((), (), s32[]{:S(2)}) async-start(), calls=%async_computation.20 | async-start | bytes 2949120 | tf_op jit(solution)/shard_map/reduce_scatter | solution.py:745
  310.3 17.7 %collective-permute-start.10 = (bf16[256,1536]{1,0:T(8,128)(2,1)S(1)}, bf16[256,1536]{1,0:T(8,128)(2,1)S(1)}, u32[]{:S(2)}, u32[]{:S(2)}) collective-permute-start(bf16[256,1536]{1,0:T(8,128)(2,1)S(1)} %slice.135), channel_id=1, source_target_pairs={{0,2},{1,3},{2,0},{3,1},{4,6},{5,7},{6,4},{7,5},{8,10},{9,11},{10,... | collective-permute-start | bytes 2359304 | tf_op jit(solution)/shard_map/ppermute | solution.py:516
  313.0 17.4 %collective-permute-start.9 = (bf16[256,1536]{1,0:T(8,128)(2,1)S(1)}, bf16[256,1536]{1,0:T(8,128)(2,1)S(1)}, u32[]{:S(2)}, u32[]{:S(2)}) collective-permute-start(bf16[256,1536]{1,0:T(8,128)(2,1)S(1)} %slice.134), channel_id=1, source_target_pairs={{0,1},{1,0},{2,3},{3,2},{4,5},{5,4},{6,7},{7,6},{8,9},{9,8},{10,11... | collective-permute-start | bytes 2359304 | tf_op jit(solution)/shard_map/ppermute | solution.py:516
  369.5 502.5 %reduce-scatter.12.cloned.1.call-start = ((), (), s32[]{:S(2)}) async-start(), calls=%async_computation.19 | async-start | bytes 2949120 | tf_op jit(solution)/shard_map/reduce_scatter | solution.py:745
  401.5 22.5 %collective-permute-start.34 = (bf16[4,3,192,1536]{3,2,1,0:T(8,128)(2,1)}, bf16[4,3,192,1536]{3,2,1,0:T(8,128)(2,1)}, u32[]{:S(2)}, u32[]{:S(2)}) collective-permute-start(bf16[4,3,192,1536]{3,2,1,0:T(8,128)(2,1)} %get-tuple-element.182), channel_id=1, source_target_pairs={{0,4},{4,0},{8,12},{12,8},{16,20},{20,16},{24,28},{28,24},{1,5},{5... | collective-permute-start | bytes 21233672 | tf_op jit(solution)/shard_map/ppermute | solution.py:516
  423.9 529.1 %reduce-scatter.10.cloned.1.call-start = ((), (), s32[]{:S(2)}) async-start(), calls=%async_computation.18 | async-start | bytes 8847360 | tf_op jit(solution)/shard_map/reduce_scatter | solution.py:745
  434.1 522.8 %reduce-scatter.8.cloned.1.call-start = ((), (), s32[]{:S(2)}) async-start(), calls=%async_computation.17 | async-start | bytes 8847360 | tf_op jit(solution)/shard_map/reduce_scatter | solution.py:745
  465.8 103.3 %collective-permute-start.33 = (bf16[4,3,192,1536]{3,2,1,0:T(8,128)(2,1)}, bf16[4,3,192,1536]{3,2,1,0:T(8,128)(2,1)}, u32[]{:S(2)}, u32[]{:S(2)}) collective-permute-start(bf16[4,3,192,1536]{3,2,1,0:T(8,128)(2,1)} %get-tuple-element.180), channel_id=1, source_target_pairs={{0,4},{4,0},{8,12},{12,8},{16,20},{20,16},{24,28},{28,24},{1,5},{5... | collective-permute-start | bytes 21233672 | tf_op jit(solution)/shard_map/ppermute | solution.py:516
  501.0 21.5 %collective-permute-start.12 = (bf16[256,1664]{1,0:T(8,128)(2,1)}, bf16[256,1664]{1,0:T(8,128)(2,1)}, u32[]{:S(2)}, u32[]{:S(2)}) collective-permute-start(bf16[256,1664]{1,0:T(8,128)(2,1)} %get-tuple-element.271), channel_id=1, source_target_pairs={{0,1},{1,0},{2,3},{3,2},{4,5},{5,4},{6,7},{7,6},{8,9},{9,8},{10,11... | collective-permute-start | bytes 2555912 | tf_op jit(solution)/shard_map/ppermute | solution.py:516
  502.0 23.9 %collective-permute-start.14 = (bf16[256,1664]{1,0:T(8,128)(2,1)}, bf16[256,1664]{1,0:T(8,128)(2,1)}, u32[]{:S(2)}, u32[]{:S(2)}) collective-permute-start(bf16[256,1664]{1,0:T(8,128)(2,1)} %get-tuple-element.270), channel_id=1, source_target_pairs={{0,2},{1,3},{2,0},{3,1},{4,6},{5,7},{6,4},{7,5},{8,10},{9,11},{10,... | collective-permute-start | bytes 2555912 | tf_op jit(solution)/shard_map/ppermute | solution.py:516
  519.5 22.1 %collective-permute-start.11 = (bf16[256,1664]{1,0:T(8,128)(2,1)}, bf16[256,1664]{1,0:T(8,128)(2,1)S(1)}, u32[]{:S(2)}, u32[]{:S(2)}) collective-permute-start(bf16[256,1664]{1,0:T(8,128)(2,1)} %slice.172), channel_id=1, source_target_pairs={{0,1},{1,0},{2,3},{3,2},{4,5},{5,4},{6,7},{7,6},{8,9},{9,8},{10,11... | collective-permute-start | bytes 2555912 | tf_op jit(solution)/shard_map/ppermute | solution.py:516
  520.7 22.1 %collective-permute-start.16 = (bf16[256,1664]{1,0:T(8,128)(2,1)}, bf16[256,1664]{1,0:T(8,128)(2,1)S(1)}, u32[]{:S(2)}, u32[]{:S(2)}) collective-permute-start(bf16[256,1664]{1,0:T(8,128)(2,1)} %slice.178), channel_id=1, source_target_pairs={{0,2},{1,3},{2,0},{3,1},{4,6},{5,7},{6,4},{7,5},{8,10},{9,11},{10,... | collective-permute-start | bytes 2555912 | tf_op jit(solution)/shard_map/ppermute | solution.py:516
  524.8 34.8 %collective-permute-start.13 = (bf16[256,1664]{1,0:T(8,128)(2,1)}, bf16[256,1664]{1,0:T(8,128)(2,1)S(1)}, u32[]{:S(2)}, u32[]{:S(2)}) collective-permute-start(bf16[256,1664]{1,0:T(8,128)(2,1)} %add_convert_fusion.7), channel_id=1, source_target_pairs={{0,2},{1,3},{2,0},{3,1},{4,6},{5,7},{6,4},{7,5},{8,10},{9,11},{10,... | collective-permute-start | bytes 2555912 | tf_op jit(solution)/shard_map/ppermute | solution.py:516
  528.1 31.4 %collective-permute-start.15 = (bf16[256,1664]{1,0:T(8,128)(2,1)}, bf16[256,1664]{1,0:T(8,128)(2,1)S(1)}, u32[]{:S(2)}, u32[]{:S(2)}) collective-permute-start(bf16[256,1664]{1,0:T(8,128)(2,1)} %add_convert_fusion.6), channel_id=1, source_target_pairs={{0,1},{1,0},{2,3},{3,2},{4,5},{5,4},{6,7},{7,6},{8,9},{9,8},{10,11... | collective-permute-start | bytes 2555912 | tf_op jit(solution)/shard_map/ppermute | solution.py:516
  569.1 43.3 %collective-permute-start.17 = (bf16[4,2,192,1536]{3,2,1,0:T(8,128)(2,1)}, bf16[4,2,192,1536]{3,2,1,0:T(8,128)(2,1)}, u32[]{:S(2)}, u32[]{:S(2)}) collective-permute-start(bf16[4,2,192,1536]{3,2,1,0:T(8,128)(2,1)} %get-tuple-element.146), channel_id=1, source_target_pairs={{0,4},{4,0},{8,12},{12,8},{16,20},{20,16},{24,28},{28,24},{1,5},{5... | collective-permute-start | bytes 14155784 | tf_op jit(solution)/shard_map/ppermute | solution.py:516
  602.7 86.7 %all-to-all-start.4 = ((bf16[8,192,512]{2,1,0:T(8,128)(2,1)}), bf16[8,192,512]{2,1,0:T(8,128)(2,1)}, u32[]{:S(2)}, u32[]{:S(2)}) async-start(bf16[8,192,512]{2,1,0:T(8,128)(2,1)} %bitcast.142), calls=%async_computation.4 | async-start | bytes 3145728 | tf_op jit(solution)/shard_map/all_to_all | solution.py:778
  618.2 31.2 %collective-permute-start.22 = (bf16[8,48,1664]{2,1,0:T(8,128)(2,1)}, bf16[8,48,1664]{2,1,0:T(8,128)(2,1)}, u32[]{:S(2)}, u32[]{:S(2)}) collective-permute-start(bf16[8,48,1664]{2,1,0:T(8,128)(2,1)} %get-tuple-element.158), channel_id=1, source_target_pairs={{0,1},{1,0},{2,3},{3,2},{4,5},{5,4},{6,7},{7,6},{8,9},{9,8},{10,11... | collective-permute-start | bytes 3833864 | tf_op jit(solution)/shard_map/ppermute | solution.py:516
  619.9 58.6 %collective-permute-start.23 = (bf16[8,48,1664]{2,1,0:T(8,128)(2,1)}, bf16[8,48,1664]{2,1,0:T(8,128)(2,1)}, u32[]{:S(2)}, u32[]{:S(2)}) collective-permute-start(bf16[8,48,1664]{2,1,0:T(8,128)(2,1)} %get-tuple-element.159), channel_id=1, source_target_pairs={{0,2},{1,3},{2,0},{3,1},{4,6},{5,7},{6,4},{7,5},{8,10},{9,11},{10,... | collective-permute-start | bytes 3833864 | tf_op jit(solution)/shard_map/ppermute | solution.py:516
  620.7 64.6 %collective-permute-start.24 = (bf16[8,48,1664]{2,1,0:T(8,128)(2,1)}, bf16[8,48,1664]{2,1,0:T(8,128)(2,1)}, u32[]{:S(2)}, u32[]{:S(2)}) collective-permute-start(bf16[8,48,1664]{2,1,0:T(8,128)(2,1)} %get-tuple-element.160), channel_id=1, source_target_pairs={{0,3},{1,2},{2,1},{3,0},{4,7},{5,6},{6,5},{7,4},{8,11},{9,10},{10,... | collective-permute-start | bytes 3833864 | tf_op jit(solution)/shard_map/ppermute | solution.py:516
  643.5 50.2 %collective-permute-start.18 = (bf16[256,1536]{1,0:T(8,128)(2,1)}, bf16[256,1536]{1,0:T(8,128)(2,1)}, u32[]{:S(2)}, u32[]{:S(2)}) collective-permute-start(bf16[256,1536]{1,0:T(8,128)(2,1)} %get-tuple-element.279), channel_id=1, source_target_pairs={{0,1},{1,0},{2,3},{3,2},{4,5},{5,4},{6,7},{7,6},{8,9},{9,8},{10,11... | collective-permute-start | bytes 2359304 | tf_op jit(solution)/shard_map/ppermute | solution.py:516
  645.2 50.1 %collective-permute-start.19 = (bf16[256,1536]{1,0:T(8,128)(2,1)}, bf16[256,1536]{1,0:T(8,128)(2,1)}, u32[]{:S(2)}, u32[]{:S(2)}) collective-permute-start(bf16[256,1536]{1,0:T(8,128)(2,1)} %get-tuple-element.278), channel_id=1, source_target_pairs={{0,2},{1,3},{2,0},{3,1},{4,6},{5,7},{6,4},{7,5},{8,10},{9,11},{10,... | collective-permute-start | bytes 2359304 | tf_op jit(solution)/shard_map/ppermute | solution.py:516
  649.4 62.1 %collective-permute-start.21 = (bf16[256,1536]{1,0:T(8,128)(2,1)}, bf16[256,1536]{1,0:T(8,128)(2,1)}, u32[]{:S(2)}, u32[]{:S(2)}) collective-permute-start(bf16[256,1536]{1,0:T(8,128)(2,1)} %slice.186), channel_id=1, source_target_pairs={{0,2},{1,3},{2,0},{3,1},{4,6},{5,7},{6,4},{7,5},{8,10},{9,11},{10,... | collective-permute-start | bytes 2359304 | tf_op jit(solution)/shard_map/ppermute | solution.py:516
  678.5 33.0 %collective-permute-start.20 = (bf16[256,1536]{1,0:T(8,128)(2,1)}, bf16[256,1536]{1,0:T(8,128)(2,1)}, u32[]{:S(2)}, u32[]{:S(2)}) collective-permute-start(bf16[256,1536]{1,0:T(8,128)(2,1)} %slice.185), channel_id=1, source_target_pairs={{0,1},{1,0},{2,3},{3,2},{4,5},{5,4},{6,7},{7,6},{8,9},{9,8},{10,11... | collective-permute-start | bytes 2359304 | tf_op jit(solution)/shard_map/ppermute | solution.py:516
  711.5 89.9 %all-to-all-start.5 = ((bf16[8,48,1664]{2,1,0:T(8,128)(2,1)}), bf16[8,48,1664]{2,1,0:T(8,128)(2,1)}, u32[]{:S(2)}, u32[]{:S(2)}) async-start(bf16[8,48,1664]{2,1,0:T(8,128)(2,1)} %add_convert_fusion.5), calls=%async_computation.5 | async-start | bytes 2555904 | tf_op jit(solution)/shard_map/all_to_all | solution.py:792
  801.3 65.6 %all-to-all-start.6 = ((bf16[8,320,512]{2,1,0:T(8,128)(2,1)}), bf16[8,320,512]{2,1,0:T(8,128)(2,1)}, u32[]{:S(2)}, u32[]{:S(2)}) async-start(bf16[8,320,512]{2,1,0:T(8,128)(2,1)} %attend_back.1.back_ref), calls=%async_computation.6 | async-start | bytes 5242880 | tf_op jit(solution)/shard_map/all_to_all | solution.py:800
  806.6 154.4 %reduce-scatter.6.cloned.1.call-start = ((), (), s32[]{:S(2)}) async-start(), calls=%async_computation.16 | async-start | bytes 5898240 | tf_op jit(solution)/shard_map/reduce_scatter | solution.py:745
  809.0 65.2 %collective-permute-start.26 = (bf16[256,1536]{1,0:T(8,128)(2,1)}, bf16[256,1536]{1,0:T(8,128)(2,1)}, u32[]{:S(2)}, u32[]{:S(2)}) collective-permute-start(bf16[256,1536]{1,0:T(8,128)(2,1)} %add_convert_fusion.8), channel_id=1, source_target_pairs={{0,1},{1,0},{2,3},{3,2},{4,5},{5,4},{6,7},{7,6},{8,9},{9,8},{10,11... | collective-permute-start | bytes 2359304 | tf_op jit(solution)/shard_map/ppermute | solution.py:516
  825.9 16.2 %collective-permute-start.28 = (bf16[8,48,320]{2,1,0:T(8,128)(2,1)S(1)}, bf16[8,48,320]{2,1,0:T(8,128)(2,1)S(1)}, u32[]{:S(2)}, u32[]{:S(2)}) collective-permute-start(bf16[8,48,320]{2,1,0:T(8,128)(2,1)S(1)} %get-tuple-element.284), channel_id=1, source_target_pairs={{0,2},{1,3},{2,0},{3,1},{4,6},{5,7},{6,4},{7,5},{8,10},{9,11},{10,... | collective-permute-start | bytes 737288 | tf_op jit(solution)/shard_map/ppermute | solution.py:516
  826.4 15.7 %collective-permute-start.29 = (bf16[8,48,320]{2,1,0:T(8,128)(2,1)S(1)}, bf16[8,48,320]{2,1,0:T(8,128)(2,1)S(1)}, u32[]{:S(2)}, u32[]{:S(2)}) collective-permute-start(bf16[8,48,320]{2,1,0:T(8,128)(2,1)S(1)} %get-tuple-element.283), channel_id=1, source_target_pairs={{0,3},{1,2},{2,1},{3,0},{4,7},{5,6},{6,5},{7,4},{8,11},{9,10},{10,... | collective-permute-start | bytes 737288 | tf_op jit(solution)/shard_map/ppermute | solution.py:516
  830.0 44.2 %collective-permute-start.25 = (bf16[256,1536]{1,0:T(8,128)(2,1)}, bf16[256,1536]{1,0:T(8,128)(2,1)}, u32[]{:S(2)}, u32[]{:S(2)}) collective-permute-start(bf16[256,1536]{1,0:T(8,128)(2,1)} %add_convert_fusion.9), channel_id=1, source_target_pairs={{0,2},{1,3},{2,0},{3,1},{4,6},{5,7},{6,4},{7,5},{8,10},{9,11},{10,... | collective-permute-start | bytes 2359304 | tf_op jit(solution)/shard_map/ppermute | solution.py:516
  881.0 22.1 %all-to-all-start.7 = ((bf16[8,48,320]{2,1,0:T(8,128)(2,1)}), bf16[8,48,320]{2,1,0:T(8,128)(2,1)S(1)}, u32[]{:S(2)}, u32[]{:S(2)}) async-start(bf16[8,48,320]{2,1,0:T(8,128)(2,1)} %fusion.16), calls=%async_computation.7 | async-start | bytes 589824 | tf_op jit(solution)/shard_map/all_to_all | solution.py:814
  907.5 19.8 %collective-permute-start.31 = (bf16[48,4224]{1,0:T(8,128)(2,1)S(1)}, bf16[48,4224]{1,0:T(8,128)(2,1)S(1)}, u32[]{:S(2)}, u32[]{:S(2)}) collective-permute-start(bf16[48,4224]{1,0:T(8,128)(2,1)S(1)} %get-tuple-element.290), channel_id=1, source_target_pairs={{0,2},{1,3},{2,0},{3,1},{4,6},{5,7},{6,4},{7,5},{8,10},{9,11},{10,... | collective-permute-start | bytes 1216520 | tf_op jit(solution)/shard_map/ppermute | solution.py:516
  909.0 18.3 %collective-permute-start.32 = (bf16[48,4224]{1,0:T(8,128)(2,1)S(1)}, bf16[48,4224]{1,0:T(8,128)(2,1)S(1)}, u32[]{:S(2)}, u32[]{:S(2)}) collective-permute-start(bf16[48,4224]{1,0:T(8,128)(2,1)S(1)} %get-tuple-element.290), channel_id=1, source_target_pairs={{0,3},{1,2},{2,1},{3,0},{4,7},{5,6},{6,5},{7,4},{8,11},{9,10},{10,... | collective-permute-start | bytes 1216520 | tf_op jit(solution)/shard_map/ppermute | solution.py:516
  (52 other events, 863.8 us)
Sparse Core Ops, SparseCore 0:
  10.3 73.6 all-gather.5
  86.2 63.3 all-gather.7
  158.8 50.3 all-gather.9
  269.9 76.5 all-gather.11
  369.6 47.2 reduce-scatter.13
  424.0 47.3 reduce-scatter.11
  473.7 122.9 reduce-scatter.9
  599.1 168.0 reduce-scatter.7
  867.1 87.5 reduce-scatter.5

commit v2 on v1

--- a/solution.py
+++ b/solution.py
@@ -146,7 +146,9 @@
             out[g, :, i * columns : (i + 1) * columns] = refs[i, g * size : (g + 1) * size, :]
 
 
-def attend_kernel(bk, sub, span, part_ref, pos_ref, q_ref, kv_ref, o_ref, lse_ref, q, keys, values, peak, total, acc):
+def attend_kernel(
+    bk, sub, span, part_ref, pos_ref, q_ref, kv_ref, o_ref, lse_ref, q, keys, values, peak, total, acc, highest
+):
     groups, size, bq = q.shape
     tile = pl.program_id(0)
 
@@ -159,30 +161,54 @@
 
     unpack_blocks(q_ref, q)
     unmasked, ends = key_tiles(tile * bq, bq, sub, span, part_ref[0], bk)
-    peak[...] = jnp.full(peak.shape, NEG, F32)
-    total[...] = jnp.zeros(total.shape, F32)
-    acc[...] = jnp.zeros(acc.shape, F32)
-
-    def step(j, masked):
+
+    def reset():
+        peak[...] = jnp.full(peak.shape, NEG, F32)
+        total[...] = jnp.zeros(total.shape, F32)
+        acc[...] = jnp.zeros(acc.shape, F32)
+
+    def step(j, masked, moving):
         start = pl.multiple_of(j * bk, bk)
         k = keys[pl.ds(start, bk), :]
         v = values[:, pl.ds(start, bk)]
         if masked:
             allowed = (start + lax.broadcasted_iota(jnp.int32, (bk, bq), 0)) <= pos_ref[...]
+
+        def score(g):
+            scores = jnp.dot(k, q[g], preferred_element_type=F32)
+            return jnp.where(allowed, scores, NEG) if masked else scores
+
+        ahead = score(0)
         for g in range(groups):
-            scores = jnp.dot(k, q[g], preferred_element_type=F32)
-            if masked:
-                scores = jnp.where(allowed, scores, NEG)
+            scores = ahead
+            if g + 1 < groups:
+                ahead = score(g + 1)
             old = peak[g]
-            new = jnp.maximum(old, jnp.max(scores, axis=0, keepdims=True))
+            most = jnp.max(scores, axis=0, keepdims=True)
+            if moving:
+                new = jnp.maximum(old, most)
+                factor = jnp.exp(old - new)
+                peak[g] = new
+                total[g] = total[g] * factor
+                acc[g] = acc[g] * factor
+            else:
+                new = old
+                highest[g] = jnp.maximum(highest[g], most)
             weights = jnp.exp(scores - new)
-            factor = jnp.exp(old - new)
-            peak[g] = new
-            total[g] = total[g] * factor + jnp.sum(weights, axis=0, keepdims=True)
-            acc[g] = acc[g] * factor + jnp.dot(v, weights.astype(BF16), preferred_element_type=F32)
-
-    loop(0, unmasked, lambda j: step(j, False))
-    loop(unmasked, ends, lambda j: step(j, True))
+            total[g] += jnp.sum(weights, axis=0, keepdims=True)
+            acc[g] += jnp.dot(v, weights.astype(BF16), preferred_element_type=F32)
+
+    reset()
+    loop(unmasked, ends, lambda j: step(j, True, True))
+    highest[...] = peak[...]
+    loop(0, unmasked, lambda j: step(j, False, False))
+
+    @pl.when(jnp.max(highest[...] - peak[...]) > 30.0)
+    def _():
+        reset()
+        loop(0, unmasked, lambda j: step(j, False, True))
+        loop(unmasked, ends, lambda j: step(j, True, True))
+
     for g in range(groups):
         out = (acc[g] / total[g]).astype(BF16)
         lse_ref[g] = peak[g] + jnp.log(total[g])
@@ -217,6 +243,7 @@
             pltpu.VMEM((groups, 1, bq), F32),
             pltpu.VMEM((groups, 1, bq), F32),
             pltpu.VMEM((groups, size, bq), F32),
+            pltpu.VMEM((groups, 1, bq), F32),
         ],
         compiler_params=params("arbitrary"),
         cost_estimate=COST,
@@ -450,15 +477,128 @@
         ],
         scratch_shapes=[pltpu.VMEM((width, 3 * FFE), BF16)],
         compiler_params=params("arbitrary"),
-        cost_estimate=COST,
+        cost_estimate=pl.CostEstimate(
+            flops=2 * count * rows * width * 9 * FFE, bytes_accessed=count * rows * width * 8, transcendentals=0
+        ),
         name="experts",
     )(place, rank, prob, *xs, *gs, gateup, down)
+
+
+def add_kernel(left_ref, right_ref, sum_ref):
+    sum_ref[...] = (left_ref[...].astype(F32) + right_ref[...].astype(F32)).astype(BF16)
+
+
+def add(left, right):
+    pairs, count, own, wide = left.shape
+    block = pl.BlockSpec((1, 1, own, wide), lambda i, e: (i, e, 0, 0))
+    return pl.pallas_call(
+        add_kernel,
+        grid=(pairs, count),
+        in_specs=[block, block],
+        out_specs=block,
+        out_shape=jax.ShapeDtypeStruct(left.shape, BF16),
+        compiler_params=params("arbitrary", "arbitrary"),
+        cost_estimate=COST,
+        name="add",
+    )(left, right)
+
+
+def outer_kernel(rows_ref, grad_ref, side_ref, full_ref):
+    owners, _, piece, _ = full_ref.shape
+    width = grad_ref.shape[1]
+    product = jnp.dot(rows_ref[...], grad_ref[...], preferred_element_type=F32).astype(BF16)
+    for i in range(owners):
+        part = slice(i * piece, (i + 1) * piece)
+        full_ref[i, 0, :, :width] = product[part]
+        full_ref[i, 0, :, width:] = side_ref[part, :]
+
+
+def outer(rows, grad, side, owners, own):
+    height, span = rows.shape
+    width = grad.shape[1]
+    wide = width + side.shape[1]
+    return pl.pallas_call(
+        outer_kernel,
+        grid=(height // own,),
+        in_specs=[
+            pl.BlockSpec((own, span), lambda c: (c, 0)),
+            whole(span, width),
+            pl.BlockSpec((own, side.shape[1]), lambda c: (c, 0)),
+        ],
+        out_specs=pl.BlockSpec((owners, 1, own // owners, wide), lambda c: (0, c, 0, 0)),
+        out_shape=jax.ShapeDtypeStruct((owners, height // own, own // owners, wide), BF16),
+        compiler_params=params("arbitrary"),
+        cost_estimate=COST,
+        name="outer",
+    )(rows, grad, side)
+
+
+def gather_parts_kernel(mixed_ref, head_ref, part_ref):
+    count, _, wide = mixed_ref.shape
+    part_ref[:, :wide] = sum(mixed_ref[c].astype(F32) for c in range(count)).astype(BF16)
+    for h in range(KEY_VALUE_HEADS):
+        head = head_ref[h]
+        part_ref[:, wide + h * QROWS : wide + (h + 1) * QROWS] = head[:, :QROWS]
+        base = wide + KEY_VALUE_HEADS * QROWS
+        for i in range(2):
+            start = base + (i * KEY_VALUE_HEADS + h) * HEAD_SIZE
+            part_ref[:, start : start + HEAD_SIZE] = head[:, QROWS + i * HEAD_SIZE : QROWS + (i + 1) * HEAD_SIZE]
+
+
+def gather_parts(mixed, heads):
+    _, piece, wide = mixed.shape
+    total = wide + KEY_VALUE_HEADS * SLICE
+    return pl.pallas_call(
+        gather_parts_kernel,
+        grid=(1,),
+        in_specs=[whole(*mixed.shape), whole(*heads.shape)],
+        out_specs=whole(piece, total),
+        out_shape=jax.ShapeDtypeStruct((piece, total), BF16),
+        compiler_params=params("arbitrary"),
+        cost_estimate=COST,
+        name="gather_parts",
+    )(mixed, heads)
+
+
+def finish_kernel(count, me_ref, *refs):
+    blocks, (wq, wk, wv, q_ref, k_ref, v_ref, o_ref, side_ref) = refs[:count], refs[count:]
+    piece = blocks[0].shape[0]
+    width, heads, pair = q_ref.shape[1], k_ref.shape[1], EXPERTS + 1
+    for i in range(count):
+        rows = pl.ds(pl.multiple_of((me_ref[0] ^ i) * piece, piece), piece)
+        block = blocks[i][...].astype(F32)
+        o_ref[rows, :] = block[:, :width]
+        start = width + EXTRA
+        query, key = block[:, start : start + width], block[:, start + width : start + width + heads]
+        value = block[:, start + width + heads :]
+        q_ref[rows, :], k_ref[rows, :], v_ref[rows, :] = query, key, value
+        inner = jnp.sum(wq[rows, :].astype(F32) * query, axis=1, keepdims=True)
+        inner += jnp.sum(wk[rows, :].astype(F32) * key, axis=1, keepdims=True)
+        inner += jnp.sum(wv[rows, :].astype(F32) * value, axis=1, keepdims=True)
+        column = lax.broadcasted_iota(jnp.int32, (piece, EXTRA), 1)
+        side_ref[rows, :] = jnp.where(column == pair, inner, block[:, width:start])
+
+
+def finish(me, blocks, query_weight, key_matrix, value_matrix):
+    weights = [query_weight, key_matrix, value_matrix]
+    own, width = query_weight.shape
+    shapes = [array.shape for array in weights] + [(own, width), (own, EXTRA)]
+    return pl.pallas_call(
+        functools.partial(finish_kernel, len(blocks)),
+        grid=(1,),
+        in_specs=[pl.BlockSpec(memory_space=pltpu.SMEM)] + [whole(*array.shape) for array in [*blocks, *weights]],
+        out_specs=[whole(*shape) for shape in shapes],
+        out_shape=[jax.ShapeDtypeStruct(shape, F32) for shape in shapes],
+        compiler_params=params("arbitrary"),
+        cost_estimate=COST,
+        name="finish",
+    )(me.astype(jnp.int32).reshape(1), *blocks, *weights)
 
 
 def unpack_kernel(sum_ref, *refs):
     gateup_ref, down_ref = refs[-2:]
     gateup_ref[0] = sum_ref[0, :, : 2 * FFE].astype(F32)
-    down_ref[0] = jnp.transpose(sum_ref[0, :, 2 * FFE :].astype(F32), (1, 0))
+    down_ref[0] = sum_ref[0, :, 2 * FFE :].astype(F32)
 
 
 def unpack(total, offset, experts, held):
@@ -469,11 +609,11 @@
         in_specs=[pl.BlockSpec((1, own, wide), lambda e: (e, 0, 0))] + [pl.BlockSpec(memory_space=pl.ANY)] * len(held),
         out_specs=[
             pl.BlockSpec((1, own, 2 * FFE), lambda e: (e + offset, 0, 0)),
-            pl.BlockSpec((1, FFE, own), lambda e: (e + offset, 0, 0)),
+            pl.BlockSpec((1, own, FFE), lambda e: (e + offset, 0, 0)),
         ],
         out_shape=[
             jax.ShapeDtypeStruct((experts, own, 2 * FFE), F32),
-            jax.ShapeDtypeStruct((experts, FFE, own), F32),
+            jax.ShapeDtypeStruct((experts, own, FFE), F32),
         ],
         input_output_aliases={1 + i: i for i in range(len(held))},
         compiler_params=params("arbitrary"),
@@ -548,7 +688,8 @@
     own = use(array, 0)
     own, one, two, early = lax.optimization_barrier((own, one, two, early))
     far = jnp.concatenate([swapped(two[:half], axis, 1), swapped(one[half:], axis, 2)], axis=0)
-    return [own, use(one, 1), use(two, 2), use(far, 3)], early
+    one, two, far = lax.optimization_barrier((use(one, 1), use(two, 2), far))
+    return [own, one, two, use(far, 3)], early
 
 
 def wide_sum(*arrays):
@@ -678,10 +819,9 @@
 
     every = jnp.arange(n_ctx * span, dtype=jnp.int32).reshape(n_ctx, span)
     table = angles(every)
-    pieces = 2
+    cut = span * 3 // 4 if span % 512 == 0 else span // 2
     x_pieces = [
-        lax.all_gather(piece, "ctx", axis=0, tiled=False)
-        for piece in jnp.split(tokens_in, pieces, axis=0)
+        lax.all_gather(part_in, "ctx", axis=0, tiled=False) for part_in in (tokens_in[:cut], tokens_in[cut:])
     ]
     grad_in = cotangent.reshape(span, width)
     held = gather_start(grad_in, "expert")
@@ -691,7 +831,7 @@
     grad_blocks = gather_end(*held, "expert")
     buffers = project(x_pieces[0], gain_one[None], head_weight, table, 0, ())
     x_pieces[1], grad_blocks, buffers = lax.optimization_barrier((x_pieces[1], grad_blocks, buffers))
-    normed_all, q_all, kv_all = project(x_pieces[1], gain_one[None], head_weight, table, 1, buffers)
+    normed_all, q_all, kv_all = project(x_pieces[1], gain_one[None], head_weight, table, cut // (span - cut), buffers)
     if parts == 1:
         queries, positions, q_table = q_all, every, table
     else:
@@ -738,25 +878,29 @@
     backs, outs, sums = [], [], []
     core_line = [[z * 2 + core for z in range(n_ctx // 2)] for core in range(2)]
 
-    def pair_sum(mine, theirs):
-        return wide_sum(mine, swapped(theirs, "ctx", 1)).astype(BF16)
-
     def line_sum(pair):
         total = lax.psum_scatter(
             pair.reshape(-1, 3 * FFE), "ctx", scatter_dimension=0, tiled=True, axis_index_groups=core_line
         )
         return total.reshape(-1, own_rows, 3 * FFE)
 
+    pairs, pair_sums = [], []
     for number, (offset, count) in enumerate(cuts):
+        if number == 1:
+            w_heads, place, _ = lax.optimization_barrier((w_heads, place, backs[0]))
+        elif number > 1:
+            if number > 2:
+                pairs[number - 2], _ = lax.optimization_barrier((pairs[number - 2], backs[-1]))
+            pair_sums.append(add(*pairs[number - 2]))
+            place, _, _ = lax.optimization_barrier((place, backs[-1], pair_sums[-1]))
         back, out, mine, theirs = run_experts(
             place, rank, prob, token_rows, grad_rows, gateup_weight, down_weight, offset, count, n_ctx, span, cap
         )
         backs.append(back)
         outs.append(out)
-        if number < len(cuts) - 1:
-            sums.append(line_sum(pair_sum(mine, theirs)))
-            if number == 1:
-                w_heads, place = lax.optimization_barrier((w_heads, place))
+        pairs.append((mine, swapped(theirs, "ctx", 1)))
+        if number > 1:
+            sums.append(line_sum(pair_sums[-1]))
     ranks = [rank[offset : offset + count] for offset, count in cuts]
 
     def to_tokens(rows):
@@ -768,34 +912,37 @@
     route_grad = back_sum[:, width : width + EXPERTS] + back_sum[:, width + EXPERTS : width + 2 * EXPERTS]
     chosen_grad = probs * (route_grad - jnp.sum(probs * route_grad, axis=-1, keepdims=True))
     logit_grad = chosen_grad.astype(BF16)
-    router_full = contract(normed_two, logit_grad, 0, 0)
     normed_two_grad = back_sum[:, :width] + contract(logit_grad, router, 1, 1)
     ffn_gain_full = jnp.sum(normed_two_grad * hidden * rms_two, axis=0)
     hidden_grad = grad + norm_back(normed_two_grad, hidden, rms_two, gain_two)
     hidden_low = hidden_grad.astype(BF16)
     attended_grad = contract(w_output, hidden_low, 1, 1).astype(BF16)
+    attended_grad, hidden_low, logit_grad, pairs = lax.optimization_barrier(
+        (attended_grad, hidden_low, logit_grad, pairs[-2:])
+    )
+    sums.append(line_sum(add(*pairs[0])))
+    router_full = contract(normed_two, logit_grad, 0, 0)
     attended_grad = attended_grad.reshape(KEY_VALUE_HEADS, QROWS, parts, sub).transpose(0, 2, 1, 3)
     attended_grad = lax.all_to_all(attended_grad.reshape(n_ctx, QROWS, sub), "ctx", 0, 0, tiled=True)
-    outproj_full = jnp.dot(attended_rows, hidden_low, preferred_element_type=F32)
     column = jnp.arange(EXTRA)[None]
     side = jnp.where(
         column == EXPERTS, ffn_gain_full[:, None], jnp.pad(router_full, ((0, 0), (0, EXTRA - EXPERTS)))
     ).astype(BF16)
-    mixed_full = jnp.concatenate([outproj_full.astype(BF16), lax.optimization_barrier(side)], axis=1)
-
-    mixed_parts = for_partners(mixed_full.reshape(n_ctx, n_owner, -1, mixed_full.shape[1]), "expert", 1)
-    theirs, hidden_low = lax.optimization_barrier((theirs, hidden_low))
-    pair, outs, mixed_parts = lax.optimization_barrier((pair_sum(mine, theirs), outs, mixed_parts))
-    mixed_part = sum_from_partners(mixed_parts, "expert")
-    out_parts = return_start(to_tokens(outs), "expert")
-    out_parts, attended_grad, mixed_part = lax.optimization_barrier((out_parts, attended_grad, mixed_part))
+    mixed_parts = for_partners(outer(attended_rows, hidden_low, side, n_owner, own_rows), "expert", 0)
+    earlier = sums[:-1]
+    pairs[1], outs, earlier, mixed_parts = lax.optimization_barrier((pairs[1], outs, earlier, mixed_parts))
+    pair = add(*pairs[1])
+    grads = ()
+    for (offset, _), total in zip(cuts, earlier):
+        grads = unpack(total, offset, local_experts, grads)
+    out_parts, attended_grad, grads, mixed_part, pair = lax.optimization_barrier(
+        (to_tokens(outs), attended_grad, grads, sum_from_partners(mixed_parts, "expert"), pair)
+    )
     mixed_part = lax.all_to_all(mixed_part, "ctx", 0, 0, tiled=True)
     backs = attend_back(
         part_arg, pos, queries, attended, attended_grad, lse, kv_all, q_table, table, tile, tile, sub, span
     )
     mixed_part, backs = lax.optimization_barrier((mixed_part, backs))
-    output = hidden + return_end(out_parts, "expert")
-    output = output.astype(BF16).reshape(1, span, width)
     if len(backs) == 1:
         rows_back = lax.all_to_all(backs[0], "ctx", 0, 0, tiled=True).reshape(-1, span)
         head_grad = head_grads(backs[0], normed_all)
@@ -810,36 +957,32 @@
         head_grad = jnp.concatenate([head_grads(query_back, normed_part), head_grads(kv_back, normed_all)], axis=1)
     head_parts = for_partners(head_grad.reshape(n_ctx, n_owner, -1, SLICE), "expert", 1)
     head_part = sum_from_partners(head_parts, "expert")
+    grads = unpack(sums[-1], cuts[-2][0], local_experts, grads)
     pair, rows_back, head_part = lax.optimization_barrier((pair, rows_back, head_part))
+    head_part, out_parts = lax.optimization_barrier((head_part, out_parts))
     head_part = lax.all_to_all(head_part, "ctx", 0, 0, tiled=True)
+    output = hidden + return_end(return_start(out_parts, "expert"), "expert")
+    output = output.astype(BF16).reshape(1, span, width)
     sums.append(line_sum(pair))
-    grads = ()
-    for (offset, _), total in zip(cuts, sums):
-        grads = unpack(total, offset, local_experts, grads)
-    gateup_grad, down_grad = grads
-    mixed_sum = jnp.sum(mixed_part.astype(F32), axis=0).astype(BF16)
-    head_sum = jnp.sum(head_part.astype(F32).reshape(KEY_VALUE_HEADS, parts, -1, SLICE), axis=1).astype(BF16)
-    head_sum = head_sum.transpose(1, 0, 2).reshape(-1, KEY_VALUE_HEADS * SLICE)
-    last = all_of_expert(jnp.concatenate([mixed_sum, head_sum], axis=1)).reshape(own_rows, -1).astype(F32)
-    mixed_sum = last[:, : -KEY_VALUE_HEADS * SLICE]
-    head_grad = last[:, -KEY_VALUE_HEADS * SLICE :].reshape(own_rows, KEY_VALUE_HEADS, SLICE)
+    gateup_grad, down_grad = unpack(sums[-1], cuts[-1][0], local_experts, grads)
+    down_grad = down_grad.transpose(0, 2, 1)
+    if parts > 1:
+        head_part = jnp.sum(head_part.astype(F32).reshape(KEY_VALUE_HEADS, parts, piece, SLICE), axis=1).astype(BF16)
+    summed = gather_parts(mixed_part, head_part)
+    summed = [summed] + [swapped(summed, "expert", k) for k in range(1, n_owner)]
+    place = me
+    if piece % 16:
+        summed, place = [in_order(summed, "expert").reshape(own_rows, -1)], 0 * me
+    query_grad, key_grad, value_grad, outproj_grad, side = finish(
+        place, summed, query_weight, key_matrix, value_matrix
+    )
+    router_grad, ffn_gain_grad = side[:, :EXPERTS], side[:, EXPERTS]
+    attn_gain_grad = side[:, EXPERTS + 1] / attn_gain.astype(F32)
     normed_one_grad = contract(rows_back, w_heads, 0, 0)
     rms_one = lax.rsqrt(jnp.mean(flat_in * flat_in, axis=-1, keepdims=True) + EPS)
     input_grad = (
         (hidden_grad + norm_back(normed_one_grad, flat_in, rms_one, gain_one)).astype(BF16).reshape(1, span, width)
     )
-
-    outproj_grad = mixed_sum[:, :width]
-    router_grad = mixed_sum[:, width : width + EXPERTS]
-    ffn_gain_grad = mixed_sum[:, width + EXPERTS]
-    query_grad = head_grad[..., :QROWS].reshape(own_rows, -1)
-    key_grad = head_grad[..., QROWS : QROWS + HEAD_SIZE].reshape(own_rows, -1)
-    value_grad = head_grad[..., QROWS + HEAD_SIZE :].reshape(own_rows, -1)
-    attn_gain_grad = (
-        jnp.sum(query_weight.astype(F32) * query_grad, axis=1)
-        + jnp.sum(key_matrix.astype(F32) * key_grad, axis=1)
-        + jnp.sum(value_matrix.astype(F32) * value_grad, axis=1)
-    ) / attn_gain.astype(F32)
     return (
         output,
         input_grad,

time: 986 us -> 910 us (0.923)
  other arithmetic: 85.4 us -> 43.7 us
  Pallas kernels: 399 us -> 437 us
  waiting for transfers between devices: 291 us -> 255 us
  local copies, waits for them, and re-layouts: 76.6 us -> 47.1 us
    pallas_call x0 -> x8, Pallas kernels: none -> 55.9 us  [the longest x5 41.3 us: add(): pl.pallas_call(add_kernel, grid=(pairs, count), in_specs=[block, block],...]
    convert_element_type x6 -> x1, other arithmetic: 33.7 us -> 0.28 us  [per_device(): logit_grad = chosen_grad.astype(BF16)]
    ppermute x37, waiting for transfers between devices: 140 us -> 110 us  [swapped(): return lax.ppermute(array, axis, [(i, i ^ mask) for i in range(count)])]
    pallas_call x1, Pallas kernels: 61 us -> 42.6 us  [attend(): pl.pallas_call(functools.partial(attend_kernel, bk, sub, span), grid=(nq...]
    unnamed x99 -> x98, local copies, waits for them, and re-layouts: 22.2 us -> 11.8 us
  transfers between devices with their start and end apart: 54 -> 54, of which waited for: 29 -> 28; matrix products, arithmetic and copies ran while one was open for 18% -> 11% of each run, Pallas kernels for 40% -> 48%
where the time goes in v2:
time: 910 us; the launch traced here: 898 us
  Pallas kernels  437 us (48%)
  waiting for transfers between devices  255 us (28%)
  starting transfers between devices  75.3 us (8%)
  local copies, waits for them, and re-layouts  47.1 us (5%)
  other arithmetic  43.7 us (5%)
  matrix products  24.6 us (3%)
  between operations  14.8 us (2%)
    pallas_call x5, Pallas kernels, run_experts(): pl.pallas_call(functools.partial(experts_kernel, span, cap, offset, block...  115 us
    ppermute x37, waiting for transfers between devices, swapped(): return lax.ppermute(array, axis, [(i, i ^ mask) for i in range(count)])  110 us
    pallas_call x1, Pallas kernels, attend_back(): pl.pallas_call(functools.partial(attend_back_kernel, bk, sub, span), grid...  84.1 us
    all_gather x2, waiting for transfers between devices, per_device(): lax.all_gather(part_in, 'ctx', axis=0, tiled=False)  56.8 us
    pallas_call x8, Pallas kernels, combine(): pl.pallas_call(functools.partial(combine_kernel, cap, len(ranks)), grid=(...  53.3 us
    pallas_call x1, Pallas kernels, attend(): pl.pallas_call(functools.partial(attend_kernel, bk, sub, span), grid=(nq...  42.6 us
    pallas_call x5, Pallas kernels, add(): pl.pallas_call(add_kernel, grid=(pairs, count), in_specs=[block, block],...  41.3 us
    ppermute x37, starting transfers between devices, swapped(): return lax.ppermute(array, axis, [(i, i ^ mask) for i in range(count)])  40.3 us
  transfers between devices with their start and end apart: 54, of which 28 were waited for; matrix products, arithmetic and copies ran while one was open for 11% of the time, Pallas kernels for 48%

profile of v2, /device:TPU:0, one launch (start us, length us, event | category | flops | bytes accessed | tf_op | source)
XLA Modules:
  0.0 897.6 jit_solution(9745342609582484804)
XLA Ops:
  18.6 4.9 all-to-all-start
  24.4 17.3 %all-to-all-done = bf16[8,48,384]{2,1,0:T(8,128)(2,1)S(1)} async-done(((bf16[8,48,384]{2,1,0:T(8,128)(2,1)}), bf16[8,48,384]{2,1,0:T(8,128)(2,1)S(1)}, u32[]{:S(2)}, u32[]{:S(2)}) %all-to-all-start) | async-done | bytes 294944 | tf_op jit(solution)/shard_map/all_to_all | solution.py:802
  57.1 5.5 collective-permute-done.3
  65.1 44.8 %all-gather.6.cloned.1.call-done.x_ref = bf16[8,384,1536]{2,1,0:T(8,128)(2,1)} async-done(((bf16[1,384,1536]{2,1,0:T(8,128)(2,1)}), bf16[8,384,1536]{2,1,0:T(8,128)(2,1)}) %all-gather.6.cloned.1.call-update) | async-done | bytes 9437200 | tf_op jit(solution)/shard_map/all_gather | solution.py:824
  120.8 11.6 %project.2 = (bf16[8,512,1536]{2,1,0:T(8,128)(2,1)}, bf16[8,192,512]{2,1,0:T(8,128)(2,1)}, bf16[8,128,512]{2,1,0:T(8,128)(2,1)}) custom-call(bf16[8,384,1536]{2,1,0:T(8,128)(2,1)} %all-gather.6.cloned.1.call-done.x_ref, f32[1,1536]{1,0:T(1,128)} %reshape.225.gain_ref, bf16[320,1536]{1,0:T(8,128)(2,1)} %bitcast.111, ...), custom_call_target="tpu_custom_call" | custom-call | flops 1024 | bytes 1024 | tf_op jit(solution)/shard_map/project/pallas_call | solution.py:67
  136.8 12.0 %all-gather.8.cloned.1.call-done.x_ref = bf16[8,128,1536]{2,1,0:T(8,128)(2,1)} async-done(((bf16[1,128,1536]{2,1,0:T(8,128)(2,1)}), bf16[8,128,1536]{2,1,0:T(8,128)(2,1)}) %all-gather.8.cloned.1.call-update) | async-done | bytes 3145744 | tf_op jit(solution)/shard_map/all_gather | solution.py:824
  148.8 8.0 project.3
  157.4 42.6 %attend.1 = (bf16[8,192,512]{2,1,0:T(8,128)(2,1)}, f32[3,1,4096]{2,1,0:T(1,128)}) custom-call(s32[1]{0:T(128)} %constant.101.clone.1.part_ref, s32[1,4096]{1,0:T(1,128)} %iota.44.pos_ref, bf16[8,192,512]{2,1,0:T(8,128)(2,1)} %get-tuple-element.147.q_ref, bf16[8,128,512]{2,1,0:T(8,128)(2,1)} %get-tuple-element.148.kv_ref), custom_call_target="tpu_custom_call" | custom-call | flops 1024 | bytes 1024 | tf_op jit(solution)/shard_map/attend/pallas_call | solution.py:225
  205.5 4.9 dispatch.8.refs_4_
  210.4 4.9 dispatch.11.refs_7_
  215.3 4.9 dispatch.10.refs_6_
  220.2 4.9 dispatch.9.refs_5_
  225.1 17.2 %all-to-all-done.2 = bf16[8,192,512]{2,1,0:T(8,128)(2,1)} async-done(((bf16[8,192,512]{2,1,0:T(8,128)(2,1)}), bf16[8,192,512]{2,1,0:T(8,128)(2,1)}, u32[]{:S(2)}, u32[]{:S(2)}) %all-to-all-start.2) | async-done | bytes 1572896 | tf_op jit(solution)/shard_map/all_to_all | solution.py:853
  242.3 5.3 multiply_reduce_fusion.2
  263.3 24.9 %all-to-all-done.3 = f32[4,10,512]{2,1,0:T(8,128)S(1)} async-done(((f32[4,10,512]{2,1,0:T(8,128)}), f32[4,10,512]{2,1,0:T(8,128)S(1)}, u32[]{:S(2)}, u32[]{:S(2)}) %all-to-all-start.3) | async-done | bytes 81952 | tf_op jit(solution)/shard_map/all_to_all | solution.py:816
  294.9 5.0 dispatch.14.refs_2_
  311.8 5.3 dispatch.15.refs_3_
  317.1 13.9 %experts.5 = (bf16[1,512,1664]{2,1,0:T(8,128)(2,1)}, bf16[1,512,1536]{2,1,0:T(8,128)(2,1)}, bf16[4,1,192,1536]{3,2,1,0:T(8,128)(2,1)}, bf16[4,1,192,1536]{3,2,1,0:T(8,128)(2,1)}) custom-call(s32[2]{0:T(128)} %pad_add_fusion.place_ref, s32[10,1,2048]{2,1,0:T(1,128)} %copy_convert_fusion.rank_ref, f32[10,1,2048]{2,1,0:T(1,128)} %broadcast_in_dim.74.prob_ref, ...), custom_call_target="tpu_custom_call" | custom-call | flops 7247757312 | bytes 6291456 | tf_op jit(solution)/shard_map/experts/pallas_call | solution.py:465
  342.0 13.9 %experts.6 = (bf16[1,512,1664]{2,1,0:T(8,128)(2,1)}, bf16[1,512,1536]{2,1,0:T(8,128)(2,1)}, bf16[4,1,192,1536]{3,2,1,0:T(8,128)(2,1)}, bf16[4,1,192,1536]{3,2,1,0:T(8,128)(2,1)}) custom-call(s32[2]{0:T(128)} %pad_add_fusion.place_ref, s32[10,1,2048]{2,1,0:T(1,128)} %copy_convert_fusion.rank_ref, f32[10,1,2048]{2,1,0:T(1,128)} %broadcast_in_dim.74.prob_ref, ...), custom_call_target="tpu_custom_call" | custom-call | flops 7247757312 | bytes 6291456 | tf_op jit(solution)/shard_map/experts/pallas_call | solution.py:465
  356.0 31.6 %experts.7 = (bf16[3,512,1664]{2,1,0:T(8,128)(2,1)}, bf16[3,512,1536]{2,1,0:T(8,128)(2,1)}, bf16[4,3,192,1536]{3,2,1,0:T(8,128)(2,1)}, bf16[4,3,192,1536]{3,2,1,0:T(8,128)(2,1)}) custom-call(s32[2]{0:T(128)} %pad_add_fusion.place_ref, s32[10,1,2048]{2,1,0:T(1,128)} %copy_convert_fusion.rank_ref, f32[10,1,2048]{2,1,0:T(1,128)} %broadcast_in_dim.74.prob_ref, ...), custom_call_target="tpu_custom_call" | custom-call | flops 21743271936 | bytes 18874368 | tf_op jit(solution)/shard_map/experts/pallas_call | solution.py:465
  394.0 31.5 %experts.8 = (bf16[3,512,1664]{2,1,0:T(8,128)(2,1)}, bf16[3,512,1536]{2,1,0:T(8,128)(2,1)}, bf16[4,3,192,1536]{3,2,1,0:T(8,128)(2,1)}, bf16[4,3,192,1536]{3,2,1,0:T(8,128)(2,1)}) custom-call(s32[2]{0:T(128)} %pad_add_fusion.place_ref, s32[10,1,2048]{2,1,0:T(1,128)} %copy_convert_fusion.rank_ref, f32[10,1,2048]{2,1,0:T(1,128)} %broadcast_in_dim.74.prob_ref, ...), custom_call_target="tpu_custom_call" | custom-call | flops 21743271936 | bytes 18874368 | tf_op jit(solution)/shard_map/experts/pallas_call | solution.py:465
  425.5 12.0 %add.261 = bf16[4,3,192,1536]{3,2,1,0:T(8,128)(2,1)} custom-call(bf16[4,3,192,1536]{3,2,1,0:T(8,128)(2,1)} %get-tuple-element.186.left_ref, bf16[4,3,192,1536]{3,2,1,0:T(8,128)(2,1)} %collective-permute-done.13.right_ref), custom_call_target="tpu_custom_call" | custom-call | flops 1024 | bytes 1024 | tf_op jit(solution)/shard_map/add/pallas_call | solution.py:494
  440.5 23.7 %experts.9 = (bf16[2,512,1664]{2,1,0:T(8,128)(2,1)}, bf16[2,512,1536]{2,1,0:T(8,128)(2,1)}, bf16[4,2,192,1536]{3,2,1,0:T(8,128)(2,1)}, bf16[4,2,192,1536]{3,2,1,0:T(8,128)(2,1)}) custom-call(s32[2]{0:T(128)} %pad_add_fusion.place_ref, s32[10,1,2048]{2,1,0:T(1,128)} %copy_convert_fusion.rank_ref, f32[10,1,2048]{2,1,0:T(1,128)} %broadcast_in_dim.74.prob_ref, ...), custom_call_target="tpu_custom_call" | custom-call | flops 14495514624 | bytes 12582912 | tf_op jit(solution)/shard_map/experts/pallas_call | solution.py:465
  464.1 6.8 combine.11
  475.7 6.8 combine.10
  482.6 7.0 combine.9
  501.1 12.3 %collective-permute-done.19 = bf16[256,1664]{1,0:T(8,128)(2,1)S(1)} collective-permute-done((bf16[256,1664]{1,0:T(8,128)(2,1)S(1)}, bf16[256,1664]{1,0:T(8,128)(2,1)S(1)}, u32[]{:S(2)}, u32[]{:S(2)}) %collective-permute-start.19) | collective-permute-done | bytes 852000 | tf_op jit(solution)/shard_map/ppermute | solution.py:656
  514.9 7.4 combine.8
  522.3 10.7 %collective-permute-done.18 = bf16[256,1664]{1,0:T(8,128)(2,1)} collective-permute-done((bf16[256,1664]{1,0:T(8,128)(2,1)}, bf16[256,1664]{1,0:T(8,128)(2,1)}, u32[]{:S(2)}, u32[]{:S(2)}) %collective-permute-start.18) | collective-permute-done | bytes 852000 | tf_op jit(solution)/shard_map/ppermute | solution.py:656
  547.0 12.1 %add.263 = bf16[4,3,192,1536]{3,2,1,0:T(8,128)(2,1)} custom-call(bf16[4,3,192,1536]{3,2,1,0:T(8,128)(2,1)} %get-tuple-element.249.left_ref, bf16[4,3,192,1536]{3,2,1,0:T(8,128)(2,1)} %collective-permute-done.20.right_ref), custom_call_target="tpu_custom_call" | custom-call | flops 1024 | bytes 1024 | tf_op jit(solution)/shard_map/add/pallas_call | solution.py:494
  566.4 8.6 outer.1
  575.0 5.7 dynamic-slice_bitcast_fusion
  584.3 6.3 combine.15
  590.6 6.3 combine.14
  596.9 6.3 combine.13
  603.2 6.3 combine.12
  611.7 8.3 add.262
  625.8 13.0 %collective-permute-done.23 = bf16[8,48,1664]{2,1,0:T(8,128)(2,1)} collective-permute-done((bf16[8,48,1664]{2,1,0:T(8,128)(2,1)}, bf16[8,48,1664]{2,1,0:T(8,128)(2,1)}, u32[]{:S(2)}, u32[]{:S(2)}) %collective-permute-start.23) | collective-permute-done | bytes 1277984 | tf_op jit(solution)/shard_map/ppermute | solution.py:656
  644.1 4.9 all-to-all-start.5
  649.6 84.1 %attend_back.1.back_ref = bf16[8,320,512]{2,1,0:T(8,128)(2,1)} custom-call(s32[1]{0:T(128)} %constant.101.clone.1.part_ref, s32[1,4096]{1,0:T(1,128)} %iota.49.pos_ref, bf16[8,192,512]{2,1,0:T(8,128)(2,1)} %get-tuple-element.147.q_ref, bf16[8,192,512]{2,1,0:T(8,128)(2,1)} %get-tuple-element.149.o_ref, bf16[8,192,512]{2,1,0:T(8,128)(2,1)} %all-to-all-done.4.do_ref, ...), custom_call_target="tpu_custom_call" | custom-call | flops 1024 | bytes 1024 | tf_op jit(solution)/shard_map/attend_back/pallas_call | solution.py:347
  733.7 5.1 all-to-all-start.6
  738.9 13.5 %head_grads.1 = bf16[1536,320]{1,0:T(8,128)(2,1)} custom-call(bf16[8,320,512]{2,1,0:T(8,128)(2,1)} %attend_back.1.back_ref, bf16[8,512,1536]{2,1,0:T(8,128)(2,1)} %get-tuple-element.229.n_ref), custom_call_target="tpu_custom_call" | custom-call | flops 1024 | bytes 1024 | tf_op jit(solution)/shard_map/head_grads/pallas_call | solution.py:110
  757.2 6.3 collective-permute-done.25
  763.5 6.8 collective-permute-done.27
  773.5 25.7 %all-to-all-done.6 = bf16[8,320,512]{2,1,0:T(8,128)(2,1)} async-done(((bf16[8,320,512]{2,1,0:T(8,128)(2,1)}), bf16[8,320,512]{2,1,0:T(8,128)(2,1)}, u32[]{:S(2)}, u32[]{:S(2)}) %all-to-all-start.6) | async-done | bytes 2621472 | tf_op jit(solution)/shard_map/all_to_all | solution.py:947
  811.7 10.3 %fusion.2 = (f32[512]{0:T(512)S(1)}, f32[512]{0:T(512)S(1)}, f32[512,1536]{1,0:T(8,128)}) fusion(bf16[1,512,1536]{2,1,0:T(8,128)(2,1)S(1)} %copy-done.11, f32[1536]{0:T(1024)S(1)} %copy-done.33, bf16[2560,512]{1,0:T(8,128)(2,1)} %bitcast.36, bf16[2560,1536]{1,0:T(8,128)(2,1)} %all-gather.12.cloned.1.call-done), kind=kOutput, calls=%fused_computation.11 | convolution fusion | flops 4031249408 | bytes 15214592 | tf_op jit(solution)/shard_map/dot_general | solution.py:32
  838.7 17.8 %collective-permute-done.36.refs_3_ = bf16[48,4224]{1,0:T(8,128)(2,1)S(1)} collective-permute-done((bf16[48,4224]{1,0:T(8,128)(2,1)}, bf16[48,4224]{1,0:T(8,128)(2,1)S(1)}, u32[]{:S(2)}, u32[]{:S(2)}) %collective-permute-start.36) | collective-permute-done | bytes 405536 | tf_op jit(solution)/shard_map/ppermute | solution.py:656
  857.0 8.3 collective-permute-done.35.refs_2_
  (295 shorter events, 225.4 us)
Async XLA Ops:
  7.2 102.7 %all-gather.6.cloned.1.call-start = ((), (), s32[]{:S(2)}) async-start(), calls=%async_computation.13 | async-start | bytes 10616832 | tf_op jit(solution)/shard_map/all_gather | solution.py:824
  9.7 139.1 %all-gather.8.cloned.1.call-start = ((), (), s32[]{:S(2)}) async-start(), calls=%async_computation.14 | async-start | bytes 3538944 | tf_op jit(solution)/shard_map/all_gather | solution.py:824
  10.6 54.5 %collective-permute-start.1 = (bf16[512,1536]{1,0:T(8,128)(2,1)}, bf16[512,1536]{1,0:T(8,128)(2,1)}, u32[]{:S(2)}, u32[]{:S(2)}) collective-permute-start(bf16[512,1536]{1,0:T(8,128)(2,1)} %bitcast.120), channel_id=1, source_target_pairs={{0,2},{1,3},{2,0},{3,1},{4,6},{5,7},{6,4},{7,5},{8,10},{9,11},{10,... | collective-permute-start | bytes 4718600 | tf_op jit(solution)/shard_map/ppermute | solution.py:656
  13.6 51.5 %collective-permute-start = (bf16[512,1536]{1,0:T(8,128)(2,1)}, bf16[512,1536]{1,0:T(8,128)(2,1)}, u32[]{:S(2)}, u32[]{:S(2)}) collective-permute-start(bf16[512,1536]{1,0:T(8,128)(2,1)} %bitcast.121), channel_id=1, source_target_pairs={{0,1},{1,0},{2,3},{3,2},{4,5},{5,4},{6,7},{7,6},{8,9},{9,8},{10,11... | collective-permute-start | bytes 4718600 | tf_op jit(solution)/shard_map/ppermute | solution.py:656
  18.6 23.2 %all-to-all-start = ((bf16[8,48,384]{2,1,0:T(8,128)(2,1)}), bf16[8,48,384]{2,1,0:T(8,128)(2,1)S(1)}, u32[]{:S(2)}, u32[]{:S(2)}) async-start(bf16[8,48,384]{2,1,0:T(8,128)(2,1)} %copy.93), calls=%async_computation | async-start | bytes 589824 | tf_op jit(solution)/shard_map/all_to_all | solution.py:802
  45.2 197.1 %all-gather.10.cloned.1.call-start = ((), (), s32[]{:S(2)}) async-start(), calls=%async_computation.15 | async-start | bytes 5308416 | tf_op jit(solution)/shard_map/all_gather | solution.py:847
  113.2 20.0 %collective-permute-start.5 = (bf16[256,1536]{1,0:T(8,128)(2,1)}, bf16[256,1536]{1,0:T(8,128)(2,1)}, u32[]{:S(2)}, u32[]{:S(2)}) collective-permute-start(bf16[256,1536]{1,0:T(8,128)(2,1)} %slice.116), channel_id=1, source_target_pairs={{0,1},{1,0},{2,3},{3,2},{4,5},{5,4},{6,7},{7,6},{8,9},{9,8},{10,11... | collective-permute-start | bytes 2359304 | tf_op jit(solution)/shard_map/ppermute | solution.py:656
  114.7 19.5 %collective-permute-start.6 = (bf16[256,1536]{1,0:T(8,128)(2,1)S(1)}, bf16[256,1536]{1,0:T(8,128)(2,1)}, u32[]{:S(2)}, u32[]{:S(2)}) collective-permute-start(bf16[256,1536]{1,0:T(8,128)(2,1)S(1)} %slice.117), channel_id=1, source_target_pairs={{0,2},{1,3},{2,0},{3,1},{4,6},{5,7},{6,4},{7,5},{8,10},{9,11},{10,... | collective-permute-start | bytes 2359304 | tf_op jit(solution)/shard_map/ppermute | solution.py:656
  200.1 42.3 %all-to-all-start.2 = ((bf16[8,192,512]{2,1,0:T(8,128)(2,1)}), bf16[8,192,512]{2,1,0:T(8,128)(2,1)}, u32[]{:S(2)}, u32[]{:S(2)}) async-start(bf16[8,192,512]{2,1,0:T(8,128)(2,1)} %get-tuple-element.149.o_ref), calls=%async_computation.2 | async-start | bytes 3145728 | tf_op jit(solution)/shard_map/all_to_all | solution.py:853
  204.5 137.4 %all-gather.12.cloned.1.call-start = ((), (), s32[]{:S(2)}) async-start(), calls=%async_computation.21 | async-start | bytes 8847360 | tf_op jit(solution)/shard_map/all_gather | solution.py:862
  249.6 39.3 %collective-permute-start.8 = (bf16[512,1536]{1,0:T(8,128)(2,1)S(1)}, bf16[512,1536]{1,0:T(8,128)(2,1)}, u32[]{:S(2)}, u32[]{:S(2)}) collective-permute-start(bf16[512,1536]{1,0:T(8,128)(2,1)S(1)} %multiply_convert_fusion.token_ref), channel_id=1, source_target_pairs={{0,2},{1,3},{2,0},{3,1},{4,6},{5,7},{6,4},{7,5},{8,10},{9,11},{10,... | collective-permute-start | bytes 4718600 | tf_op jit(solution)/shard_map/ppermute | solution.py:656
  251.1 37.8 %collective-permute-start.7 = (bf16[512,1536]{1,0:T(8,128)(2,1)S(1)}, bf16[512,1536]{1,0:T(8,128)(2,1)}, u32[]{:S(2)}, u32[]{:S(2)}) collective-permute-start(bf16[512,1536]{1,0:T(8,128)(2,1)S(1)} %multiply_convert_fusion.token_ref), channel_id=1, source_target_pairs={{0,1},{1,0},{2,3},{3,2},{4,5},{5,4},{6,7},{7,6},{8,9},{9,8},{10,11... | collective-permute-start | bytes 4718600 | tf_op jit(solution)/shard_map/ppermute | solution.py:656
  254.8 33.4 %all-to-all-start.3 = ((f32[4,10,512]{2,1,0:T(8,128)}), f32[4,10,512]{2,1,0:T(8,128)S(1)}, u32[]{:S(2)}, u32[]{:S(2)}) async-start(f32[4,10,512]{2,1,0:T(8,128)} %reshape.207), calls=%async_computation.3 | async-start | bytes 262144 | tf_op jit(solution)/shard_map/all_to_all | solution.py:816
  258.2 322.5 %reduce-scatter.6.cloned.1.call-start = ((), (), s32[]{:S(2)}) async-start(), calls=%async_computation.16 | async-start | bytes 2949120 | tf_op jit(solution)/shard_map/reduce_scatter | solution.py:882
  291.3 18.0 %collective-permute-start.9 = (bf16[256,1536]{1,0:T(8,128)(2,1)S(1)}, bf16[256,1536]{1,0:T(8,128)(2,1)S(1)}, u32[]{:S(2)}, u32[]{:S(2)}) collective-permute-start(bf16[256,1536]{1,0:T(8,128)(2,1)S(1)} %slice.126), channel_id=1, source_target_pairs={{0,1},{1,0},{2,3},{3,2},{4,5},{5,4},{6,7},{7,6},{8,9},{9,8},{10,11... | collective-permute-start | bytes 2359304 | tf_op jit(solution)/shard_map/ppermute | solution.py:656
  292.9 17.7 %collective-permute-start.10 = (bf16[256,1536]{1,0:T(8,128)(2,1)S(1)}, bf16[256,1536]{1,0:T(8,128)(2,1)S(1)}, u32[]{:S(2)}, u32[]{:S(2)}) collective-permute-start(bf16[256,1536]{1,0:T(8,128)(2,1)S(1)} %slice.127), channel_id=1, source_target_pairs={{0,2},{1,3},{2,0},{3,1},{4,6},{5,7},{6,4},{7,5},{8,10},{9,11},{10,... | collective-permute-start | bytes 2359304 | tf_op jit(solution)/shard_map/ppermute | solution.py:656
  341.7 239.0 %reduce-scatter.8.cloned.1.call-start = ((), (), s32[]{:S(2)}) async-start(), calls=%async_computation.17 | async-start | bytes 2949120 | tf_op jit(solution)/shard_map/reduce_scatter | solution.py:882
  355.8 32.2 %collective-permute-start.12 = (bf16[4,1,192,1536]{3,2,1,0:T(8,128)(2,1)}, bf16[4,1,192,1536]{3,2,1,0:T(8,128)(2,1)S(1)}, u32[]{:S(2)}, u32[]{:S(2)}) collective-permute-start(bf16[4,1,192,1536]{3,2,1,0:T(8,128)(2,1)} %get-tuple-element.179), channel_id=1, source_target_pairs={{0,4},{4,0},{8,12},{12,8},{16,20},{20,16},{24,28},{28,24},{1,5},{5... | collective-permute-start | bytes 7077896 | tf_op jit(solution)/shard_map/ppermute | solution.py:656
  387.6 38.0 %collective-permute-start.13 = (bf16[4,3,192,1536]{3,2,1,0:T(8,128)(2,1)}, bf16[4,3,192,1536]{3,2,1,0:T(8,128)(2,1)}, u32[]{:S(2)}, u32[]{:S(2)}) collective-permute-start(bf16[4,3,192,1536]{3,2,1,0:T(8,128)(2,1)} %get-tuple-element.185), channel_id=1, source_target_pairs={{0,4},{4,0},{8,12},{12,8},{16,20},{20,16},{24,28},{28,24},{1,5},{5... | collective-permute-start | bytes 21233672 | tf_op jit(solution)/shard_map/ppermute | solution.py:656
  393.9 186.8 %reduce-scatter.10.cloned.1.call-start = ((), (), s32[]{:S(2)}) async-start(), calls=%async_computation.18 | async-start | bytes 8847360 | tf_op jit(solution)/shard_map/reduce_scatter | solution.py:882
  437.6 361.7 %reduce-scatter.14.cloned.1.call-start = ((), (), s32[]{:S(2)}) async-start(), calls=%async_computation.20 | async-start | bytes 8847360 | tf_op jit(solution)/shard_map/reduce_scatter | solution.py:882
  440.3 106.7 %collective-permute-start.20 = (bf16[4,3,192,1536]{3,2,1,0:T(8,128)(2,1)}, bf16[4,3,192,1536]{3,2,1,0:T(8,128)(2,1)}, u32[]{:S(2)}, u32[]{:S(2)}) collective-permute-start(bf16[4,3,192,1536]{3,2,1,0:T(8,128)(2,1)} %get-tuple-element.191), channel_id=1, source_target_pairs={{0,4},{4,0},{8,12},{12,8},{16,20},{20,16},{24,28},{28,24},{1,5},{5... | collective-permute-start | bytes 21233672 | tf_op jit(solution)/shard_map/ppermute | solution.py:656
  473.8 22.1 %collective-permute-start.17 = (bf16[256,1664]{1,0:T(8,128)(2,1)}, bf16[256,1664]{1,0:T(8,128)(2,1)}, u32[]{:S(2)}, u32[]{:S(2)}) collective-permute-start(bf16[256,1664]{1,0:T(8,128)(2,1)} %get-tuple-element.330), channel_id=1, source_target_pairs={{0,2},{1,3},{2,0},{3,1},{4,6},{5,7},{6,4},{7,5},{8,10},{9,11},{10,... | collective-permute-start | bytes 2555912 | tf_op jit(solution)/shard_map/ppermute | solution.py:656
  475.3 22.9 %collective-permute-start.15 = (bf16[256,1664]{1,0:T(8,128)(2,1)}, bf16[256,1664]{1,0:T(8,128)(2,1)}, u32[]{:S(2)}, u32[]{:S(2)}) collective-permute-start(bf16[256,1664]{1,0:T(8,128)(2,1)} %get-tuple-element.331), channel_id=1, source_target_pairs={{0,1},{1,0},{2,3},{3,2},{4,5},{5,4},{6,7},{7,6},{8,9},{9,8},{10,11... | collective-permute-start | bytes 2555912 | tf_op jit(solution)/shard_map/ppermute | solution.py:656
  489.6 23.8 %collective-permute-start.19 = (bf16[256,1664]{1,0:T(8,128)(2,1)S(1)}, bf16[256,1664]{1,0:T(8,128)(2,1)S(1)}, u32[]{:S(2)}, u32[]{:S(2)}) collective-permute-start(bf16[256,1664]{1,0:T(8,128)(2,1)S(1)} %slice.166), channel_id=1, source_target_pairs={{0,2},{1,3},{2,0},{3,1},{4,6},{5,7},{6,4},{7,5},{8,10},{9,11},{10,... | collective-permute-start | bytes 2555912 | tf_op jit(solution)/shard_map/ppermute | solution.py:656
  492.0 30.3 %collective-permute-start.14 = (bf16[256,1664]{1,0:T(8,128)(2,1)}, bf16[256,1664]{1,0:T(8,128)(2,1)S(1)}, u32[]{:S(2)}, u32[]{:S(2)}) collective-permute-start(bf16[256,1664]{1,0:T(8,128)(2,1)} %slice.160), channel_id=1, source_target_pairs={{0,1},{1,0},{2,3},{3,2},{4,5},{5,4},{6,7},{7,6},{8,9},{9,8},{10,11... | collective-permute-start | bytes 2555912 | tf_op jit(solution)/shard_map/ppermute | solution.py:656
  495.9 51.0 %collective-permute-start.21 = (bf16[4,2,192,1536]{3,2,1,0:T(8,128)(2,1)}, bf16[4,2,192,1536]{3,2,1,0:T(8,128)(2,1)}, u32[]{:S(2)}, u32[]{:S(2)}) collective-permute-start(bf16[4,2,192,1536]{3,2,1,0:T(8,128)(2,1)} %get-tuple-element.193), channel_id=1, source_target_pairs={{0,4},{4,0},{8,12},{12,8},{16,20},{20,16},{24,28},{28,24},{1,5},{5... | collective-permute-start | bytes 14155784 | tf_op jit(solution)/shard_map/ppermute | solution.py:656
  498.2 34.7 %collective-permute-start.18 = (bf16[256,1664]{1,0:T(8,128)(2,1)}, bf16[256,1664]{1,0:T(8,128)(2,1)}, u32[]{:S(2)}, u32[]{:S(2)}) collective-permute-start(bf16[256,1664]{1,0:T(8,128)(2,1)} %add_convert_fusion.1), channel_id=1, source_target_pairs={{0,1},{1,0},{2,3},{3,2},{4,5},{5,4},{6,7},{7,6},{8,9},{9,8},{10,11... | collective-permute-start | bytes 2555912 | tf_op jit(solution)/shard_map/ppermute | solution.py:656
  513.4 20.6 %collective-permute-start.16 = (bf16[256,1664]{1,0:T(8,128)(2,1)}, bf16[256,1664]{1,0:T(8,128)(2,1)S(1)}, u32[]{:S(2)}, u32[]{:S(2)}) collective-permute-start(bf16[256,1664]{1,0:T(8,128)(2,1)} %add_convert_fusion.2), channel_id=1, source_target_pairs={{0,2},{1,3},{2,0},{3,1},{4,6},{5,7},{6,4},{7,5},{8,10},{9,11},{10,... | collective-permute-start | bytes 2555912 | tf_op jit(solution)/shard_map/ppermute | solution.py:656
  559.1 85.0 %all-to-all-start.4 = ((bf16[8,192,512]{2,1,0:T(8,128)(2,1)}), bf16[8,192,512]{2,1,0:T(8,128)(2,1)}, u32[]{:S(2)}, u32[]{:S(2)}) async-start(bf16[8,192,512]{2,1,0:T(8,128)(2,1)} %bitcast.127), calls=%async_computation.7 | async-start | bytes 3145728 | tf_op jit(solution)/shard_map/all_to_all | solution.py:926
  580.7 45.1 %collective-permute-start.22 = (bf16[8,48,1664]{2,1,0:T(8,128)(2,1)}, bf16[8,48,1664]{2,1,0:T(8,128)(2,1)}, u32[]{:S(2)}, u32[]{:S(2)}) collective-permute-start(bf16[8,48,1664]{2,1,0:T(8,128)(2,1)} %get-tuple-element.219), channel_id=1, source_target_pairs={{0,1},{1,0},{2,3},{3,2},{4,5},{5,4},{6,7},{7,6},{8,9},{9,8},{10,11... | collective-permute-start | bytes 3833864 | tf_op jit(solution)/shard_map/ppermute | solution.py:656
  582.2 56.6 %collective-permute-start.23 = (bf16[8,48,1664]{2,1,0:T(8,128)(2,1)}, bf16[8,48,1664]{2,1,0:T(8,128)(2,1)}, u32[]{:S(2)}, u32[]{:S(2)}) collective-permute-start(bf16[8,48,1664]{2,1,0:T(8,128)(2,1)} %get-tuple-element.220), channel_id=1, source_target_pairs={{0,2},{1,3},{2,0},{3,1},{4,6},{5,7},{6,4},{7,5},{8,10},{9,11},{10,... | collective-permute-start | bytes 3833864 | tf_op jit(solution)/shard_map/ppermute | solution.py:656
  583.6 56.3 %collective-permute-start.24 = (bf16[8,48,1664]{2,1,0:T(8,128)(2,1)}, bf16[8,48,1664]{2,1,0:T(8,128)(2,1)}, u32[]{:S(2)}, u32[]{:S(2)}) collective-permute-start(bf16[8,48,1664]{2,1,0:T(8,128)(2,1)} %get-tuple-element.221), channel_id=1, source_target_pairs={{0,3},{1,2},{2,1},{3,0},{4,7},{5,6},{6,5},{7,4},{8,11},{9,10},{10,... | collective-permute-start | bytes 3833864 | tf_op jit(solution)/shard_map/ppermute | solution.py:656
  644.1 89.6 %all-to-all-start.5 = ((bf16[8,48,1664]{2,1,0:T(8,128)(2,1)}), bf16[8,48,1664]{2,1,0:T(8,128)(2,1)}, u32[]{:S(2)}, u32[]{:S(2)}) async-start(bf16[8,48,1664]{2,1,0:T(8,128)(2,1)} %add_convert_fusion), calls=%async_computation.8 | async-start | bytes 2555904 | tf_op jit(solution)/shard_map/all_to_all | solution.py:941
  733.7 65.5 %all-to-all-start.6 = ((bf16[8,320,512]{2,1,0:T(8,128)(2,1)}), bf16[8,320,512]{2,1,0:T(8,128)(2,1)}, u32[]{:S(2)}, u32[]{:S(2)}) async-start(bf16[8,320,512]{2,1,0:T(8,128)(2,1)} %attend_back.1.back_ref), calls=%async_computation.9 | async-start | bytes 5242880 | tf_op jit(solution)/shard_map/all_to_all | solution.py:947
  738.8 149.5 %reduce-scatter.12.cloned.1.call-start = ((), (), s32[]{:S(2)}) async-start(), calls=%async_computation.19 | async-start | bytes 5898240 | tf_op jit(solution)/shard_map/reduce_scatter | solution.py:882
  754.8 15.5 %collective-permute-start.27 = (bf16[8,48,320]{2,1,0:T(8,128)(2,1)S(1)}, bf16[8,48,320]{2,1,0:T(8,128)(2,1)S(1)}, u32[]{:S(2)}, u32[]{:S(2)}) collective-permute-start(bf16[8,48,320]{2,1,0:T(8,128)(2,1)S(1)} %get-tuple-element.337), channel_id=1, source_target_pairs={{0,3},{1,2},{2,1},{3,0},{4,7},{5,6},{6,5},{7,4},{8,11},{9,10},{10,... | collective-permute-start | bytes 737288 | tf_op jit(solution)/shard_map/ppermute | solution.py:656
  756.6 15.1 %collective-permute-start.26 = (bf16[8,48,320]{2,1,0:T(8,128)(2,1)S(1)}, bf16[8,48,320]{2,1,0:T(8,128)(2,1)S(1)}, u32[]{:S(2)}, u32[]{:S(2)}) collective-permute-start(bf16[8,48,320]{2,1,0:T(8,128)(2,1)S(1)} %get-tuple-element.338), channel_id=1, source_target_pairs={{0,2},{1,3},{2,0},{3,1},{4,6},{5,7},{6,4},{7,5},{8,10},{9,11},{10,... | collective-permute-start | bytes 737288 | tf_op jit(solution)/shard_map/ppermute | solution.py:656
  803.0 23.8 %all-to-all-start.7 = ((bf16[8,48,320]{2,1,0:T(8,128)(2,1)}), bf16[8,48,320]{2,1,0:T(8,128)(2,1)S(1)}, u32[]{:S(2)}, u32[]{:S(2)}) async-start(bf16[8,48,320]{2,1,0:T(8,128)(2,1)} %fusion.16), calls=%async_computation.10 | async-start | bytes 589824 | tf_op jit(solution)/shard_map/all_to_all | solution.py:963
  809.4 22.3 %collective-permute-start.29 = (bf16[256,1536]{1,0:T(8,128)(2,1)}, bf16[256,1536]{1,0:T(8,128)(2,1)}, u32[]{:S(2)}, u32[]{:S(2)}) collective-permute-start(bf16[256,1536]{1,0:T(8,128)(2,1)} %get-tuple-element.334), channel_id=1, source_target_pairs={{0,1},{1,0},{2,3},{3,2},{4,5},{5,4},{6,7},{7,6},{8,9},{9,8},{10,11... | collective-permute-start | bytes 2359304 | tf_op jit(solution)/shard_map/ppermute | solution.py:656
  810.6 24.7 %collective-permute-start.31 = (bf16[256,1536]{1,0:T(8,128)(2,1)}, bf16[256,1536]{1,0:T(8,128)(2,1)}, u32[]{:S(2)}, u32[]{:S(2)}) collective-permute-start(bf16[256,1536]{1,0:T(8,128)(2,1)} %get-tuple-element.335), channel_id=1, source_target_pairs={{0,2},{1,3},{2,0},{3,1},{4,6},{5,7},{6,4},{7,5},{8,10},{9,11},{10,... | collective-permute-start | bytes 2359304 | tf_op jit(solution)/shard_map/ppermute | solution.py:656
  824.5 53.9 %collective-permute-start.33 = (bf16[256,1536]{1,0:T(8,128)(2,1)}, bf16[256,1536]{1,0:T(8,128)(2,1)}, u32[]{:S(2)}, u32[]{:S(2)}) collective-permute-start(bf16[256,1536]{1,0:T(8,128)(2,1)} %slice.146), channel_id=1, source_target_pairs={{0,2},{1,3},{2,0},{3,1},{4,6},{5,7},{6,4},{7,5},{8,10},{9,11},{10,... | collective-permute-start | bytes 2359304 | tf_op jit(solution)/shard_map/ppermute | solution.py:656
  825.4 53.0 %collective-permute-start.28 = (bf16[256,1536]{1,0:T(8,128)(2,1)}, bf16[256,1536]{1,0:T(8,128)(2,1)}, u32[]{:S(2)}, u32[]{:S(2)}) collective-permute-start(bf16[256,1536]{1,0:T(8,128)(2,1)} %slice.140), channel_id=1, source_target_pairs={{0,1},{1,0},{2,3},{3,2},{4,5},{5,4},{6,7},{7,6},{8,9},{9,8},{10,11... | collective-permute-start | bytes 2359304 | tf_op jit(solution)/shard_map/ppermute | solution.py:656
  830.0 26.4 %collective-permute-start.36 = (bf16[48,4224]{1,0:T(8,128)(2,1)}, bf16[48,4224]{1,0:T(8,128)(2,1)S(1)}, u32[]{:S(2)}, u32[]{:S(2)}) collective-permute-start(bf16[48,4224]{1,0:T(8,128)(2,1)} %gather_parts.1.refs_0_), channel_id=1, source_target_pairs={{0,3},{1,2},{2,1},{3,0},{4,7},{5,6},{6,5},{7,4},{8,11},{9,10},{10,... | collective-permute-start | bytes 1216520 | tf_op jit(solution)/shard_map/ppermute | solution.py:656
  831.7 33.6 %collective-permute-start.35 = (bf16[48,4224]{1,0:T(8,128)(2,1)}, bf16[48,4224]{1,0:T(8,128)(2,1)S(1)}, u32[]{:S(2)}, u32[]{:S(2)}) collective-permute-start(bf16[48,4224]{1,0:T(8,128)(2,1)} %gather_parts.1.refs_0_), channel_id=1, source_target_pairs={{0,2},{1,3},{2,0},{3,1},{4,6},{5,7},{6,4},{7,5},{8,10},{9,11},{10,... | collective-permute-start | bytes 1216520 | tf_op jit(solution)/shard_map/ppermute | solution.py:656
  835.2 34.9 %collective-permute-start.34 = (bf16[48,4224]{1,0:T(8,128)(2,1)}, bf16[48,4224]{1,0:T(8,128)(2,1)S(1)}, u32[]{:S(2)}, u32[]{:S(2)}) collective-permute-start(bf16[48,4224]{1,0:T(8,128)(2,1)} %gather_parts.1.refs_0_), channel_id=1, source_target_pairs={{0,1},{1,0},{2,3},{3,2},{4,5},{5,4},{6,7},{7,6},{8,9},{9,8},{10,11... | collective-permute-start | bytes 1216520 | tf_op jit(solution)/shard_map/ppermute | solution.py:656
  856.4 25.1 %collective-permute-start.30 = (bf16[256,1536]{1,0:T(8,128)(2,1)}, bf16[256,1536]{1,0:T(8,128)(2,1)}, u32[]{:S(2)}, u32[]{:S(2)}) collective-permute-start(bf16[256,1536]{1,0:T(8,128)(2,1)} %add_convert_fusion.4), channel_id=1, source_target_pairs={{0,2},{1,3},{2,0},{3,1},{4,6},{5,7},{6,4},{7,5},{8,10},{9,11},{10,... | collective-permute-start | bytes 2359304 | tf_op jit(solution)/shard_map/ppermute | solution.py:656
  865.4 18.4 %collective-permute-start.32 = (bf16[256,1536]{1,0:T(8,128)(2,1)}, bf16[256,1536]{1,0:T(8,128)(2,1)}, u32[]{:S(2)}, u32[]{:S(2)}) collective-permute-start(bf16[256,1536]{1,0:T(8,128)(2,1)} %add_convert_fusion.3), channel_id=1, source_target_pairs={{0,1},{1,0},{2,3},{3,2},{4,5},{5,4},{6,7},{7,6},{8,9},{9,8},{10,11... | collective-permute-start | bytes 2359304 | tf_op jit(solution)/shard_map/ppermute | solution.py:656
  (54 other events, 729.0 us)
Sparse Core Ops, SparseCore 0:
  10.2 99.6 all-gather.5
  112.1 36.6 all-gather.7
  156.9 50.1 all-gather.9
  249.7 76.5 all-gather.11
  341.8 46.8 reduce-scatter.5
  394.1 46.8 reduce-scatter.7
  443.3 122.9 reduce-scatter.9
  568.6 162.1 reduce-scatter.13
  799.4 88.1 reduce-scatter.11

commit v3 on v2

--- a/solution.py
+++ b/solution.py
@@ -21,6 +21,7 @@
 EPS = 1e-05
 NEG = -1e30
 THETA = 10000.0
+LOG2_E = 1.4426950408889634
 
 F32 = jnp.float32
 BF16 = jnp.bfloat16
@@ -49,14 +50,14 @@
     n_ref[0] = normed
     raw = contract(w_ref[...], normed, 1, 1)
     cosine, sine = table_ref[0, :half], table_ref[0, half:]
-    scale = HEAD_SIZE**-0.5
+    scale = HEAD_SIZE**-0.5 * LOG2_E
     for g in range(GROUP + 1):
         a, b = raw[g * HEAD_SIZE : g * HEAD_SIZE + half], raw[g * HEAD_SIZE + half : (g + 1) * HEAD_SIZE]
-        turned = jnp.concatenate([a * cosine - b * sine, b * cosine + a * sine], axis=0).astype(BF16)
+        turned = jnp.concatenate([a * cosine - b * sine, b * cosine + a * sine], axis=0)
         if g < GROUP:
-            q_ref[0, g * HEAD_SIZE : (g + 1) * HEAD_SIZE, :] = turned * BF16(scale)
+            q_ref[0, g * HEAD_SIZE : (g + 1) * HEAD_SIZE, :] = (turned * scale).astype(BF16)
         else:
-            kv_ref[0, :HEAD_SIZE, :] = turned
+            kv_ref[0, :HEAD_SIZE, :] = turned.astype(BF16)
     kv_ref[0, HEAD_SIZE:, :] = raw[QROWS + HEAD_SIZE :].astype(BF16)
 
 
@@ -130,6 +131,13 @@
     return (low + 1) // bk, (high + bk) // bk
 
 
+def tile_parts(bk, bq, sub, span, masked):
+    if masked and bk == bq == sub == span:
+        half = bk // 2
+        return [(0, half, slice(0, bq)), (half, half, slice(half, bq))]
+    return [(0, bk, slice(0, bq))]
+
+
 def loop(first, last, step):
     def body(j, carry):
         step(j)
@@ -167,15 +175,15 @@
         total[...] = jnp.zeros(total.shape, F32)
         acc[...] = jnp.zeros(acc.shape, F32)
 
-    def step(j, masked, moving):
-        start = pl.multiple_of(j * bk, bk)
-        k = keys[pl.ds(start, bk), :]
-        v = values[:, pl.ds(start, bk)]
+    def part_step(start, rows, cols, masked, moving):
+        k = keys[pl.ds(start, rows), :]
+        v = values[:, pl.ds(start, rows)]
         if masked:
-            allowed = (start + lax.broadcasted_iota(jnp.int32, (bk, bq), 0)) <= pos_ref[...]
+            shape = (rows, cols.stop - cols.start)
+            allowed = (start + lax.broadcasted_iota(jnp.int32, shape, 0)) <= pos_ref[:, cols]
 
         def score(g):
-            scores = jnp.dot(k, q[g], preferred_element_type=F32)
+            scores = jnp.dot(k, q[g, :, cols], preferred_element_type=F32)
             return jnp.where(allowed, scores, NEG) if masked else scores
 
         ahead = score(0)
@@ -183,20 +191,24 @@
             scores = ahead
             if g + 1 < groups:
                 ahead = score(g + 1)
-            old = peak[g]
+            old = peak[g, :, cols]
             most = jnp.max(scores, axis=0, keepdims=True)
             if moving:
                 new = jnp.maximum(old, most)
-                factor = jnp.exp(old - new)
-                peak[g] = new
-                total[g] = total[g] * factor
-                acc[g] = acc[g] * factor
+                factor = jnp.exp2(old - new)
+                peak[g, :, cols] = new
+                total[g, :, cols] = total[g, :, cols] * factor
+                acc[g, :, cols] = acc[g, :, cols] * factor
             else:
                 new = old
-                highest[g] = jnp.maximum(highest[g], most)
-            weights = jnp.exp(scores - new)
-            total[g] += jnp.sum(weights, axis=0, keepdims=True)
-            acc[g] += jnp.dot(v, weights.astype(BF16), preferred_element_type=F32)
+                highest[g, :, cols] = jnp.maximum(highest[g, :, cols], most)
+            weights = jnp.exp2(scores - new)
+            total[g, :, cols] += jnp.sum(weights, axis=0, keepdims=True)
+            acc[g, :, cols] += jnp.dot(v, weights.astype(BF16), preferred_element_type=F32)
+
+    def step(j, masked, moving):
+        for first, rows, cols in tile_parts(bk, bq, sub, span, masked):
+            part_step(pl.multiple_of(j * bk + first, rows), rows, cols, masked, moving)
 
     reset()
     loop(unmasked, ends, lambda j: step(j, True, True))
@@ -211,7 +223,7 @@
 
     for g in range(groups):
         out = (acc[g] / total[g]).astype(BF16)
-        lse_ref[g] = peak[g] + jnp.log(total[g])
+        lse_ref[g] = peak[g] + jnp.log2(total[g])
         for i in range(o_ref.shape[0]):
             o_ref[i, g * size : (g + 1) * size, :] = out[:, i * o_ref.shape[2] : (i + 1) * o_ref.shape[2]]
 
@@ -299,7 +311,7 @@
         dk_part = jnp.zeros((bk, size), F32)
         for g in range(groups):
             scores = jnp.dot(k, q[g], preferred_element_type=F32)
-            prob = jnp.exp(scores - lse_ref[g])
+            prob = jnp.exp2(scores - lse_ref[g])
             if masked:
                 prob = jnp.where(allowed, prob, 0.0)
             dv_part = dv_part + jnp.dot(prob.astype(BF16), do_rows[g], preferred_element_type=F32)
@@ -326,7 +338,7 @@
         for i in range(dkv_ref.shape[0]):
             part = slice(i * span, (i + 1) * span)
             back = turn_back(jnp.transpose(dk[part, :], (1, 0)), ktab_ref[i, :half], ktab_ref[i, half:])
-            dkv_ref[i, base : base + size, :] = back.astype(BF16)
+            dkv_ref[i, base : base + size, :] = (back * (1.0 / LOG2_E)).astype(BF16)
             dkv_ref[i, base + size : base + 2 * size, :] = jnp.transpose(dv[part, :], (1, 0)).astype(BF16)
 
 

time: 910 us -> 907 us (level)
  transfers between devices with their start and end apart: 54 -> 54, of which waited for: 28 -> 28; matrix products, arithmetic and copies ran while one was open for 11% -> 11% of each run, Pallas kernels for 48% -> 47%
where the time goes in v3:
time: 907 us; the launch traced here: 895 us
  Pallas kernels  433 us (48%)
  waiting for transfers between devices  257 us (28%)
  starting transfers between devices  75.3 us (8%)
  local copies, waits for them, and re-layouts  46.4 us (5%)
  other arithmetic  43.7 us (5%)
  matrix products  24.6 us (3%)
  between operations  14.8 us (2%)
    pallas_call x5, Pallas kernels, run_experts(): pl.pallas_call(functools.partial(experts_kernel, span, cap, offset, block...  115 us
    ppermute x37, waiting for transfers between devices, swapped(): return lax.ppermute(array, axis, [(i, i ^ mask) for i in range(count)])  109 us
    pallas_call x1, Pallas kernels, attend_back(): pl.pallas_call(functools.partial(attend_back_kernel, bk, sub, span), grid...  84 us
    all_gather x2, waiting for transfers between devices, per_device(): lax.all_gather(part_in, 'ctx', axis=0, tiled=False)  56.8 us
    pallas_call x8, Pallas kernels, combine(): pl.pallas_call(functools.partial(combine_kernel, cap, len(ranks)), grid=(...  53.2 us
    pallas_call x5, Pallas kernels, add(): pl.pallas_call(add_kernel, grid=(pairs, count), in_specs=[block, block],...  41.3 us
    ppermute x37, starting transfers between devices, swapped(): return lax.ppermute(array, axis, [(i, i ^ mask) for i in range(count)])  40.6 us
    pallas_call x8, Pallas kernels, dispatch(): pl.pallas_call(functools.partial(dispatch_kernel, cap), grid=(width // wi...  39.5 us
  transfers between devices with their start and end apart: 54, of which 28 were waited for; matrix products, arithmetic and copies ran while one was open for 11% of the time, Pallas kernels for 47%

profile of v3, /device:TPU:0, one launch (start us, length us, event | category | flops | bytes accessed | tf_op | source)
XLA Modules:
  0.0 895.1 jit_solution(10368631383419017206)
XLA Ops:
  18.6 4.9 all-to-all-start
  24.4 17.3 %all-to-all-done = bf16[8,48,384]{2,1,0:T(8,128)(2,1)S(1)} async-done(((bf16[8,48,384]{2,1,0:T(8,128)(2,1)}), bf16[8,48,384]{2,1,0:T(8,128)(2,1)S(1)}, u32[]{:S(2)}, u32[]{:S(2)}) %all-to-all-start) | async-done | bytes 294944 | tf_op jit(solution)/shard_map/all_to_all | solution.py:814
  57.1 5.5 collective-permute-done.3
  65.1 44.8 %all-gather.6.cloned.1.call-done.x_ref = bf16[8,384,1536]{2,1,0:T(8,128)(2,1)} async-done(((bf16[1,384,1536]{2,1,0:T(8,128)(2,1)}), bf16[8,384,1536]{2,1,0:T(8,128)(2,1)}) %all-gather.6.cloned.1.call-update) | async-done | bytes 9437200 | tf_op jit(solution)/shard_map/all_gather | solution.py:836
  120.8 11.6 %project.2 = (bf16[8,512,1536]{2,1,0:T(8,128)(2,1)}, bf16[8,192,512]{2,1,0:T(8,128)(2,1)}, bf16[8,128,512]{2,1,0:T(8,128)(2,1)}) custom-call(bf16[8,384,1536]{2,1,0:T(8,128)(2,1)} %all-gather.6.cloned.1.call-done.x_ref, f32[1,1536]{1,0:T(1,128)} %reshape.225.gain_ref, bf16[320,1536]{1,0:T(8,128)(2,1)} %bitcast.111, ...), custom_call_target="tpu_custom_call" | custom-call | flops 1024 | bytes 1024 | tf_op jit(solution)/shard_map/project/pallas_call | solution.py:68
  136.8 12.0 %all-gather.8.cloned.1.call-done.x_ref = bf16[8,128,1536]{2,1,0:T(8,128)(2,1)} async-done(((bf16[1,128,1536]{2,1,0:T(8,128)(2,1)}), bf16[8,128,1536]{2,1,0:T(8,128)(2,1)}) %all-gather.8.cloned.1.call-update) | async-done | bytes 3145744 | tf_op jit(solution)/shard_map/all_gather | solution.py:836
  148.8 8.0 project.3
  157.4 38.3 %attend.1 = (bf16[8,192,512]{2,1,0:T(8,128)(2,1)}, f32[3,1,4096]{2,1,0:T(1,128)}) custom-call(s32[1]{0:T(128)} %constant.101.clone.1.part_ref, s32[1,4096]{1,0:T(1,128)} %iota.44.pos_ref, bf16[8,192,512]{2,1,0:T(8,128)(2,1)} %get-tuple-element.147.q_ref, bf16[8,128,512]{2,1,0:T(8,128)(2,1)} %get-tuple-element.148.kv_ref), custom_call_target="tpu_custom_call" | custom-call | flops 1024 | bytes 1024 | tf_op jit(solution)/shard_map/attend/pallas_call | solution.py:237
  201.2 4.9 dispatch.8.refs_4_
  210.9 4.9 dispatch.10.refs_6_
  215.9 4.9 dispatch.9.refs_5_
  220.8 19.0 %all-to-all-done.2 = bf16[8,192,512]{2,1,0:T(8,128)(2,1)} async-done(((bf16[8,192,512]{2,1,0:T(8,128)(2,1)}), bf16[8,192,512]{2,1,0:T(8,128)(2,1)}, u32[]{:S(2)}, u32[]{:S(2)}) %all-to-all-start.2) | async-done | bytes 1572896 | tf_op jit(solution)/shard_map/all_to_all | solution.py:865
  239.8 5.3 multiply_reduce_fusion.2
  260.5 25.6 %all-to-all-done.3 = f32[4,10,512]{2,1,0:T(8,128)S(1)} async-done(((f32[4,10,512]{2,1,0:T(8,128)}), f32[4,10,512]{2,1,0:T(8,128)S(1)}, u32[]{:S(2)}, u32[]{:S(2)}) %all-to-all-start.3) | async-done | bytes 81952 | tf_op jit(solution)/shard_map/all_to_all | solution.py:828
  292.9 5.0 dispatch.14.refs_2_
  302.7 5.1 collective-permute-done.9
  310.2 5.2 dispatch.15.refs_3_
  315.5 14.0 %experts.5 = (bf16[1,512,1664]{2,1,0:T(8,128)(2,1)}, bf16[1,512,1536]{2,1,0:T(8,128)(2,1)}, bf16[4,1,192,1536]{3,2,1,0:T(8,128)(2,1)}, bf16[4,1,192,1536]{3,2,1,0:T(8,128)(2,1)}) custom-call(s32[2]{0:T(128)} %pad_add_fusion.place_ref, s32[10,1,2048]{2,1,0:T(1,128)} %copy_convert_fusion.rank_ref, f32[10,1,2048]{2,1,0:T(1,128)} %broadcast_in_dim.74.prob_ref, ...), custom_call_target="tpu_custom_call" | custom-call | flops 7247757312 | bytes 6291456 | tf_op jit(solution)/shard_map/experts/pallas_call | solution.py:477
  340.4 13.9 %experts.6 = (bf16[1,512,1664]{2,1,0:T(8,128)(2,1)}, bf16[1,512,1536]{2,1,0:T(8,128)(2,1)}, bf16[4,1,192,1536]{3,2,1,0:T(8,128)(2,1)}, bf16[4,1,192,1536]{3,2,1,0:T(8,128)(2,1)}) custom-call(s32[2]{0:T(128)} %pad_add_fusion.place_ref, s32[10,1,2048]{2,1,0:T(1,128)} %copy_convert_fusion.rank_ref, f32[10,1,2048]{2,1,0:T(1,128)} %broadcast_in_dim.74.prob_ref, ...), custom_call_target="tpu_custom_call" | custom-call | flops 7247757312 | bytes 6291456 | tf_op jit(solution)/shard_map/experts/pallas_call | solution.py:477
  354.4 31.6 %experts.7 = (bf16[3,512,1664]{2,1,0:T(8,128)(2,1)}, bf16[3,512,1536]{2,1,0:T(8,128)(2,1)}, bf16[4,3,192,1536]{3,2,1,0:T(8,128)(2,1)}, bf16[4,3,192,1536]{3,2,1,0:T(8,128)(2,1)}) custom-call(s32[2]{0:T(128)} %pad_add_fusion.place_ref, s32[10,1,2048]{2,1,0:T(1,128)} %copy_convert_fusion.rank_ref, f32[10,1,2048]{2,1,0:T(1,128)} %broadcast_in_dim.74.prob_ref, ...), custom_call_target="tpu_custom_call" | custom-call | flops 21743271936 | bytes 18874368 | tf_op jit(solution)/shard_map/experts/pallas_call | solution.py:477
  392.5 31.6 %experts.8 = (bf16[3,512,1664]{2,1,0:T(8,128)(2,1)}, bf16[3,512,1536]{2,1,0:T(8,128)(2,1)}, bf16[4,3,192,1536]{3,2,1,0:T(8,128)(2,1)}, bf16[4,3,192,1536]{3,2,1,0:T(8,128)(2,1)}) custom-call(s32[2]{0:T(128)} %pad_add_fusion.place_ref, s32[10,1,2048]{2,1,0:T(1,128)} %copy_convert_fusion.rank_ref, f32[10,1,2048]{2,1,0:T(1,128)} %broadcast_in_dim.74.prob_ref, ...), custom_call_target="tpu_custom_call" | custom-call | flops 21743271936 | bytes 18874368 | tf_op jit(solution)/shard_map/experts/pallas_call | solution.py:477
  424.1 12.1 %add.261 = bf16[4,3,192,1536]{3,2,1,0:T(8,128)(2,1)} custom-call(bf16[4,3,192,1536]{3,2,1,0:T(8,128)(2,1)} %get-tuple-element.186.left_ref, bf16[4,3,192,1536]{3,2,1,0:T(8,128)(2,1)} %collective-permute-done.13.right_ref), custom_call_target="tpu_custom_call" | custom-call | flops 1024 | bytes 1024 | tf_op jit(solution)/shard_map/add/pallas_call | solution.py:506
  439.0 23.7 %experts.9 = (bf16[2,512,1664]{2,1,0:T(8,128)(2,1)}, bf16[2,512,1536]{2,1,0:T(8,128)(2,1)}, bf16[4,2,192,1536]{3,2,1,0:T(8,128)(2,1)}, bf16[4,2,192,1536]{3,2,1,0:T(8,128)(2,1)}) custom-call(s32[2]{0:T(128)} %pad_add_fusion.place_ref, s32[10,1,2048]{2,1,0:T(1,128)} %copy_convert_fusion.rank_ref, f32[10,1,2048]{2,1,0:T(1,128)} %broadcast_in_dim.74.prob_ref, ...), custom_call_target="tpu_custom_call" | custom-call | flops 14495514624 | bytes 12582912 | tf_op jit(solution)/shard_map/experts/pallas_call | solution.py:477
  462.7 6.8 combine.11
  474.0 6.8 combine.10
  480.8 7.0 combine.9
  499.4 12.5 %collective-permute-done.19 = bf16[256,1664]{1,0:T(8,128)(2,1)S(1)} collective-permute-done((bf16[256,1664]{1,0:T(8,128)(2,1)S(1)}, bf16[256,1664]{1,0:T(8,128)(2,1)S(1)}, u32[]{:S(2)}, u32[]{:S(2)}) %collective-permute-start.19) | collective-permute-done | bytes 852000 | tf_op jit(solution)/shard_map/ppermute | solution.py:668
  513.4 7.3 combine.8
  520.7 10.8 %collective-permute-done.18 = bf16[256,1664]{1,0:T(8,128)(2,1)} collective-permute-done((bf16[256,1664]{1,0:T(8,128)(2,1)}, bf16[256,1664]{1,0:T(8,128)(2,1)}, u32[]{:S(2)}, u32[]{:S(2)}) %collective-permute-start.18) | collective-permute-done | bytes 852000 | tf_op jit(solution)/shard_map/ppermute | solution.py:668
  545.5 12.0 %add.263 = bf16[4,3,192,1536]{3,2,1,0:T(8,128)(2,1)} custom-call(bf16[4,3,192,1536]{3,2,1,0:T(8,128)(2,1)} %get-tuple-element.249.left_ref, bf16[4,3,192,1536]{3,2,1,0:T(8,128)(2,1)} %collective-permute-done.20.right_ref), custom_call_target="tpu_custom_call" | custom-call | flops 1024 | bytes 1024 | tf_op jit(solution)/shard_map/add/pallas_call | solution.py:506
  565.0 8.7 outer.1
  573.6 5.0 dynamic-slice_bitcast_fusion
  582.2 6.3 combine.15
  588.5 6.3 combine.14
  594.9 6.3 combine.13
  601.2 6.3 combine.12
  609.7 8.3 add.262
  623.8 12.6 %collective-permute-done.23 = bf16[8,48,1664]{2,1,0:T(8,128)(2,1)} collective-permute-done((bf16[8,48,1664]{2,1,0:T(8,128)(2,1)}, bf16[8,48,1664]{2,1,0:T(8,128)(2,1)}, u32[]{:S(2)}, u32[]{:S(2)}) %collective-permute-start.23) | collective-permute-done | bytes 1277984 | tf_op jit(solution)/shard_map/ppermute | solution.py:668
  641.9 4.9 all-to-all-start.5
  647.5 84.0 %attend_back.1.back_ref = bf16[8,320,512]{2,1,0:T(8,128)(2,1)} custom-call(s32[1]{0:T(128)} %constant.101.clone.1.part_ref, s32[1,4096]{1,0:T(1,128)} %iota.49.pos_ref, bf16[8,192,512]{2,1,0:T(8,128)(2,1)} %get-tuple-element.147.q_ref, bf16[8,192,512]{2,1,0:T(8,128)(2,1)} %get-tuple-element.149.o_ref, bf16[8,192,512]{2,1,0:T(8,128)(2,1)} %all-to-all-done.4.do_ref, ...), custom_call_target="tpu_custom_call" | custom-call | flops 1024 | bytes 1024 | tf_op jit(solution)/shard_map/attend_back/pallas_call | solution.py:359
  731.5 5.1 all-to-all-start.6
  736.6 13.5 %head_grads.1 = bf16[1536,320]{1,0:T(8,128)(2,1)} custom-call(bf16[8,320,512]{2,1,0:T(8,128)(2,1)} %attend_back.1.back_ref, bf16[8,512,1536]{2,1,0:T(8,128)(2,1)} %get-tuple-element.229.n_ref), custom_call_target="tpu_custom_call" | custom-call | flops 1024 | bytes 1024 | tf_op jit(solution)/shard_map/head_grads/pallas_call | solution.py:111
  754.9 6.3 collective-permute-done.25
  761.2 6.5 collective-permute-done.27
  770.9 26.2 %all-to-all-done.6 = bf16[8,320,512]{2,1,0:T(8,128)(2,1)} async-done(((bf16[8,320,512]{2,1,0:T(8,128)(2,1)}), bf16[8,320,512]{2,1,0:T(8,128)(2,1)}, u32[]{:S(2)}, u32[]{:S(2)}) %all-to-all-start.6) | async-done | bytes 2621472 | tf_op jit(solution)/shard_map/all_to_all | solution.py:959
  809.5 10.3 %fusion.2 = (f32[512]{0:T(512)S(1)}, f32[512]{0:T(512)S(1)}, f32[512,1536]{1,0:T(8,128)}) fusion(bf16[1,512,1536]{2,1,0:T(8,128)(2,1)S(1)} %copy-done.11, f32[1536]{0:T(1024)S(1)} %copy-done.33, bf16[2560,512]{1,0:T(8,128)(2,1)} %bitcast.36, bf16[2560,1536]{1,0:T(8,128)(2,1)} %all-gather.12.cloned.1.call-done), kind=kOutput, calls=%fused_computation.11 | convolution fusion | flops 4031249408 | bytes 15214592 | tf_op jit(solution)/shard_map/dot_general | solution.py:33
  836.5 17.8 %collective-permute-done.36.refs_3_ = bf16[48,4224]{1,0:T(8,128)(2,1)S(1)} collective-permute-done((bf16[48,4224]{1,0:T(8,128)(2,1)}, bf16[48,4224]{1,0:T(8,128)(2,1)S(1)}, u32[]{:S(2)}, u32[]{:S(2)}) %collective-permute-start.36) | collective-permute-done | bytes 405536 | tf_op jit(solution)/shard_map/ppermute | solution.py:668
  854.9 8.0 collective-permute-done.35.refs_2_
  (295 shorter events, 225.6 us)
Async XLA Ops:
  7.2 102.7 %all-gather.6.cloned.1.call-start = ((), (), s32[]{:S(2)}) async-start(), calls=%async_computation.13 | async-start | bytes 10616832 | tf_op jit(solution)/shard_map/all_gather | solution.py:836
  9.7 139.1 %all-gather.8.cloned.1.call-start = ((), (), s32[]{:S(2)}) async-start(), calls=%async_computation.14 | async-start | bytes 3538944 | tf_op jit(solution)/shard_map/all_gather | solution.py:836
  10.6 54.5 %collective-permute-start.1 = (bf16[512,1536]{1,0:T(8,128)(2,1)}, bf16[512,1536]{1,0:T(8,128)(2,1)}, u32[]{:S(2)}, u32[]{:S(2)}) collective-permute-start(bf16[512,1536]{1,0:T(8,128)(2,1)} %bitcast.120), channel_id=1, source_target_pairs={{0,2},{1,3},{2,0},{3,1},{4,6},{5,7},{6,4},{7,5},{8,10},{9,11},{10,... | collective-permute-start | bytes 4718600 | tf_op jit(solution)/shard_map/ppermute | solution.py:668
  13.6 51.5 %collective-permute-start = (bf16[512,1536]{1,0:T(8,128)(2,1)}, bf16[512,1536]{1,0:T(8,128)(2,1)}, u32[]{:S(2)}, u32[]{:S(2)}) collective-permute-start(bf16[512,1536]{1,0:T(8,128)(2,1)} %bitcast.121), channel_id=1, source_target_pairs={{0,1},{1,0},{2,3},{3,2},{4,5},{5,4},{6,7},{7,6},{8,9},{9,8},{10,11... | collective-permute-start | bytes 4718600 | tf_op jit(solution)/shard_map/ppermute | solution.py:668
  18.6 23.2 %all-to-all-start = ((bf16[8,48,384]{2,1,0:T(8,128)(2,1)}), bf16[8,48,384]{2,1,0:T(8,128)(2,1)S(1)}, u32[]{:S(2)}, u32[]{:S(2)}) async-start(bf16[8,48,384]{2,1,0:T(8,128)(2,1)} %copy.93), calls=%async_computation | async-start | bytes 589824 | tf_op jit(solution)/shard_map/all_to_all | solution.py:814
  45.2 194.5 %all-gather.10.cloned.1.call-start = ((), (), s32[]{:S(2)}) async-start(), calls=%async_computation.15 | async-start | bytes 5308416 | tf_op jit(solution)/shard_map/all_gather | solution.py:859
  113.2 20.0 %collective-permute-start.5 = (bf16[256,1536]{1,0:T(8,128)(2,1)}, bf16[256,1536]{1,0:T(8,128)(2,1)}, u32[]{:S(2)}, u32[]{:S(2)}) collective-permute-start(bf16[256,1536]{1,0:T(8,128)(2,1)} %slice.116), channel_id=1, source_target_pairs={{0,1},{1,0},{2,3},{3,2},{4,5},{5,4},{6,7},{7,6},{8,9},{9,8},{10,11... | collective-permute-start | bytes 2359304 | tf_op jit(solution)/shard_map/ppermute | solution.py:668
  114.7 19.5 %collective-permute-start.6 = (bf16[256,1536]{1,0:T(8,128)(2,1)S(1)}, bf16[256,1536]{1,0:T(8,128)(2,1)}, u32[]{:S(2)}, u32[]{:S(2)}) collective-permute-start(bf16[256,1536]{1,0:T(8,128)(2,1)S(1)} %slice.117), channel_id=1, source_target_pairs={{0,2},{1,3},{2,0},{3,1},{4,6},{5,7},{6,4},{7,5},{8,10},{9,11},{10,... | collective-permute-start | bytes 2359304 | tf_op jit(solution)/shard_map/ppermute | solution.py:668
  195.7 44.0 %all-to-all-start.2 = ((bf16[8,192,512]{2,1,0:T(8,128)(2,1)}), bf16[8,192,512]{2,1,0:T(8,128)(2,1)}, u32[]{:S(2)}, u32[]{:S(2)}) async-start(bf16[8,192,512]{2,1,0:T(8,128)(2,1)} %get-tuple-element.149.o_ref), calls=%async_computation.2 | async-start | bytes 3145728 | tf_op jit(solution)/shard_map/all_to_all | solution.py:865
  200.2 140.2 %all-gather.12.cloned.1.call-start = ((), (), s32[]{:S(2)}) async-start(), calls=%async_computation.21 | async-start | bytes 8847360 | tf_op jit(solution)/shard_map/all_gather | solution.py:874
  247.0 39.8 %collective-permute-start.8 = (bf16[512,1536]{1,0:T(8,128)(2,1)S(1)}, bf16[512,1536]{1,0:T(8,128)(2,1)}, u32[]{:S(2)}, u32[]{:S(2)}) collective-permute-start(bf16[512,1536]{1,0:T(8,128)(2,1)S(1)} %multiply_convert_fusion.token_ref), channel_id=1, source_target_pairs={{0,2},{1,3},{2,0},{3,1},{4,6},{5,7},{6,4},{7,5},{8,10},{9,11},{10,... | collective-permute-start | bytes 4718600 | tf_op jit(solution)/shard_map/ppermute | solution.py:668
  248.6 38.3 %collective-permute-start.7 = (bf16[512,1536]{1,0:T(8,128)(2,1)S(1)}, bf16[512,1536]{1,0:T(8,128)(2,1)}, u32[]{:S(2)}, u32[]{:S(2)}) collective-permute-start(bf16[512,1536]{1,0:T(8,128)(2,1)S(1)} %multiply_convert_fusion.token_ref), channel_id=1, source_target_pairs={{0,1},{1,0},{2,3},{3,2},{4,5},{5,4},{6,7},{7,6},{8,9},{9,8},{10,11... | collective-permute-start | bytes 4718600 | tf_op jit(solution)/shard_map/ppermute | solution.py:668
  252.3 33.9 %all-to-all-start.3 = ((f32[4,10,512]{2,1,0:T(8,128)}), f32[4,10,512]{2,1,0:T(8,128)S(1)}, u32[]{:S(2)}, u32[]{:S(2)}) async-start(f32[4,10,512]{2,1,0:T(8,128)} %reshape.207), calls=%async_computation.3 | async-start | bytes 262144 | tf_op jit(solution)/shard_map/all_to_all | solution.py:828
  255.6 323.1 %reduce-scatter.6.cloned.1.call-start = ((), (), s32[]{:S(2)}) async-start(), calls=%async_computation.16 | async-start | bytes 2949120 | tf_op jit(solution)/shard_map/reduce_scatter | solution.py:894
  289.3 18.5 %collective-permute-start.9 = (bf16[256,1536]{1,0:T(8,128)(2,1)S(1)}, bf16[256,1536]{1,0:T(8,128)(2,1)S(1)}, u32[]{:S(2)}, u32[]{:S(2)}) collective-permute-start(bf16[256,1536]{1,0:T(8,128)(2,1)S(1)} %slice.126), channel_id=1, source_target_pairs={{0,1},{1,0},{2,3},{3,2},{4,5},{5,4},{6,7},{7,6},{8,9},{9,8},{10,11... | collective-permute-start | bytes 2359304 | tf_op jit(solution)/shard_map/ppermute | solution.py:668
  290.8 18.2 %collective-permute-start.10 = (bf16[256,1536]{1,0:T(8,128)(2,1)S(1)}, bf16[256,1536]{1,0:T(8,128)(2,1)S(1)}, u32[]{:S(2)}, u32[]{:S(2)}) collective-permute-start(bf16[256,1536]{1,0:T(8,128)(2,1)S(1)} %slice.127), channel_id=1, source_target_pairs={{0,2},{1,3},{2,0},{3,1},{4,6},{5,7},{6,4},{7,5},{8,10},{9,11},{10,... | collective-permute-start | bytes 2359304 | tf_op jit(solution)/shard_map/ppermute | solution.py:668
  340.1 238.5 %reduce-scatter.8.cloned.1.call-start = ((), (), s32[]{:S(2)}) async-start(), calls=%async_computation.17 | async-start | bytes 2949120 | tf_op jit(solution)/shard_map/reduce_scatter | solution.py:894
  354.3 32.2 %collective-permute-start.12 = (bf16[4,1,192,1536]{3,2,1,0:T(8,128)(2,1)}, bf16[4,1,192,1536]{3,2,1,0:T(8,128)(2,1)S(1)}, u32[]{:S(2)}, u32[]{:S(2)}) collective-permute-start(bf16[4,1,192,1536]{3,2,1,0:T(8,128)(2,1)} %get-tuple-element.179), channel_id=1, source_target_pairs={{0,4},{4,0},{8,12},{12,8},{16,20},{20,16},{24,28},{28,24},{1,5},{5... | collective-permute-start | bytes 7077896 | tf_op jit(solution)/shard_map/ppermute | solution.py:668
  386.0 38.0 %collective-permute-start.13 = (bf16[4,3,192,1536]{3,2,1,0:T(8,128)(2,1)}, bf16[4,3,192,1536]{3,2,1,0:T(8,128)(2,1)}, u32[]{:S(2)}, u32[]{:S(2)}) collective-permute-start(bf16[4,3,192,1536]{3,2,1,0:T(8,128)(2,1)} %get-tuple-element.185), channel_id=1, source_target_pairs={{0,4},{4,0},{8,12},{12,8},{16,20},{20,16},{24,28},{28,24},{1,5},{5... | collective-permute-start | bytes 21233672 | tf_op jit(solution)/shard_map/ppermute | solution.py:668
  392.4 186.3 %reduce-scatter.10.cloned.1.call-start = ((), (), s32[]{:S(2)}) async-start(), calls=%async_computation.18 | async-start | bytes 8847360 | tf_op jit(solution)/shard_map/reduce_scatter | solution.py:894
  436.2 361.0 %reduce-scatter.14.cloned.1.call-start = ((), (), s32[]{:S(2)}) async-start(), calls=%async_computation.20 | async-start | bytes 8847360 | tf_op jit(solution)/shard_map/reduce_scatter | solution.py:894
  438.8 106.7 %collective-permute-start.20 = (bf16[4,3,192,1536]{3,2,1,0:T(8,128)(2,1)}, bf16[4,3,192,1536]{3,2,1,0:T(8,128)(2,1)}, u32[]{:S(2)}, u32[]{:S(2)}) collective-permute-start(bf16[4,3,192,1536]{3,2,1,0:T(8,128)(2,1)} %get-tuple-element.191), channel_id=1, source_target_pairs={{0,4},{4,0},{8,12},{12,8},{16,20},{20,16},{24,28},{28,24},{1,5},{5... | collective-permute-start | bytes 21233672 | tf_op jit(solution)/shard_map/ppermute | solution.py:668
  472.3 22.1 %collective-permute-start.17 = (bf16[256,1664]{1,0:T(8,128)(2,1)}, bf16[256,1664]{1,0:T(8,128)(2,1)}, u32[]{:S(2)}, u32[]{:S(2)}) collective-permute-start(bf16[256,1664]{1,0:T(8,128)(2,1)} %get-tuple-element.330), channel_id=1, source_target_pairs={{0,2},{1,3},{2,0},{3,1},{4,6},{5,7},{6,4},{7,5},{8,10},{9,11},{10,... | collective-permute-start | bytes 2555912 | tf_op jit(solution)/shard_map/ppermute | solution.py:668
  473.8 22.9 %collective-permute-start.15 = (bf16[256,1664]{1,0:T(8,128)(2,1)}, bf16[256,1664]{1,0:T(8,128)(2,1)}, u32[]{:S(2)}, u32[]{:S(2)}) collective-permute-start(bf16[256,1664]{1,0:T(8,128)(2,1)} %get-tuple-element.331), channel_id=1, source_target_pairs={{0,1},{1,0},{2,3},{3,2},{4,5},{5,4},{6,7},{7,6},{8,9},{9,8},{10,11... | collective-permute-start | bytes 2555912 | tf_op jit(solution)/shard_map/ppermute | solution.py:668
  487.9 24.0 %collective-permute-start.19 = (bf16[256,1664]{1,0:T(8,128)(2,1)S(1)}, bf16[256,1664]{1,0:T(8,128)(2,1)S(1)}, u32[]{:S(2)}, u32[]{:S(2)}) collective-permute-start(bf16[256,1664]{1,0:T(8,128)(2,1)S(1)} %slice.166), channel_id=1, source_target_pairs={{0,2},{1,3},{2,0},{3,1},{4,6},{5,7},{6,4},{7,5},{8,10},{9,11},{10,... | collective-permute-start | bytes 2555912 | tf_op jit(solution)/shard_map/ppermute | solution.py:668
  490.3 30.4 %collective-permute-start.14 = (bf16[256,1664]{1,0:T(8,128)(2,1)}, bf16[256,1664]{1,0:T(8,128)(2,1)S(1)}, u32[]{:S(2)}, u32[]{:S(2)}) collective-permute-start(bf16[256,1664]{1,0:T(8,128)(2,1)} %slice.160), channel_id=1, source_target_pairs={{0,1},{1,0},{2,3},{3,2},{4,5},{5,4},{6,7},{7,6},{8,9},{9,8},{10,11... | collective-permute-start | bytes 2555912 | tf_op jit(solution)/shard_map/ppermute | solution.py:668
  494.4 51.2 %collective-permute-start.21 = (bf16[4,2,192,1536]{3,2,1,0:T(8,128)(2,1)}, bf16[4,2,192,1536]{3,2,1,0:T(8,128)(2,1)}, u32[]{:S(2)}, u32[]{:S(2)}) collective-permute-start(bf16[4,2,192,1536]{3,2,1,0:T(8,128)(2,1)} %get-tuple-element.193), channel_id=1, source_target_pairs={{0,4},{4,0},{8,12},{12,8},{16,20},{20,16},{24,28},{28,24},{1,5},{5... | collective-permute-start | bytes 14155784 | tf_op jit(solution)/shard_map/ppermute | solution.py:668
  496.7 34.8 %collective-permute-start.18 = (bf16[256,1664]{1,0:T(8,128)(2,1)}, bf16[256,1664]{1,0:T(8,128)(2,1)}, u32[]{:S(2)}, u32[]{:S(2)}) collective-permute-start(bf16[256,1664]{1,0:T(8,128)(2,1)} %add_convert_fusion.1), channel_id=1, source_target_pairs={{0,1},{1,0},{2,3},{3,2},{4,5},{5,4},{6,7},{7,6},{8,9},{9,8},{10,11... | collective-permute-start | bytes 2555912 | tf_op jit(solution)/shard_map/ppermute | solution.py:668
  511.9 20.7 %collective-permute-start.16 = (bf16[256,1664]{1,0:T(8,128)(2,1)}, bf16[256,1664]{1,0:T(8,128)(2,1)S(1)}, u32[]{:S(2)}, u32[]{:S(2)}) collective-permute-start(bf16[256,1664]{1,0:T(8,128)(2,1)} %add_convert_fusion.2), channel_id=1, source_target_pairs={{0,2},{1,3},{2,0},{3,1},{4,6},{5,7},{6,4},{7,5},{8,10},{9,11},{10,... | collective-permute-start | bytes 2555912 | tf_op jit(solution)/shard_map/ppermute | solution.py:668
  557.6 84.3 %all-to-all-start.4 = ((bf16[8,192,512]{2,1,0:T(8,128)(2,1)}), bf16[8,192,512]{2,1,0:T(8,128)(2,1)}, u32[]{:S(2)}, u32[]{:S(2)}) async-start(bf16[8,192,512]{2,1,0:T(8,128)(2,1)} %bitcast.127), calls=%async_computation.7 | async-start | bytes 3145728 | tf_op jit(solution)/shard_map/all_to_all | solution.py:938
  578.7 45.1 %collective-permute-start.22 = (bf16[8,48,1664]{2,1,0:T(8,128)(2,1)}, bf16[8,48,1664]{2,1,0:T(8,128)(2,1)}, u32[]{:S(2)}, u32[]{:S(2)}) collective-permute-start(bf16[8,48,1664]{2,1,0:T(8,128)(2,1)} %get-tuple-element.219), channel_id=1, source_target_pairs={{0,1},{1,0},{2,3},{3,2},{4,5},{5,4},{6,7},{7,6},{8,9},{9,8},{10,11... | collective-permute-start | bytes 3833864 | tf_op jit(solution)/shard_map/ppermute | solution.py:668
  579.8 56.6 %collective-permute-start.23 = (bf16[8,48,1664]{2,1,0:T(8,128)(2,1)}, bf16[8,48,1664]{2,1,0:T(8,128)(2,1)}, u32[]{:S(2)}, u32[]{:S(2)}) collective-permute-start(bf16[8,48,1664]{2,1,0:T(8,128)(2,1)} %get-tuple-element.220), channel_id=1, source_target_pairs={{0,2},{1,3},{2,0},{3,1},{4,6},{5,7},{6,4},{7,5},{8,10},{9,11},{10,... | collective-permute-start | bytes 3833864 | tf_op jit(solution)/shard_map/ppermute | solution.py:668
  581.2 56.6 %collective-permute-start.24 = (bf16[8,48,1664]{2,1,0:T(8,128)(2,1)}, bf16[8,48,1664]{2,1,0:T(8,128)(2,1)}, u32[]{:S(2)}, u32[]{:S(2)}) collective-permute-start(bf16[8,48,1664]{2,1,0:T(8,128)(2,1)} %get-tuple-element.221), channel_id=1, source_target_pairs={{0,3},{1,2},{2,1},{3,0},{4,7},{5,6},{6,5},{7,4},{8,11},{9,10},{10,... | collective-permute-start | bytes 3833864 | tf_op jit(solution)/shard_map/ppermute | solution.py:668
  641.9 89.5 %all-to-all-start.5 = ((bf16[8,48,1664]{2,1,0:T(8,128)(2,1)}), bf16[8,48,1664]{2,1,0:T(8,128)(2,1)}, u32[]{:S(2)}, u32[]{:S(2)}) async-start(bf16[8,48,1664]{2,1,0:T(8,128)(2,1)} %add_convert_fusion), calls=%async_computation.8 | async-start | bytes 2555904 | tf_op jit(solution)/shard_map/all_to_all | solution.py:953
  731.5 65.6 %all-to-all-start.6 = ((bf16[8,320,512]{2,1,0:T(8,128)(2,1)}), bf16[8,320,512]{2,1,0:T(8,128)(2,1)}, u32[]{:S(2)}, u32[]{:S(2)}) async-start(bf16[8,320,512]{2,1,0:T(8,128)(2,1)} %attend_back.1.back_ref), calls=%async_computation.9 | async-start | bytes 5242880 | tf_op jit(solution)/shard_map/all_to_all | solution.py:959
  736.5 149.3 %reduce-scatter.12.cloned.1.call-start = ((), (), s32[]{:S(2)}) async-start(), calls=%async_computation.19 | async-start | bytes 5898240 | tf_op jit(solution)/shard_map/reduce_scatter | solution.py:894
  752.3 15.5 %collective-permute-start.27 = (bf16[8,48,320]{2,1,0:T(8,128)(2,1)S(1)}, bf16[8,48,320]{2,1,0:T(8,128)(2,1)S(1)}, u32[]{:S(2)}, u32[]{:S(2)}) collective-permute-start(bf16[8,48,320]{2,1,0:T(8,128)(2,1)S(1)} %get-tuple-element.337), channel_id=1, source_target_pairs={{0,3},{1,2},{2,1},{3,0},{4,7},{5,6},{6,5},{7,4},{8,11},{9,10},{10,... | collective-permute-start | bytes 737288 | tf_op jit(solution)/shard_map/ppermute | solution.py:668
  754.0 15.1 %collective-permute-start.26 = (bf16[8,48,320]{2,1,0:T(8,128)(2,1)S(1)}, bf16[8,48,320]{2,1,0:T(8,128)(2,1)S(1)}, u32[]{:S(2)}, u32[]{:S(2)}) collective-permute-start(bf16[8,48,320]{2,1,0:T(8,128)(2,1)S(1)} %get-tuple-element.338), channel_id=1, source_target_pairs={{0,2},{1,3},{2,0},{3,1},{4,6},{5,7},{6,4},{7,5},{8,10},{9,11},{10,... | collective-permute-start | bytes 737288 | tf_op jit(solution)/shard_map/ppermute | solution.py:668
  800.9 23.8 %all-to-all-start.7 = ((bf16[8,48,320]{2,1,0:T(8,128)(2,1)}), bf16[8,48,320]{2,1,0:T(8,128)(2,1)S(1)}, u32[]{:S(2)}, u32[]{:S(2)}) async-start(bf16[8,48,320]{2,1,0:T(8,128)(2,1)} %fusion.16), calls=%async_computation.10 | async-start | bytes 589824 | tf_op jit(solution)/shard_map/all_to_all | solution.py:975
  807.3 22.3 %collective-permute-start.29 = (bf16[256,1536]{1,0:T(8,128)(2,1)}, bf16[256,1536]{1,0:T(8,128)(2,1)}, u32[]{:S(2)}, u32[]{:S(2)}) collective-permute-start(bf16[256,1536]{1,0:T(8,128)(2,1)} %get-tuple-element.334), channel_id=1, source_target_pairs={{0,1},{1,0},{2,3},{3,2},{4,5},{5,4},{6,7},{7,6},{8,9},{9,8},{10,11... | collective-permute-start | bytes 2359304 | tf_op jit(solution)/shard_map/ppermute | solution.py:668
  808.0 24.7 %collective-permute-start.31 = (bf16[256,1536]{1,0:T(8,128)(2,1)}, bf16[256,1536]{1,0:T(8,128)(2,1)}, u32[]{:S(2)}, u32[]{:S(2)}) collective-permute-start(bf16[256,1536]{1,0:T(8,128)(2,1)} %get-tuple-element.335), channel_id=1, source_target_pairs={{0,2},{1,3},{2,0},{3,1},{4,6},{5,7},{6,4},{7,5},{8,10},{9,11},{10,... | collective-permute-start | bytes 2359304 | tf_op jit(solution)/shard_map/ppermute | solution.py:668
  822.3 53.9 %collective-permute-start.33 = (bf16[256,1536]{1,0:T(8,128)(2,1)}, bf16[256,1536]{1,0:T(8,128)(2,1)}, u32[]{:S(2)}, u32[]{:S(2)}) collective-permute-start(bf16[256,1536]{1,0:T(8,128)(2,1)} %slice.146), channel_id=1, source_target_pairs={{0,2},{1,3},{2,0},{3,1},{4,6},{5,7},{6,4},{7,5},{8,10},{9,11},{10,... | collective-permute-start | bytes 2359304 | tf_op jit(solution)/shard_map/ppermute | solution.py:668
  822.8 53.4 %collective-permute-start.28 = (bf16[256,1536]{1,0:T(8,128)(2,1)}, bf16[256,1536]{1,0:T(8,128)(2,1)}, u32[]{:S(2)}, u32[]{:S(2)}) collective-permute-start(bf16[256,1536]{1,0:T(8,128)(2,1)} %slice.140), channel_id=1, source_target_pairs={{0,1},{1,0},{2,3},{3,2},{4,5},{5,4},{6,7},{7,6},{8,9},{9,8},{10,11... | collective-permute-start | bytes 2359304 | tf_op jit(solution)/shard_map/ppermute | solution.py:668
  827.9 26.4 %collective-permute-start.36 = (bf16[48,4224]{1,0:T(8,128)(2,1)}, bf16[48,4224]{1,0:T(8,128)(2,1)S(1)}, u32[]{:S(2)}, u32[]{:S(2)}) collective-permute-start(bf16[48,4224]{1,0:T(8,128)(2,1)} %gather_parts.1.refs_0_), channel_id=1, source_target_pairs={{0,3},{1,2},{2,1},{3,0},{4,7},{5,6},{6,5},{7,4},{8,11},{9,10},{10,... | collective-permute-start | bytes 1216520 | tf_op jit(solution)/shard_map/ppermute | solution.py:668
  829.5 33.3 %collective-permute-start.35 = (bf16[48,4224]{1,0:T(8,128)(2,1)}, bf16[48,4224]{1,0:T(8,128)(2,1)S(1)}, u32[]{:S(2)}, u32[]{:S(2)}) collective-permute-start(bf16[48,4224]{1,0:T(8,128)(2,1)} %gather_parts.1.refs_0_), channel_id=1, source_target_pairs={{0,2},{1,3},{2,0},{3,1},{4,6},{5,7},{6,4},{7,5},{8,10},{9,11},{10,... | collective-permute-start | bytes 1216520 | tf_op jit(solution)/shard_map/ppermute | solution.py:668
  832.7 35.3 %collective-permute-start.34 = (bf16[48,4224]{1,0:T(8,128)(2,1)}, bf16[48,4224]{1,0:T(8,128)(2,1)S(1)}, u32[]{:S(2)}, u32[]{:S(2)}) collective-permute-start(bf16[48,4224]{1,0:T(8,128)(2,1)} %gather_parts.1.refs_0_), channel_id=1, source_target_pairs={{0,1},{1,0},{2,3},{3,2},{4,5},{5,4},{6,7},{7,6},{8,9},{9,8},{10,11... | collective-permute-start | bytes 1216520 | tf_op jit(solution)/shard_map/ppermute | solution.py:668
  854.3 24.7 %collective-permute-start.30 = (bf16[256,1536]{1,0:T(8,128)(2,1)}, bf16[256,1536]{1,0:T(8,128)(2,1)}, u32[]{:S(2)}, u32[]{:S(2)}) collective-permute-start(bf16[256,1536]{1,0:T(8,128)(2,1)} %add_convert_fusion.4), channel_id=1, source_target_pairs={{0,2},{1,3},{2,0},{3,1},{4,6},{5,7},{6,4},{7,5},{8,10},{9,11},{10,... | collective-permute-start | bytes 2359304 | tf_op jit(solution)/shard_map/ppermute | solution.py:668
  862.8 18.4 %collective-permute-start.32 = (bf16[256,1536]{1,0:T(8,128)(2,1)}, bf16[256,1536]{1,0:T(8,128)(2,1)}, u32[]{:S(2)}, u32[]{:S(2)}) collective-permute-start(bf16[256,1536]{1,0:T(8,128)(2,1)} %add_convert_fusion.3), channel_id=1, source_target_pairs={{0,1},{1,0},{2,3},{3,2},{4,5},{5,4},{6,7},{7,6},{8,9},{9,8},{10,11... | collective-permute-start | bytes 2359304 | tf_op jit(solution)/shard_map/ppermute | solution.py:668
  (54 other events, 726.6 us)
Sparse Core Ops, SparseCore 0:
  10.2 99.6 all-gather.5
  112.1 36.6 all-gather.7
  156.9 52.4 all-gather.9
  247.2 76.4 all-gather.11
  340.3 45.6 reduce-scatter.5
  392.5 45.6 reduce-scatter.7
  440.5 123.0 reduce-scatter.9
  565.9 163.4 reduce-scatter.13
  797.2 88.0 reduce-scatter.11
